TPU v7x, 128 devices: a whole 4x4x4 slice. The times are simulated.
128 devices in a mesh: col: 16 (over y_hi, x, core), row: 8 (over z, y_lo).
Axes of the slice: x: 4, y: 4 (y_hi: 2, y_lo: 2; y = y_hi * 2 + y_lo), z: 4, core: 2. Of those that a mesh axis runs over, the one named last changes fastest.
Arguments:
- weight: bfloat16 [4096, 16384], P('row', 'col'), may hold values from -10 to 10
Outputs:
- codes: bfloat16 [4096, 16384], P('row')
- scales: float32 [4096], P('row')
All inputs are finite; a program needn't handle non-finite values. Where the computation divides by a largest or mean magnitude, that divisor is 1e-20 or more.
Results may differ from a plain program's by a relative error of at most 0.015.
Values may be sent and summed in bfloat16 or wider, within the bound.
No kernel may reach another device: no remote copies, remote signals or barrier semaphores. Data moves between devices by JAX's collectives and lax.ppermute only.
A program may use at most 128 MiB of HBM per device.

v0:
```python
import jax
import jax.numpy as jnp
from jax import lax
from jax.sharding import PartitionSpec as P


def swapped(value, axis, bit):
    mask = 2**bit
    pairs = [(source, source ^ mask) for source in range(lax.axis_size(axis))]
    return lax.ppermute(value, axis, pairs)


def hadamard(order):
    table = jnp.ones((1, 1), jnp.float32)
    while table.shape[0] < order:
        table = jnp.concatenate(
            [jnp.concatenate([table, table], 1), jnp.concatenate([table, -table], 1)], 0
        )
    return table


def local(weight):
    ordered = lax.all_to_all(weight, "row", split_axis=0, concat_axis=0, tiled=True)
    local_cols = ordered.shape[1]
    groups = lax.axis_size("col")
    width = local_cols * groups
    norm_factor = 1.0 / jnp.sqrt(jnp.float32(width))
    block_table = hadamard(local_cols).astype(jnp.bfloat16)
    partial_rot = jnp.dot(ordered, block_table, preferred_element_type=jnp.float32)
    position = lax.axis_index("col")
    levels = groups.bit_length() - 1
    bit_order = list(range(levels))
    for level in bit_order:
        partner = swapped(partial_rot.astype(jnp.bfloat16), "col", level).astype(partial_rot.dtype)
        upper = position // (1 << level) % 2 == 1
        partial_rot = jnp.where(upper, partner - partial_rot, partial_rot + partner)
    rotated = partial_rot * norm_factor
    peak = lax.pmax(jnp.max(jnp.abs(rotated), axis=1), "col")
    scales = peak + 1e-06
    local_codes = (rotated / scales[:, None]).astype(jnp.bfloat16)
    codes = lax.all_gather(local_codes, "col", axis=1, tiled=True)
    return (codes, scales)


def solution(mesh):
    placed = (P("row", "col"),)
    return jax.shard_map(
        local, mesh=mesh, in_specs=placed, out_specs=(P("row", None), P("row")), check_vma=False
    )
```

profile of v0, /device:TPU:1, one launch (start us, length us, event | category | flops | bytes accessed | tf_op | source)
XLA Modules:
  0.0 292.1 jit_solution(15686149864510555744)
XLA Ops:
  7.2 0.0 all-gather.2.cloned.1.call-start
  7.2 0.0 copy-start.2
  7.2 21.9 %all_to_all.12 = bf16[8,64,1024]{2,1,0:T(8,128)(2,1)S(1)} all-to-all(bf16[8,64,1024]{2,1,0:T(8,128)(2,1)} %bitcast.12), channel_id=1, replica_groups=mesh['col'=16,'row'=8] {'row'}, dimensions={0} | all-to-all | bytes 2097152 | tf_op jit(solution)/shard_map/all_to_all | solution.py:23
  29.2 0.0 copy-done.2
  29.2 2.3 bitcast_convert_fusion
  31.4 0.0 copy-start
  31.4 1.9 collective-permute-start
  33.3 2.5 collective-permute-done
  35.8 1.4 fusion.6
  37.2 0.0 copy-done
  37.2 1.2 collective-permute-start.1
  38.4 23.5 %collective-permute-done.1 = bf16[512,1024]{0,1:T(8,128)(2,1)} collective-permute-done((bf16[512,1024]{0,1:T(8,128)(2,1)}, bf16[512,1024]{0,1:T(8,128)(2,1)}, u32[]{:S(2)}, u32[]{:S(2)}) %collective-permute-start.1) | collective-permute-done | bytes 1048608 | tf_op jit(solution)/shard_map/ppermute | solution.py:10
  61.9 3.5 %fusion.7 = (bf16[512,1024]{0,1:T(8,128)(2,1)}, f32[512,1024]{0,1:T(8,128)S(1)}) fusion(f32[1024,512]{1,0:T(8,128)} %copy-done, bf16[512,1024]{0,1:T(8,128)(2,1)S(1)} %collective-permute-done, pred[]{:T(512)S(6)} %eq.20, bf16[512,1024]{0,1:T(8,128)(2,1)} %collective-permute-done.1, pred[]{:T(512)S(6)} %eq.19), kind=kLoop, calls=%fused_computation.19 | loop fusion | flops 4718592 | bytes 7340034 | tf_op jit(solution)/shard_map/convert_element_type | solution.py:34
  65.4 2.7 collective-permute-start.2
  68.1 22.4 %collective-permute-done.2 = bf16[512,1024]{0,1:T(8,128)(2,1)S(1)} collective-permute-done((bf16[512,1024]{0,1:T(8,128)(2,1)}, bf16[512,1024]{0,1:T(8,128)(2,1)S(1)}, u32[]{:S(2)}, u32[]{:S(2)}) %collective-permute-start.2) | collective-permute-done | bytes 1048608 | tf_op jit(solution)/shard_map/ppermute | solution.py:10
  90.5 1.3 fusion.5
  91.9 2.6 collective-permute-start.3
  94.5 21.7 %collective-permute-done.3 = bf16[512,1024]{0,1:T(8,128)(2,1)} collective-permute-done((bf16[512,1024]{0,1:T(8,128)(2,1)}, bf16[512,1024]{0,1:T(8,128)(2,1)}, u32[]{:S(2)}, u32[]{:S(2)}) %collective-permute-start.3) | collective-permute-done | bytes 1048608 | tf_op jit(solution)/shard_map/ppermute | solution.py:10
  116.2 1.9 abs_reduce_fusion
  118.1 35.6 %pmax.7 = f32[512]{0:T(512)S(1)} all-reduce(f32[512]{0:T(512)S(1)} %abs_reduce_fusion), channel_id=1, replica_groups=mesh['col'=16,'row'=8] {'col'}, use_global_device_ids=true, to_apply=%region_1.2 | all-reduce | flops 512 | bytes 4096 | tf_op jit(solution)/shard_map/pmax | solution.py:38
  153.7 0.0 copy-start.1
  153.7 2.9 %divide_convert_fusion = bf16[512,1024]{0,1:T(8,128)(2,1)} fusion(f32[512]{0:T(512)S(1)} %broadcast_add_fusion, f32[512,1024]{0,1:T(8,128)S(1)} %get-tuple-element.5, bf16[512,1024]{0,1:T(8,128)(2,1)S(1)} %collective-permute-done.2, pred[]{:T(512)S(6)} %eq.18, bf16[512,1024]{0,1:T(8,128)(2,1)} %collective-permute-done.3, pred[]{:T(512)S(6)} %eq.17), kind=kLoop, calls=%fused_computation.14 | loop fusion | flops 5767168 | bytes 5244930 | tf_op jit(solution)/shard_map/convert_element_type | solution.py:40
  156.6 0.0 copy-done.1
  156.6 0.0 all-gather.2.cloned.1.call-update
  156.6 107.5 %all-gather.2.cloned.1.call-done = bf16[512,16384]{0,1:T(8,128)(2,1)} async-done(((bf16[512,1024]{0,1:T(8,128)(2,1)}), bf16[512,16384]{0,1:T(8,128)(2,1)}) %all-gather.2.cloned.1.call-update) | async-done | bytes 16777232 | tf_op jit(solution)/shard_map/all_gather | solution.py:41
  264.1 21.2 %copy.3 = bf16[512,16384]{1,0:T(8,128)(2,1)} copy(bf16[512,16384]{0,1:T(8,128)(2,1)} %all-gather.2.cloned.1.call-done) | data formatting | bytes 33554432
  (1 shorter events, 0.0 us)
Async XLA Ops:
  7.2 256.9 %all-gather.2.cloned.1.call-start = ((), (), s32[]{:S(2)}) async-start(), calls=%async_computation.1 | async-start | bytes 17825792 | tf_op jit(solution)/shard_map/all_gather | solution.py:41
  7.2 22.0 %copy-start.2 = (bf16[1024,1024]{1,0:T(8,128)(2,1)S(1)}, bf16[1024,1024]{1,0:T(8,128)(2,1)}, u32[]{:S(2)}) copy-start(bf16[1024,1024]{1,0:T(8,128)(2,1)} %constant.84.clone.1) | copy-start | bytes 6291460
  31.4 5.8 %copy-start = (f32[1024,512]{1,0:T(8,128)}, f32[1024,512]{1,0:T(8,128)S(1)}, u32[]{:S(2)}) copy-start(f32[1024,512]{1,0:T(8,128)S(1)} %get-tuple-element.7) | copy-start | bytes 6291460
  31.4 4.4 %collective-permute-start = (bf16[512,1024]{0,1:T(8,128)(2,1)}, bf16[512,1024]{0,1:T(8,128)(2,1)S(1)}, u32[]{:S(2)}, u32[]{:S(2)}) collective-permute-start(bf16[512,1024]{0,1:T(8,128)(2,1)} %get-tuple-element.6), channel_id=1, source_target_pairs={{0,8},{8,0},{16,24},{24,16},{32,40},{40,32},{48,56},{56,48},{64,72... | collective-permute-start | bytes 3145736 | tf_op jit(solution)/shard_map/ppermute | solution.py:10
  37.2 24.7 %collective-permute-start.1 = (bf16[512,1024]{0,1:T(8,128)(2,1)}, bf16[512,1024]{0,1:T(8,128)(2,1)}, u32[]{:S(2)}, u32[]{:S(2)}) collective-permute-start(bf16[512,1024]{0,1:T(8,128)(2,1)} %fusion.6), channel_id=1, source_target_pairs={{0,16},{8,24},{16,0},{24,8},{32,48},{40,56},{48,32},{56,40},{64,80... | collective-permute-start | bytes 3145736 | tf_op jit(solution)/shard_map/ppermute | solution.py:10
  65.4 25.2 %collective-permute-start.2 = (bf16[512,1024]{0,1:T(8,128)(2,1)}, bf16[512,1024]{0,1:T(8,128)(2,1)S(1)}, u32[]{:S(2)}, u32[]{:S(2)}) collective-permute-start(bf16[512,1024]{0,1:T(8,128)(2,1)} %get-tuple-element.4), channel_id=1, source_target_pairs={{0,32},{8,40},{16,48},{24,56},{32,0},{40,8},{48,16},{56,24},{64,96... | collective-permute-start | bytes 3145736 | tf_op jit(solution)/shard_map/ppermute | solution.py:10
  91.9 24.3 %collective-permute-start.3 = (bf16[512,1024]{0,1:T(8,128)(2,1)}, bf16[512,1024]{0,1:T(8,128)(2,1)}, u32[]{:S(2)}, u32[]{:S(2)}) collective-permute-start(bf16[512,1024]{0,1:T(8,128)(2,1)} %fusion.5), channel_id=1, source_target_pairs={{0,64},{8,72},{16,80},{24,88},{32,96},{40,104},{48,112},{56,120},{... | collective-permute-start | bytes 3145736 | tf_op jit(solution)/shard_map/ppermute | solution.py:10
  153.7 2.9 %copy-start.1 = (f32[512]{0:T(512)}, f32[512]{0:T(512)S(1)}, u32[]{:S(2)}) copy-start(f32[512]{0:T(512)S(1)} %broadcast_add_fusion) | copy-start | bytes 6148
Sparse Core Ops, SparseCore 0:
  156.8 107.3 all-gather.1
where the time goes:
time: 293 us; the launch traced here: 292 us
  waiting for transfers between devices  178 us (61%)
  blocking collectives  57.5 us (20%)
  local copies, waits for them, and re-layouts  21.2 us (7%)
  between operations  14 us (5%)
  other arithmetic  11 us (4%)
  starting transfers between devices  8.48 us (3%)
    all_gather x1, waiting for transfers between devices, local(): codes = lax.all_gather(local_codes, 'col', axis=1, tiled=True)  107 us
    ppermute x4, waiting for transfers between devices, swapped(): return lax.ppermute(value, axis, pairs)  70.1 us
    pmax x1, blocking collectives, local(): peak = lax.pmax(jnp.max(jnp.abs(rotated), axis=1), 'col')  35.6 us
    all_to_all x1, blocking collectives, local(): lax.all_to_all(weight, 'row', split_axis=0, concat_axis=0, tiled=True)  21.9 us
    unnamed x7, local copies, waits for them, and re-layouts  21.2 us
    ppermute x4, starting transfers between devices, swapped(): return lax.ppermute(value, axis, pairs)  8.44 us
    convert_element_type x3, other arithmetic, local(): partial_rot.astype(jnp.bfloat16)  6.22 us
  transfers between devices with their start and end apart: 5, of which 5 were waited for; matrix products, arithmetic and copies ran while one was open for 0% of the time, Pallas kernels for 0%

commit v1 on v0

v1 whole, which is shorter than its diff:
```python
import functools

import jax
import jax.numpy as jnp
import numpy as np
from jax import lax
from jax.experimental import pallas as pl
from jax.experimental.pallas import tpu as pltpu
from jax.sharding import PartitionSpec as P

UNIT = 16
BASE = 256
LANES = 256

XA, XB, YH = 1, 3, 4

CHUNKS = (
    (3, (YH, XA, XB)),
    (3, (XA, XB, YH)),
    (3, (XB, YH, XA)),
    (2, (YH, XA, XB)),
    (2, (XA, XB, YH)),
    (3, (XB, YH, XA)),
)


def hadamard(order):
    table = np.ones((1, 1), np.float32)
    while table.shape[0] < order:
        table = np.block([[table, table], [table, -table]])
    return table


def swapped(value, axis, mask):
    pairs = [(source, source ^ mask) for source in range(lax.axis_size(axis))]
    return lax.ppermute(value, axis, pairs)


def butterfly(parts):
    parts = list(parts)
    span = 1
    while span < len(parts):
        for i in range(len(parts)):
            if not i & span:
                a, b = parts[i], parts[i | span]
                parts[i], parts[i | span] = a + b, a - b
        span *= 2
    return parts


def first_kernel(core_ref, own_ref, got_ref, table_ref, out_ref):
    sign = jnp.where(core_ref[0] == 0, 1.0, -1.0).astype(jnp.float32)
    cols = own_ref.shape[-1]
    rows = own_ref.shape[0] * own_ref.shape[1]
    table = table_ref[...]

    def rotated(ref):
        value = ref[...].reshape(rows, cols)
        return butterfly(
            jnp.dot(value[:, c : c + BASE], table, preferred_element_type=jnp.float32)
            for c in range(0, cols, BASE)
        )

    shape = own_ref.shape[:2] + (BASE,)
    for i, (a, b) in enumerate(zip(rotated(own_ref), rotated(got_ref))):
        out_ref[:, :, i * BASE : (i + 1) * BASE] = (a + b).astype(out_ref.dtype).reshape(shape)
        out_ref[:, :, cols + i * BASE : cols + (i + 1) * BASE] = (
            ((a - b) * sign).astype(out_ref.dtype).reshape(shape)
        )


def first_rotation(weight, got, core):
    blocks, half, cols = got.shape
    per = blocks // 4
    grid = pltpu.PrefetchScalarGridSpec(
        num_scalar_prefetch=1,
        grid=(4,),
        in_specs=[
            pl.BlockSpec((per, half, cols), lambda g, core: (g, core[0], 0)),
            pl.BlockSpec((per, half, cols), lambda g, core: (g, 0, 0)),
            pl.BlockSpec((BASE, BASE), lambda g, core: (0, 0)),
        ],
        out_specs=pl.BlockSpec((per, half, 2 * cols), lambda g, core: (g, 0, 0)),
    )
    return pl.pallas_call(
        first_kernel,
        grid_spec=grid,
        out_shape=jax.ShapeDtypeStruct((blocks, half, 2 * cols), weight.dtype),
        compiler_params=pltpu.CompilerParams(vmem_limit_bytes=16 * 2**20),
        cost_estimate=pl.CostEstimate(
            flops=4 * blocks * half * cols * BASE,
            bytes_accessed=8 * blocks * half * cols,
            transcendentals=0,
        ),
        name="first_rotation",
    )(core, weight, got, jnp.asarray(hadamard(BASE), weight.dtype))


def last_kernel(order, norm, where_ref, c2, r2, r3a, r3b, *rest):
    out_ref, send_ref, scale_ref, work = rest[-4:]
    d1, d2, d3 = order
    place = {}
    for ref, base in ((c2, 0), (r2, d2), (r3a, d3), (r3b, d3 ^ d2)):
        place[base] = (ref, 0)
        place[base ^ d1] = (ref, 1)
    groups = len(place)
    cols = c2.shape[-1]
    peak = None
    for c in range(0, cols, LANES):
        parts = butterfly(
            place[i][0][place[i][1], :, c : c + LANES].astype(jnp.float32) for i in range(groups)
        )
        for k, part in enumerate(parts):
            work[k, :, c : c + LANES] = part
            part = jnp.abs(part)
            peak = part if peak is None else jnp.maximum(peak, part)
    scale = jnp.max(peak, axis=1, keepdims=True) * norm + 1e-06
    scale_ref[...] = jnp.broadcast_to(scale, scale_ref.shape)
    factor = norm / scale
    me = where_ref[1]
    for k in range(groups):
        both = me & k
        odd = (both ^ (both >> 1) ^ (both >> 2)) & 1
        signed = factor * jnp.where(odd == 0, 1.0, -1.0).astype(jnp.float32)
        for c in range(0, cols, LANES):
            value = (work[k, :, c : c + LANES] * signed).astype(out_ref.dtype)
            out_ref[:, k * cols + c : k * cols + c + LANES] = value
            send_ref[:, k * cols + c : k * cols + c + LANES] = value


def place_of(unit, core, units_half):
    return (unit // units_half) * (2 * units_half) + core * units_half + unit % units_half


def last_rotation(start, units, units_half, order, norm, where, shards, out, full):
    _, rows, cols = shards[0].shape
    groups = 8
    wide = groups * cols
    in_specs = [pl.BlockSpec((2, UNIT, cols), lambda g, where: (0, g, 0))] * 4
    operands = [where, *shards]
    aliases = {}
    if out is not None:
        in_specs.append(pl.BlockSpec(memory_space=pl.ANY))
        operands.append(out)
        aliases = {5: 0}
    grid = pltpu.PrefetchScalarGridSpec(
        num_scalar_prefetch=1,
        grid=(units,),
        in_specs=in_specs,
        out_specs=[
            pl.BlockSpec(
                (UNIT, wide), lambda g, where: (place_of(start + g, where[0], units_half), 0)
            ),
            pl.BlockSpec((UNIT, wide), lambda g, where: (g, 0)),
            pl.BlockSpec((UNIT, 128), lambda g, where: (g, 0)),
        ],
        scratch_shapes=[pltpu.VMEM((groups, UNIT, cols), jnp.float32)],
    )
    return pl.pallas_call(
        functools.partial(last_kernel, order, norm),
        grid_spec=grid,
        out_shape=[
            jax.ShapeDtypeStruct((full, wide), shards[0].dtype),
            jax.ShapeDtypeStruct((rows, wide), shards[0].dtype),
            jax.ShapeDtypeStruct((rows, 128), jnp.float32),
        ],
        input_output_aliases=aliases,
        compiler_params=pltpu.CompilerParams(vmem_limit_bytes=16 * 2**20),
        cost_estimate=pl.CostEstimate(
            flops=8 * rows * wide, bytes_accessed=6 * rows * wide, transcendentals=0
        ),
        name="last_rotation",
    )(*operands)


def store_kernel(where_ref, got_ref, out_in, out_ref):
    out_ref[...] = got_ref[...]


def store(start, units, units_half, where, got, out):
    rows, wide = got.shape
    grid = pltpu.PrefetchScalarGridSpec(
        num_scalar_prefetch=1,
        grid=(units,),
        in_specs=[
            pl.BlockSpec((UNIT, wide), lambda g, where: (g, 0)),
            pl.BlockSpec(memory_space=pl.ANY),
        ],
        out_specs=pl.BlockSpec(
            (UNIT, wide), lambda g, where: (place_of(start + g, 1 - where[0], units_half), 0)
        ),
    )
    return pl.pallas_call(
        store_kernel,
        grid_spec=grid,
        out_shape=jax.ShapeDtypeStruct(out.shape, out.dtype),
        input_output_aliases={2: 0},
        compiler_params=pltpu.CompilerParams(vmem_limit_bytes=16 * 2**20),
        cost_estimate=pl.CostEstimate(flops=0, bytes_accessed=4 * rows * wide, transcendentals=0),
        name="store_codes",
    )(where, got, out)


def local(weight):
    position = lax.axis_index("col")
    core = position % 2
    rows, cols = weight.shape
    blocks = lax.axis_size("row")
    block = rows // blocks
    half = block // 2
    norm = 1.0 / float(np.sqrt(cols * lax.axis_size("col")))

    weight = weight.reshape(blocks, block, cols)
    send = lax.dynamic_slice_in_dim(weight, (1 - core) * half, half, axis=1)
    got = swapped(send, "col", 1)
    part = first_rotation(weight, got, core.reshape(1))
    part = lax.all_to_all(part, "row", split_axis=0, concat_axis=0, tiled=True)
    part = part.reshape(blocks * half, 2 * cols)

    def moved(value, step):
        return swapped(value, "col", 2 * step)

    state = []
    start = 0
    for units, order in CHUNKS:
        state.append((start, units, order, part[start * UNIT : (start + units) * UNIT]))
        start += units
    firsts = [moved(own, order[0]) for _, _, order, own in state]
    pairs = [jnp.stack([own, got]) for (_, _, _, own), got in zip(state, firsts)]
    seconds = [moved(pair, order[1]) for (_, _, order, _), pair in zip(state, pairs)]
    thirds = [
        (moved(pair, order[2]), moved(second, order[2]))
        for (_, _, order, _), pair, second in zip(state, pairs, seconds)
    ]

    where = jnp.stack([core, position // 2])
    units_half = half // UNIT
    codes = None
    sent, scales = [], []
    for (start, units, order, _), pair, second, third in zip(state, pairs, seconds, thirds):
        codes, send, scale = last_rotation(
            start, units, units_half, order, norm, where, (pair, second, *third), codes, rows
        )
        sent.append(swapped(send, "col", 1))
        scales.append(scale[:, 0])
    for (start, units, _, _), got in zip(state, sent):
        codes = store(start, units, units_half, where, got, codes)
    mine = jnp.concatenate(scales)
    other = swapped(mine, "col", 1)
    low = jnp.where(core == 0, mine, other).reshape(blocks, half)
    high = jnp.where(core == 0, other, mine).reshape(blocks, half)
    return codes, jnp.concatenate([low, high], axis=1).reshape(rows)


def solution(mesh):
    return jax.shard_map(
        local,
        mesh=mesh,
        in_specs=(P("row", "col"),),
        out_specs=(P("row", None), P("row")),
        check_vma=False,
    )
```

time: 293 us -> 152 us (0.52)
  waiting for transfers between devices: 178 us -> 42 us
  Pallas kernels: 0 us -> 40.3 us
  blocking collectives: 57.5 us -> 20.8 us
  starting transfers between devices: 8.48 us -> 39.1 us
  local copies, waits for them, and re-layouts: 21.2 us -> 7.66 us
  between operations: 14 us -> 0.84 us
  other arithmetic: 11 us -> 0.36 us
    all_gather x1 -> x0, waiting for transfers between devices: 107 us -> none  [local(): codes = lax.all_gather(local_codes, 'col', axis=1, tiled=True)]
    pallas_call x0 -> x13, Pallas kernels: none -> 40.3 us  [the longest x6 21.3 us: last_rotation(): pl.pallas_call(functools.partial(last_kernel, order, norm), grid_spec=gri...]
    pmax x1 -> x0, blocking collectives: 35.6 us -> none  [local(): peak = lax.pmax(jnp.max(jnp.abs(rotated), axis=1), 'col')]
    ppermute x4 -> x32, starting transfers between devices: 8.44 us -> 39.1 us  [swapped(): return lax.ppermute(value, axis, pairs)]
    ppermute x4 -> x32, waiting for transfers between devices: 70.1 us -> 42 us  [swapped(): return lax.ppermute(value, axis, pairs)]
    unnamed x7 -> x12, local copies, waits for them, and re-layouts: 21.2 us -> 4.78 us
    convert_element_type x4 -> x0, other arithmetic: 9.15 us -> none  [the longest x3 6.22 us: local(): partial_rot.astype(jnp.bfloat16)]
  transfers between devices with their start and end apart: 5 -> 32, of which waited for: 5 -> 9; matrix products, arithmetic and copies ran while one was open for 0% -> 1% of each run, Pallas kernels for 0% -> 24%
where the time goes in v1:
time: 152 us; the launch traced here: 151 us
  waiting for transfers between devices  42 us (28%)
  Pallas kernels  40.3 us (27%)
  starting transfers between devices  39.1 us (26%)
  blocking collectives  20.8 us (14%)
  local copies, waits for them, and re-layouts  7.66 us (5%)
    ppermute x32, waiting for transfers between devices, swapped(): return lax.ppermute(value, axis, pairs)  42 us
    ppermute x32, starting transfers between devices, swapped(): return lax.ppermute(value, axis, pairs)  39.1 us
    pallas_call x6, Pallas kernels, last_rotation(): pl.pallas_call(functools.partial(last_kernel, order, norm), grid_spec=gri...  21.3 us
    all_to_all x1, blocking collectives, local(): part = lax.all_to_all(part, 'row', split_axis=0, concat_axis=0, tiled=True)  20.8 us
    pallas_call x6, Pallas kernels, store(): pl.pallas_call(store_kernel, grid_spec=grid, out_shape=jax.ShapeDtypeStru...  17.6 us
    unnamed x12, local copies, waits for them, and re-layouts  4.78 us
  transfers between devices with their start and end apart: 32, of which 9 were waited for; matrix products, arithmetic and copies ran while one was open for 1% of the time, Pallas kernels for 24%

profile of v1, /device:TPU:1, one launch (start us, length us, event | category | flops | bytes accessed | tf_op | source)
XLA Modules:
  0.0 151.0 jit_solution(17616975407877025252)
XLA Ops:
  8.4 20.8 %all_to_all.5 = bf16[8,32,2048]{2,1,0:T(8,128)(2,1)S(1)} all-to-all(bf16[8,32,2048]{2,1,0:T(8,128)(2,1)S(1)} %first_rotation.1), channel_id=1, replica_groups=mesh['col'=16,'row'=8] {'row'}, dimensions={0} | all-to-all | bytes 2097152 | tf_op jit(solution)/shard_map/all_to_all | solution.py:217
  30.7 2.7 %collective-permute-start.9 = (bf16[32,2048]{1,0:T(8,128)(2,1)S(1)}, bf16[32,2048]{1,0:T(8,128)(2,1)S(1)}, u32[]{:S(2)}, u32[]{:S(2)}) collective-permute-start(bf16[32,2048]{1,0:T(8,128)(2,1)S(1)} %get-tuple-element.48), channel_id=1, source_target_pairs={{0,64},{8,72},{16,80},{24,88},{32,96},{40,104},{48,112},{56,120},{... | collective-permute-start | bytes 393224 | tf_op jit(solution)/shard_map/ppermute | solution.py:36
  34.0 2.5 %collective-permute-start.13 = (bf16[48,2048]{1,0:T(8,128)(2,1)S(1)}, bf16[48,2048]{1,0:T(8,128)(2,1)S(1)}, u32[]{:S(2)}, u32[]{:S(2)}) collective-permute-start(bf16[48,2048]{1,0:T(8,128)(2,1)S(1)} %get-tuple-element.44), channel_id=1, source_target_pairs={{0,48},{8,56},{16,32},{24,40},{32,16},{40,24},{48,0},{56,8},{64,11... | collective-permute-start | bytes 589832 | tf_op jit(solution)/shard_map/ppermute | solution.py:36
  36.7 4.9 %collective-permute-done.21 = bf16[48,2048]{1,0:T(8,128)(2,1)S(1)} collective-permute-done((bf16[48,2048]{1,0:T(8,128)(2,1)S(1)}, bf16[48,2048]{1,0:T(8,128)(2,1)S(1)}, u32[]{:S(2)}, u32[]{:S(2)}) %collective-permute-start.21) | collective-permute-done | bytes 196640 | tf_op jit(solution)/shard_map/ppermute | solution.py:36
  41.6 1.8 %collective-permute-start.6 = (bf16[2,32,2048]{2,1,0:T(8,128)(2,1)S(1)}, bf16[2,32,2048]{2,1,0:T(8,128)(2,1)S(1)}, u32[]{:S(2)}, u32[]{:S(2)}) collective-permute-start(bf16[2,32,2048]{2,1,0:T(8,128)(2,1)S(1)} %pad_maximum_fusion.4.c2), channel_id=1, source_target_pairs={{0,48},{8,56},{16,32},{24,40},{32,16},{40,24},{48,0},{56,8},{64,11... | collective-permute-start | bytes 786440 | tf_op jit(solution)/shard_map/ppermute | solution.py:36
  44.6 2.1 %collective-permute-start.23 = (bf16[2,48,2048]{2,1,0:T(8,128)(2,1)S(1)}, bf16[2,48,2048]{2,1,0:T(8,128)(2,1)S(1)}, u32[]{:S(2)}, u32[]{:S(2)}) collective-permute-start(bf16[2,48,2048]{2,1,0:T(8,128)(2,1)S(1)} %pad_maximum_fusion.3.c2), channel_id=1, source_target_pairs={{0,48},{8,56},{16,32},{24,40},{32,16},{40,24},{48,0},{56,8},{64,11... | collective-permute-start | bytes 1179656 | tf_op jit(solution)/shard_map/ppermute | solution.py:36
  46.8 5.1 %collective-permute-done.22.r2 = bf16[2,48,2048]{2,1,0:T(8,128)(2,1)S(1)} collective-permute-done((bf16[2,48,2048]{2,1,0:T(8,128)(2,1)S(1)}, bf16[2,48,2048]{2,1,0:T(8,128)(2,1)S(1)}, u32[]{:S(2)}, u32[]{:S(2)}) %collective-permute-start.22) | collective-permute-done | bytes 393248 | tf_op jit(solution)/shard_map/ppermute | solution.py:36
  53.0 3.6 %collective-permute-done.11.r3a = bf16[2,32,2048]{2,1,0:T(8,128)(2,1)S(1)} collective-permute-done((bf16[2,32,2048]{2,1,0:T(8,128)(2,1)S(1)}, bf16[2,32,2048]{2,1,0:T(8,128)(2,1)S(1)}, u32[]{:S(2)}, u32[]{:S(2)}) %collective-permute-start.11) | collective-permute-done | bytes 262176 | tf_op jit(solution)/shard_map/ppermute | solution.py:36
  58.3 6.9 %collective-permute-done.23.r3a = bf16[2,48,2048]{2,1,0:T(8,128)(2,1)S(1)} collective-permute-done((bf16[2,48,2048]{2,1,0:T(8,128)(2,1)S(1)}, bf16[2,48,2048]{2,1,0:T(8,128)(2,1)S(1)}, u32[]{:S(2)}, u32[]{:S(2)}) %collective-permute-start.23) | collective-permute-done | bytes 393248 | tf_op jit(solution)/shard_map/ppermute | solution.py:36
  65.2 2.0 %collective-permute-start.18 = (bf16[2,48,2048]{2,1,0:T(8,128)(2,1)S(1)}, bf16[2,48,2048]{2,1,0:T(8,128)(2,1)}, u32[]{:S(2)}, u32[]{:S(2)}) collective-permute-start(bf16[2,48,2048]{2,1,0:T(8,128)(2,1)S(1)} %pad_maximum_fusion.2.c2), channel_id=1, source_target_pairs={{0,48},{8,56},{16,32},{24,40},{32,16},{40,24},{48,0},{56,8},{64,11... | collective-permute-start | bytes 1179656 | tf_op jit(solution)/shard_map/ppermute | solution.py:36
  67.1 6.4 %collective-permute-done.24.r3b = bf16[2,48,2048]{2,1,0:T(8,128)(2,1)S(1)} collective-permute-done((bf16[2,48,2048]{2,1,0:T(8,128)(2,1)S(1)}, bf16[2,48,2048]{2,1,0:T(8,128)(2,1)S(1)}, u32[]{:S(2)}, u32[]{:S(2)}) %collective-permute-start.24) | collective-permute-done | bytes 393248 | tf_op jit(solution)/shard_map/ppermute | solution.py:36
  73.7 3.3 %last_rotation.6 = (bf16[512,16384]{1,0:T(8,128)(2,1)}, bf16[48,16384]{1,0:T(8,128)(2,1)}, f32[48,128]{1,0:T(8,128)S(1)}) custom-call(s32[2]{0:T(128)S(1)} %pad_add_fusion.where_ref, bf16[2,48,2048]{2,1,0:T(8,128)(2,1)S(1)} %pad_maximum_fusion.3.c2, bf16[2,48,2048]{2,1,0:T(8,128)(2,1)S(1)} %collective-permute-done.22.r2, ...), custom_call_target="tpu_custom_call" | custom-call | flops 6291456 | bytes 4718592 | tf_op jit(solution)/shard_map/last_rotation/pallas_call | solution.py:159
  77.0 2.9 %collective-permute-start.30 = (bf16[48,16384]{1,0:T(8,128)(2,1)}, bf16[48,16384]{1,0:T(8,128)(2,1)S(1)}, u32[]{:S(2)}, u32[]{:S(2)}) collective-permute-start(bf16[48,16384]{1,0:T(8,128)(2,1)} %get-tuple-element.30), channel_id=1, source_target_pairs={{0,8},{8,0},{16,24},{24,16},{32,40},{40,32},{48,56},{56,48},{64,72... | collective-permute-start | bytes 4718600 | tf_op jit(solution)/shard_map/ppermute | solution.py:36
  79.8 4.7 %collective-permute-start.19 = (bf16[2,48,2048]{2,1,0:T(8,128)(2,1)S(1)}, bf16[2,48,2048]{2,1,0:T(8,128)(2,1)S(1)}, u32[]{:S(2)}, u32[]{:S(2)}) collective-permute-start(bf16[2,48,2048]{2,1,0:T(8,128)(2,1)S(1)} %pad_maximum_fusion.2.c2), channel_id=1, source_target_pairs={{0,64},{8,72},{16,80},{24,88},{32,96},{40,104},{48,112},{56,120},{... | collective-permute-start | bytes 1179656 | tf_op jit(solution)/shard_map/ppermute | solution.py:36
  86.0 2.6 %collective-permute-start.12 = (bf16[2,32,2048]{2,1,0:T(8,128)(2,1)}, bf16[2,32,2048]{2,1,0:T(8,128)(2,1)S(1)}, u32[]{:S(2)}, u32[]{:S(2)}) collective-permute-start(bf16[2,32,2048]{2,1,0:T(8,128)(2,1)} %collective-permute-done.10.r2), channel_id=1, source_target_pairs={{0,48},{8,56},{16,32},{24,40},{32,16},{40,24},{48,0},{56,8},{64,11... | collective-permute-start | bytes 786440 | tf_op jit(solution)/shard_map/ppermute | solution.py:36
  88.6 5.3 %collective-permute-done.19.r3a = bf16[2,48,2048]{2,1,0:T(8,128)(2,1)S(1)} collective-permute-done((bf16[2,48,2048]{2,1,0:T(8,128)(2,1)S(1)}, bf16[2,48,2048]{2,1,0:T(8,128)(2,1)S(1)}, u32[]{:S(2)}, u32[]{:S(2)}) %collective-permute-start.19) | collective-permute-done | bytes 393248 | tf_op jit(solution)/shard_map/ppermute | solution.py:36
  95.4 2.8 %collective-permute-start.7 = (bf16[2,32,2048]{2,1,0:T(8,128)(2,1)S(1)}, bf16[2,32,2048]{2,1,0:T(8,128)(2,1)S(1)}, u32[]{:S(2)}, u32[]{:S(2)}) collective-permute-start(bf16[2,32,2048]{2,1,0:T(8,128)(2,1)S(1)} %pad_maximum_fusion.4.c2), channel_id=1, source_target_pairs={{0,64},{8,72},{16,80},{24,88},{32,96},{40,104},{48,112},{56,120},{... | collective-permute-start | bytes 786440 | tf_op jit(solution)/shard_map/ppermute | solution.py:36
  98.2 4.2 %collective-permute-done.20.r3b = bf16[2,48,2048]{2,1,0:T(8,128)(2,1)S(1)} collective-permute-done((bf16[2,48,2048]{2,1,0:T(8,128)(2,1)}, bf16[2,48,2048]{2,1,0:T(8,128)(2,1)S(1)}, u32[]{:S(2)}, u32[]{:S(2)}) %collective-permute-start.20) | collective-permute-done | bytes 393248 | tf_op jit(solution)/shard_map/ppermute | solution.py:36
  102.4 2.8 %collective-permute-start.8 = (bf16[2,32,2048]{2,1,0:T(8,128)(2,1)S(1)}, bf16[2,32,2048]{2,1,0:T(8,128)(2,1)S(1)}, u32[]{:S(2)}, u32[]{:S(2)}) collective-permute-start(bf16[2,32,2048]{2,1,0:T(8,128)(2,1)S(1)} %collective-permute-done.6.r2), channel_id=1, source_target_pairs={{0,64},{8,72},{16,80},{24,88},{32,96},{40,104},{48,112},{56,120},{... | collective-permute-start | bytes 786440 | tf_op jit(solution)/shard_map/ppermute | solution.py:36
  105.2 4.2 %last_rotation.7 = (bf16[512,16384]{1,0:T(8,128)(2,1)}, bf16[48,16384]{1,0:T(8,128)(2,1)}, f32[48,128]{1,0:T(8,128)S(1)}) custom-call(s32[2]{0:T(128)S(1)} %pad_add_fusion.where_ref, bf16[2,48,2048]{2,1,0:T(8,128)(2,1)S(1)} %pad_maximum_fusion.2.c2, bf16[2,48,2048]{2,1,0:T(8,128)(2,1)} %collective-permute-done.18.r2, ...), custom_call_target="tpu_custom_call", output_to_operand_aliasing={{0}: (5, {})} | custom-call | flops 6291456 | bytes 4718592 | tf_op jit(solution)/shard_map/last_rotation/pallas_call | solution.py:159
  109.4 4.5 %last_rotation.8 = (bf16[512,16384]{1,0:T(8,128)(2,1)}, bf16[48,16384]{1,0:T(8,128)(2,1)}, f32[48,128]{1,0:T(8,128)S(1)}) custom-call(s32[2]{0:T(128)S(1)} %pad_add_fusion.where_ref, bf16[2,48,2048]{2,1,0:T(8,128)(2,1)S(1)} %pad_maximum_fusion.1.c2, bf16[2,48,2048]{2,1,0:T(8,128)(2,1)} %collective-permute-done.14.r2, ...), custom_call_target="tpu_custom_call", output_to_operand_aliasing={{0}: (5, {})} | custom-call | flops 6291456 | bytes 4718592 | tf_op jit(solution)/shard_map/last_rotation/pallas_call | solution.py:159
  113.9 2.9 %last_rotation.9 = (bf16[512,16384]{1,0:T(8,128)(2,1)}, bf16[32,16384]{1,0:T(8,128)(2,1)S(1)}, f32[32,128]{1,0:T(8,128)S(1)}) custom-call(s32[2]{0:T(128)S(1)} %pad_add_fusion.where_ref, bf16[2,32,2048]{2,1,0:T(8,128)(2,1)S(1)} %pad_maximum_fusion.5.c2, bf16[2,32,2048]{2,1,0:T(8,128)(2,1)} %collective-permute-done.10.r2, ...), custom_call_target="tpu_custom_call", output_to_operand_aliasing={{0}: (5, {})} | custom-call | flops 4194304 | bytes 3145728 | tf_op jit(solution)/shard_map/last_rotation/pallas_call | solution.py:159
  117.8 2.2 %last_rotation.10 = (bf16[512,16384]{1,0:T(8,128)(2,1)}, bf16[32,16384]{1,0:T(8,128)(2,1)S(1)}, f32[32,128]{1,0:T(8,128)S(1)}) custom-call(s32[2]{0:T(128)S(1)} %pad_add_fusion.where_ref, bf16[2,32,2048]{2,1,0:T(8,128)(2,1)S(1)} %pad_maximum_fusion.4.c2, bf16[2,32,2048]{2,1,0:T(8,128)(2,1)S(1)} %collective-permute-done.6.r2, ...), custom_call_target="tpu_custom_call", output_to_operand_aliasing={{0}: (5, {})} | custom-call | flops 4194304 | bytes 3145728 | tf_op jit(solution)/shard_map/last_rotation/pallas_call | solution.py:159
  120.9 4.2 %last_rotation.11 = (bf16[512,16384]{1,0:T(8,128)(2,1)}, bf16[48,16384]{1,0:T(8,128)(2,1)}, f32[48,128]{1,0:T(8,128)S(1)}) custom-call(s32[2]{0:T(128)S(1)} %pad_add_fusion.where_ref, bf16[2,48,2048]{2,1,0:T(8,128)(2,1)S(1)} %pad_maximum_fusion.c2, bf16[2,48,2048]{2,1,0:T(8,128)(2,1)} %collective-permute-done.2.r2, ...), custom_call_target="tpu_custom_call", output_to_operand_aliasing={{0}: (5, {})} | custom-call | flops 6291456 | bytes 4718592 | tf_op jit(solution)/shard_map/last_rotation/pallas_call | solution.py:159
  125.1 1.6 %collective-permute-start.25 = (bf16[48,16384]{1,0:T(8,128)(2,1)}, bf16[48,16384]{1,0:T(8,128)(2,1)S(1)}, u32[]{:S(2)}, u32[]{:S(2)}) collective-permute-start(bf16[48,16384]{1,0:T(8,128)(2,1)} %get-tuple-element.25), channel_id=1, source_target_pairs={{0,8},{8,0},{16,24},{24,16},{32,40},{40,32},{48,56},{56,48},{64,72... | collective-permute-start | bytes 4718600 | tf_op jit(solution)/shard_map/ppermute | solution.py:36
  128.1 3.9 %collective-permute-done.31 = f32[256]{0:T(256)S(1)} collective-permute-done((f32[256]{0:T(256)S(1)}, f32[256]{0:T(256)S(1)}, u32[]{:S(2)}, u32[]{:S(2)}) %collective-permute-start.31) | collective-permute-done | bytes 1056 | tf_op jit(solution)/shard_map/ppermute | solution.py:36
  133.4 2.2 %store_codes.6.out_in = bf16[512,16384]{1,0:T(8,128)(2,1)} custom-call(s32[2]{0:T(128)S(1)} %pad_add_fusion.where_ref, bf16[48,16384]{1,0:T(8,128)(2,1)S(1)} %collective-permute-done.30.got_ref, bf16[512,16384]{1,0:T(8,128)(2,1)} %get-tuple-element.31.out_in), custom_call_target="tpu_custom_call", output_to_operand_aliasing={{}: (2, {})} | custom-call | bytes 3145728 | tf_op jit(solution)/shard_map/store_codes/pallas_call | solution.py:193
  135.7 3.9 %store_codes.7.out_in = bf16[512,16384]{1,0:T(8,128)(2,1)} custom-call(s32[2]{0:T(128)S(1)} %pad_add_fusion.where_ref, bf16[48,16384]{1,0:T(8,128)(2,1)} %collective-permute-done.29.got_ref, bf16[512,16384]{1,0:T(8,128)(2,1)} %store_codes.6.out_in), custom_call_target="tpu_custom_call", output_to_operand_aliasing={{}: (2, {})} | custom-call | bytes 3145728 | tf_op jit(solution)/shard_map/store_codes/pallas_call | solution.py:193
  139.6 3.9 %store_codes.8.out_in = bf16[512,16384]{1,0:T(8,128)(2,1)} custom-call(s32[2]{0:T(128)S(1)} %pad_add_fusion.where_ref, bf16[48,16384]{1,0:T(8,128)(2,1)} %collective-permute-done.28.got_ref, bf16[512,16384]{1,0:T(8,128)(2,1)} %store_codes.7.out_in), custom_call_target="tpu_custom_call", output_to_operand_aliasing={{}: (2, {})} | custom-call | bytes 3145728 | tf_op jit(solution)/shard_map/store_codes/pallas_call | solution.py:193
  143.5 2.6 %store_codes.9.out_in = bf16[512,16384]{1,0:T(8,128)(2,1)} custom-call(s32[2]{0:T(128)S(1)} %pad_add_fusion.where_ref, bf16[32,16384]{1,0:T(8,128)(2,1)} %collective-permute-done.27.got_ref, bf16[512,16384]{1,0:T(8,128)(2,1)} %store_codes.8.out_in), custom_call_target="tpu_custom_call", output_to_operand_aliasing={{}: (2, {})} | custom-call | bytes 2097152 | tf_op jit(solution)/shard_map/store_codes/pallas_call | solution.py:193
  146.1 2.6 %store_codes.10.out_in = bf16[512,16384]{1,0:T(8,128)(2,1)} custom-call(s32[2]{0:T(128)S(1)} %pad_add_fusion.where_ref, bf16[32,16384]{1,0:T(8,128)(2,1)} %collective-permute-done.26.got_ref, bf16[512,16384]{1,0:T(8,128)(2,1)} %store_codes.9.out_in), custom_call_target="tpu_custom_call", output_to_operand_aliasing={{}: (2, {})} | custom-call | bytes 2097152 | tf_op jit(solution)/shard_map/store_codes/pallas_call | solution.py:193
  148.8 2.2 %store_codes.11 = bf16[512,16384]{1,0:T(8,128)(2,1)} custom-call(s32[2]{0:T(128)S(1)} %pad_add_fusion.where_ref, bf16[48,16384]{1,0:T(8,128)(2,1)S(1)} %collective-permute-done.25.got_ref, bf16[512,16384]{1,0:T(8,128)(2,1)} %store_codes.10.out_in), custom_call_target="tpu_custom_call", output_to_operand_aliasing={{}: (2, {})} | custom-call | bytes 3145728 | tf_op jit(solution)/shard_map/store_codes/pallas_call | solution.py:193
  (80 shorter events, 21.7 us)
Async XLA Ops:
  1.7 3.0 %collective-permute-start = (bf16[8,32,1024]{2,1,0:T(8,128)(2,1)S(1)}, bf16[8,32,1024]{2,1,0:T(8,128)(2,1)S(1)}, u32[]{:S(2)}, u32[]{:S(2)}) collective-permute-start(bf16[8,32,1024]{2,1,0:T(8,128)(2,1)S(1)} %constant_dynamic-slice_fusion), channel_id=1, source_target_pairs={{0,8},{8,0},{16,24},{24,16},{32,40},{40,32},{48,56},{56,48},{64,72... | collective-permute-start | bytes 1572872 | tf_op jit(solution)/shard_map/ppermute | solution.py:36
  29.2 7.3 %collective-permute-start.5 = (bf16[32,2048]{1,0:T(8,128)(2,1)S(1)}, bf16[32,2048]{1,0:T(8,128)(2,1)S(1)}, u32[]{:S(2)}, u32[]{:S(2)}) collective-permute-start(bf16[32,2048]{1,0:T(8,128)(2,1)S(1)} %get-tuple-element.49), channel_id=1, source_target_pairs={{0,16},{8,24},{16,0},{24,8},{32,48},{40,56},{48,32},{56,40},{64,80... | collective-permute-start | bytes 393224 | tf_op jit(solution)/shard_map/ppermute | solution.py:36
  30.7 12.8 %collective-permute-start.9 = (bf16[32,2048]{1,0:T(8,128)(2,1)S(1)}, bf16[32,2048]{1,0:T(8,128)(2,1)S(1)}, u32[]{:S(2)}, u32[]{:S(2)}) collective-permute-start(bf16[32,2048]{1,0:T(8,128)(2,1)S(1)} %get-tuple-element.48), channel_id=1, source_target_pairs={{0,64},{8,72},{16,80},{24,88},{32,96},{40,104},{48,112},{56,120},{... | collective-permute-start | bytes 393224 | tf_op jit(solution)/shard_map/ppermute | solution.py:36
  33.4 8.2 %collective-permute-start.21 = (bf16[48,2048]{1,0:T(8,128)(2,1)S(1)}, bf16[48,2048]{1,0:T(8,128)(2,1)S(1)}, u32[]{:S(2)}, u32[]{:S(2)}) collective-permute-start(bf16[48,2048]{1,0:T(8,128)(2,1)S(1)} %get-tuple-element.42), channel_id=1, source_target_pairs={{0,64},{8,72},{16,80},{24,88},{32,96},{40,104},{48,112},{56,120},{... | collective-permute-start | bytes 589832 | tf_op jit(solution)/shard_map/ppermute | solution.py:36
  33.7 10.1 %collective-permute-start.17 = (bf16[48,2048]{1,0:T(8,128)(2,1)S(1)}, bf16[48,2048]{1,0:T(8,128)(2,1)S(1)}, u32[]{:S(2)}, u32[]{:S(2)}) collective-permute-start(bf16[48,2048]{1,0:T(8,128)(2,1)S(1)} %get-tuple-element.43), channel_id=1, source_target_pairs={{0,16},{8,24},{16,0},{24,8},{32,48},{40,56},{48,32},{56,40},{64,80... | collective-permute-start | bytes 589832 | tf_op jit(solution)/shard_map/ppermute | solution.py:36
  34.0 18.8 %collective-permute-start.13 = (bf16[48,2048]{1,0:T(8,128)(2,1)S(1)}, bf16[48,2048]{1,0:T(8,128)(2,1)S(1)}, u32[]{:S(2)}, u32[]{:S(2)}) collective-permute-start(bf16[48,2048]{1,0:T(8,128)(2,1)S(1)} %get-tuple-element.44), channel_id=1, source_target_pairs={{0,48},{8,56},{16,32},{24,40},{32,16},{40,24},{48,0},{56,8},{64,11... | collective-permute-start | bytes 589832 | tf_op jit(solution)/shard_map/ppermute | solution.py:36
  36.4 8.2 %collective-permute-start.1 = (bf16[48,2048]{1,0:T(8,128)(2,1)S(1)}, bf16[48,2048]{1,0:T(8,128)(2,1)S(1)}, u32[]{:S(2)}, u32[]{:S(2)}) collective-permute-start(bf16[48,2048]{1,0:T(8,128)(2,1)S(1)} %get-tuple-element.45), channel_id=1, source_target_pairs={{0,48},{8,56},{16,32},{24,40},{32,16},{40,24},{48,0},{56,8},{64,11... | collective-permute-start | bytes 589832 | tf_op jit(solution)/shard_map/ppermute | solution.py:36
  41.6 11.3 %collective-permute-start.6 = (bf16[2,32,2048]{2,1,0:T(8,128)(2,1)S(1)}, bf16[2,32,2048]{2,1,0:T(8,128)(2,1)S(1)}, u32[]{:S(2)}, u32[]{:S(2)}) collective-permute-start(bf16[2,32,2048]{2,1,0:T(8,128)(2,1)S(1)} %pad_maximum_fusion.4.c2), channel_id=1, source_target_pairs={{0,48},{8,56},{16,32},{24,40},{32,16},{40,24},{48,0},{56,8},{64,11... | collective-permute-start | bytes 786440 | tf_op jit(solution)/shard_map/ppermute | solution.py:36
  43.4 8.4 %collective-permute-start.22 = (bf16[2,48,2048]{2,1,0:T(8,128)(2,1)S(1)}, bf16[2,48,2048]{2,1,0:T(8,128)(2,1)S(1)}, u32[]{:S(2)}, u32[]{:S(2)}) collective-permute-start(bf16[2,48,2048]{2,1,0:T(8,128)(2,1)S(1)} %pad_maximum_fusion.3.c2), channel_id=1, source_target_pairs={{0,16},{8,24},{16,0},{24,8},{32,48},{40,56},{48,32},{56,40},{64,80... | collective-permute-start | bytes 1179656 | tf_op jit(solution)/shard_map/ppermute | solution.py:36
  43.9 12.8 %collective-permute-start.11 = (bf16[2,32,2048]{2,1,0:T(8,128)(2,1)S(1)}, bf16[2,32,2048]{2,1,0:T(8,128)(2,1)S(1)}, u32[]{:S(2)}, u32[]{:S(2)}) collective-permute-start(bf16[2,32,2048]{2,1,0:T(8,128)(2,1)S(1)} %pad_maximum_fusion.5.c2), channel_id=1, source_target_pairs={{0,48},{8,56},{16,32},{24,40},{32,16},{40,24},{48,0},{56,8},{64,11... | collective-permute-start | bytes 786440 | tf_op jit(solution)/shard_map/ppermute | solution.py:36
  44.6 20.5 %collective-permute-start.23 = (bf16[2,48,2048]{2,1,0:T(8,128)(2,1)S(1)}, bf16[2,48,2048]{2,1,0:T(8,128)(2,1)S(1)}, u32[]{:S(2)}, u32[]{:S(2)}) collective-permute-start(bf16[2,48,2048]{2,1,0:T(8,128)(2,1)S(1)} %pad_maximum_fusion.3.c2), channel_id=1, source_target_pairs={{0,48},{8,56},{16,32},{24,40},{32,16},{40,24},{48,0},{56,8},{64,11... | collective-permute-start | bytes 1179656 | tf_op jit(solution)/shard_map/ppermute | solution.py:36
  51.9 21.7 %collective-permute-start.24 = (bf16[2,48,2048]{2,1,0:T(8,128)(2,1)S(1)}, bf16[2,48,2048]{2,1,0:T(8,128)(2,1)S(1)}, u32[]{:S(2)}, u32[]{:S(2)}) collective-permute-start(bf16[2,48,2048]{2,1,0:T(8,128)(2,1)S(1)} %collective-permute-done.22.r2), channel_id=1, source_target_pairs={{0,48},{8,56},{16,32},{24,40},{32,16},{40,24},{48,0},{56,8},{64,11... | collective-permute-start | bytes 1179656 | tf_op jit(solution)/shard_map/ppermute | solution.py:36
  52.8 24.2 %collective-permute-start.10 = (bf16[2,32,2048]{2,1,0:T(8,128)(2,1)S(1)}, bf16[2,32,2048]{2,1,0:T(8,128)(2,1)}, u32[]{:S(2)}, u32[]{:S(2)}) collective-permute-start(bf16[2,32,2048]{2,1,0:T(8,128)(2,1)S(1)} %pad_maximum_fusion.5.c2), channel_id=1, source_target_pairs={{0,16},{8,24},{16,0},{24,8},{32,48},{40,56},{48,32},{56,40},{64,80... | collective-permute-start | bytes 786440 | tf_op jit(solution)/shard_map/ppermute | solution.py:36
  52.9 26.9 %collective-permute-start.2 = (bf16[2,48,2048]{2,1,0:T(8,128)(2,1)S(1)}, bf16[2,48,2048]{2,1,0:T(8,128)(2,1)}, u32[]{:S(2)}, u32[]{:S(2)}) collective-permute-start(bf16[2,48,2048]{2,1,0:T(8,128)(2,1)S(1)} %pad_maximum_fusion.c2), channel_id=1, source_target_pairs={{0,64},{8,72},{16,80},{24,88},{32,96},{40,104},{48,112},{56,120},{... | collective-permute-start | bytes 1179656 | tf_op jit(solution)/shard_map/ppermute | solution.py:36
  57.3 27.2 %collective-permute-start.14 = (bf16[2,48,2048]{2,1,0:T(8,128)(2,1)S(1)}, bf16[2,48,2048]{2,1,0:T(8,128)(2,1)}, u32[]{:S(2)}, u32[]{:S(2)}) collective-permute-start(bf16[2,48,2048]{2,1,0:T(8,128)(2,1)S(1)} %pad_maximum_fusion.1.c2), channel_id=1, source_target_pairs={{0,64},{8,72},{16,80},{24,88},{32,96},{40,104},{48,112},{56,120},{... | collective-permute-start | bytes 1179656 | tf_op jit(solution)/shard_map/ppermute | solution.py:36
  65.2 20.8 %collective-permute-start.18 = (bf16[2,48,2048]{2,1,0:T(8,128)(2,1)S(1)}, bf16[2,48,2048]{2,1,0:T(8,128)(2,1)}, u32[]{:S(2)}, u32[]{:S(2)}) collective-permute-start(bf16[2,48,2048]{2,1,0:T(8,128)(2,1)S(1)} %pad_maximum_fusion.2.c2), channel_id=1, source_target_pairs={{0,48},{8,56},{16,32},{24,40},{32,16},{40,24},{48,0},{56,8},{64,11... | collective-permute-start | bytes 1179656 | tf_op jit(solution)/shard_map/ppermute | solution.py:36
  73.6 12.5 %collective-permute-start.15 = (bf16[2,48,2048]{2,1,0:T(8,128)(2,1)S(1)}, bf16[2,48,2048]{2,1,0:T(8,128)(2,1)}, u32[]{:S(2)}, u32[]{:S(2)}) collective-permute-start(bf16[2,48,2048]{2,1,0:T(8,128)(2,1)S(1)} %pad_maximum_fusion.1.c2), channel_id=1, source_target_pairs={{0,16},{8,24},{16,0},{24,8},{32,48},{40,56},{48,32},{56,40},{64,80... | collective-permute-start | bytes 1179656 | tf_op jit(solution)/shard_map/ppermute | solution.py:36
  77.0 55.4 %collective-permute-start.30 = (bf16[48,16384]{1,0:T(8,128)(2,1)}, bf16[48,16384]{1,0:T(8,128)(2,1)S(1)}, u32[]{:S(2)}, u32[]{:S(2)}) collective-permute-start(bf16[48,16384]{1,0:T(8,128)(2,1)} %get-tuple-element.30), channel_id=1, source_target_pairs={{0,8},{8,0},{16,24},{24,16},{32,40},{40,32},{48,56},{56,48},{64,72... | collective-permute-start | bytes 4718600 | tf_op jit(solution)/shard_map/ppermute | solution.py:36
  79.8 14.1 %collective-permute-start.19 = (bf16[2,48,2048]{2,1,0:T(8,128)(2,1)S(1)}, bf16[2,48,2048]{2,1,0:T(8,128)(2,1)S(1)}, u32[]{:S(2)}, u32[]{:S(2)}) collective-permute-start(bf16[2,48,2048]{2,1,0:T(8,128)(2,1)S(1)} %pad_maximum_fusion.2.c2), channel_id=1, source_target_pairs={{0,64},{8,72},{16,80},{24,88},{32,96},{40,104},{48,112},{56,120},{... | collective-permute-start | bytes 1179656 | tf_op jit(solution)/shard_map/ppermute | solution.py:36
  84.6 10.9 %collective-permute-start.16 = (bf16[2,48,2048]{2,1,0:T(8,128)(2,1)}, bf16[2,48,2048]{2,1,0:T(8,128)(2,1)S(1)}, u32[]{:S(2)}, u32[]{:S(2)}) collective-permute-start(bf16[2,48,2048]{2,1,0:T(8,128)(2,1)} %collective-permute-done.14.r2), channel_id=1, source_target_pairs={{0,16},{8,24},{16,0},{24,8},{32,48},{40,56},{48,32},{56,40},{64,80... | collective-permute-start | bytes 1179656 | tf_op jit(solution)/shard_map/ppermute | solution.py:36
  86.0 16.4 %collective-permute-start.20 = (bf16[2,48,2048]{2,1,0:T(8,128)(2,1)}, bf16[2,48,2048]{2,1,0:T(8,128)(2,1)S(1)}, u32[]{:S(2)}, u32[]{:S(2)}) collective-permute-start(bf16[2,48,2048]{2,1,0:T(8,128)(2,1)} %collective-permute-done.18.r2), channel_id=1, source_target_pairs={{0,64},{8,72},{16,80},{24,88},{32,96},{40,104},{48,112},{56,120},{... | collective-permute-start | bytes 1179656 | tf_op jit(solution)/shard_map/ppermute | solution.py:36
  86.0 9.3 %collective-permute-start.12 = (bf16[2,32,2048]{2,1,0:T(8,128)(2,1)}, bf16[2,32,2048]{2,1,0:T(8,128)(2,1)S(1)}, u32[]{:S(2)}, u32[]{:S(2)}) collective-permute-start(bf16[2,32,2048]{2,1,0:T(8,128)(2,1)} %collective-permute-done.10.r2), channel_id=1, source_target_pairs={{0,48},{8,56},{16,32},{24,40},{32,16},{40,24},{48,0},{56,8},{64,11... | collective-permute-start | bytes 786440 | tf_op jit(solution)/shard_map/ppermute | solution.py:36
  94.0 26.0 %collective-permute-start.3 = (bf16[2,48,2048]{2,1,0:T(8,128)(2,1)S(1)}, bf16[2,48,2048]{2,1,0:T(8,128)(2,1)S(1)}, u32[]{:S(2)}, u32[]{:S(2)}) collective-permute-start(bf16[2,48,2048]{2,1,0:T(8,128)(2,1)S(1)} %pad_maximum_fusion.c2), channel_id=1, source_target_pairs={{0,16},{8,24},{16,0},{24,8},{32,48},{40,56},{48,32},{56,40},{64,80... | collective-permute-start | bytes 1179656 | tf_op jit(solution)/shard_map/ppermute | solution.py:36
  95.3 24.6 %collective-permute-start.4 = (bf16[2,48,2048]{2,1,0:T(8,128)(2,1)}, bf16[2,48,2048]{2,1,0:T(8,128)(2,1)S(1)}, u32[]{:S(2)}, u32[]{:S(2)}) collective-permute-start(bf16[2,48,2048]{2,1,0:T(8,128)(2,1)} %collective-permute-done.2.r2), channel_id=1, source_target_pairs={{0,16},{8,24},{16,0},{24,8},{32,48},{40,56},{48,32},{56,40},{64,80... | collective-permute-start | bytes 1179656 | tf_op jit(solution)/shard_map/ppermute | solution.py:36
  95.4 21.4 %collective-permute-start.7 = (bf16[2,32,2048]{2,1,0:T(8,128)(2,1)S(1)}, bf16[2,32,2048]{2,1,0:T(8,128)(2,1)S(1)}, u32[]{:S(2)}, u32[]{:S(2)}) collective-permute-start(bf16[2,32,2048]{2,1,0:T(8,128)(2,1)S(1)} %pad_maximum_fusion.4.c2), channel_id=1, source_target_pairs={{0,64},{8,72},{16,80},{24,88},{32,96},{40,104},{48,112},{56,120},{... | collective-permute-start | bytes 786440 | tf_op jit(solution)/shard_map/ppermute | solution.py:36
  102.4 14.4 %collective-permute-start.8 = (bf16[2,32,2048]{2,1,0:T(8,128)(2,1)S(1)}, bf16[2,32,2048]{2,1,0:T(8,128)(2,1)S(1)}, u32[]{:S(2)}, u32[]{:S(2)}) collective-permute-start(bf16[2,32,2048]{2,1,0:T(8,128)(2,1)S(1)} %collective-permute-done.6.r2), channel_id=1, source_target_pairs={{0,64},{8,72},{16,80},{24,88},{32,96},{40,104},{48,112},{56,120},{... | collective-permute-start | bytes 786440 | tf_op jit(solution)/shard_map/ppermute | solution.py:36
  125.1 23.6 %collective-permute-start.25 = (bf16[48,16384]{1,0:T(8,128)(2,1)}, bf16[48,16384]{1,0:T(8,128)(2,1)S(1)}, u32[]{:S(2)}, u32[]{:S(2)}) collective-permute-start(bf16[48,16384]{1,0:T(8,128)(2,1)} %get-tuple-element.25), channel_id=1, source_target_pairs={{0,8},{8,0},{16,24},{24,16},{32,40},{40,32},{48,56},{56,48},{64,72... | collective-permute-start | bytes 4718600 | tf_op jit(solution)/shard_map/ppermute | solution.py:36
  126.8 12.9 %collective-permute-start.28 = (bf16[48,16384]{1,0:T(8,128)(2,1)}, bf16[48,16384]{1,0:T(8,128)(2,1)}, u32[]{:S(2)}, u32[]{:S(2)}) collective-permute-start(bf16[48,16384]{1,0:T(8,128)(2,1)} %get-tuple-element.28), channel_id=1, source_target_pairs={{0,8},{8,0},{16,24},{24,16},{32,40},{40,32},{48,56},{56,48},{64,72... | collective-permute-start | bytes 4718600 | tf_op jit(solution)/shard_map/ppermute | solution.py:36
  126.8 8.9 %collective-permute-start.29 = (bf16[48,16384]{1,0:T(8,128)(2,1)}, bf16[48,16384]{1,0:T(8,128)(2,1)}, u32[]{:S(2)}, u32[]{:S(2)}) collective-permute-start(bf16[48,16384]{1,0:T(8,128)(2,1)} %get-tuple-element.29), channel_id=1, source_target_pairs={{0,8},{8,0},{16,24},{24,16},{32,40},{40,32},{48,56},{56,48},{64,72... | collective-permute-start | bytes 4718600 | tf_op jit(solution)/shard_map/ppermute | solution.py:36
  128.0 4.0 %collective-permute-start.31 = (f32[256]{0:T(256)S(1)}, f32[256]{0:T(256)S(1)}, u32[]{:S(2)}, u32[]{:S(2)}) collective-permute-start(f32[256]{0:T(256)S(1)} %concatenate.6), channel_id=1, source_target_pairs={{0,8},{8,0},{16,24},{24,16},{32,40},{40,32},{48,56},{56,48},{64,72... | collective-permute-start | bytes 3080 | tf_op jit(solution)/shard_map/ppermute | solution.py:36
  132.0 11.5 %collective-permute-start.27 = (bf16[32,16384]{1,0:T(8,128)(2,1)}, bf16[32,16384]{1,0:T(8,128)(2,1)}, u32[]{:S(2)}, u32[]{:S(2)}) collective-permute-start(bf16[32,16384]{1,0:T(8,128)(2,1)} %copy-done.4), channel_id=1, source_target_pairs={{0,8},{8,0},{16,24},{24,16},{32,40},{40,32},{48,56},{56,48},{64,72... | collective-permute-start | bytes 3145736 | tf_op jit(solution)/shard_map/ppermute | solution.py:36
  132.4 13.8 %collective-permute-start.26 = (bf16[32,16384]{1,0:T(8,128)(2,1)}, bf16[32,16384]{1,0:T(8,128)(2,1)}, u32[]{:S(2)}, u32[]{:S(2)}) collective-permute-start(bf16[32,16384]{1,0:T(8,128)(2,1)} %copy-done.5), channel_id=1, source_target_pairs={{0,8},{8,0},{16,24},{24,16},{32,40},{40,32},{48,56},{56,48},{64,72... | collective-permute-start | bytes 3145736 | tf_op jit(solution)/shard_map/ppermute | solution.py:36
  (6 other events, 13.5 us)

commit v2 on v0

v2 whole, which is shorter than its diff:
```python
import functools

import jax
import jax.numpy as jnp
import numpy as np
from jax import lax
from jax.experimental import pallas as pl
from jax.experimental.pallas import tpu as pltpu
from jax.sharding import PartitionSpec as P

UNIT = 16
LANES = 256
BASE = 256
EXTRA = 128
GROUPS = 8
VMEM_LIMIT = 12 * 2**20
WORTH = pl.CostEstimate(flops=2*10**10, bytes_accessed=1, transcendentals=0)

STEPS = {"a": 1, "b": 3, "y": 4}


CHUNKS = (
    ((0,), "bay"),
    ((2, 6), "bay"),
    ((1,), "yba"),
    ((4,), "ayb"),
    ((3, 7), "yba"),
    ((5,), "yab"),
)

PLAN = (
    "z2", "m2", "z6", "g0", "g0", "z4", "g1", "m4", "g3", "g2", "g1", "m5", "g4", "g3", "g5",
    "g0", "g2", "g1", "g3", "g4", "g5", "k0", "k2", "k3", "k5r0", "k1", "k4r35", "r142",
)


def swapped(value, axis, mask):
    pairs = [(source, source ^ mask) for source in range(lax.axis_size(axis))]
    return lax.ppermute(value, axis, pairs)


def from_neighbours(value):
    height = lax.axis_size("row")
    far = 2 * STEPS["y"] * height + 1
    pairs = [(source, source ^ far) for source in range(lax.axis_size("col") * height)]
    return swapped(value, "row", 1), lax.ppermute(value, ("col", "row"), pairs)


def butterfly(parts):
    parts = list(parts)
    span = 1
    while span < len(parts):
        for i in range(len(parts)):
            if not i & span:
                a, b = parts[i], parts[i | span]
                parts[i], parts[i | span] = a + b, a - b
        span *= 2
    return parts


def whole(space=pltpu.VMEM):
    return pl.BlockSpec(memory_space=space)


def odd_bits(value, bits):
    total = value
    for bit in range(1, bits):
        total = total ^ (value >> bit)
    return total & 1


def first_kernel(where_ref, own_ref, got_ref, out_ref):
    sign = jnp.where(where_ref[0] == 0, 1.0, -1.0).astype(jnp.float32)
    me = where_ref[2]
    blocks, half, cols = got_ref.shape
    shape = (BASE, BASE)
    both = lax.broadcasted_iota(jnp.int32, shape, 0) & lax.broadcasted_iota(jnp.int32, shape, 1)
    both = both ^ (both >> 4)
    both = both ^ (both >> 2)
    both = both ^ (both >> 1)
    table = (1 - 2 * (both & 1)).astype(jnp.float32).astype(jnp.bfloat16)

    def rotated(value):
        value = value.reshape(blocks * half, cols)
        return butterfly(
            jnp.dot(value[:, c : c + BASE], table, preferred_element_type=jnp.float32)
            for c in range(0, cols, BASE)
        )

    for i, (a, b) in enumerate(zip(rotated(own_ref[...]), rotated(got_ref[...]))):
        low = (a + b).astype(out_ref.dtype)
        high = ((a - b) * sign).astype(out_ref.dtype)
        for block in range(blocks):
            rows = slice(block * half, (block + 1) * half)
            out_ref[block ^ me, :, i * BASE : (i + 1) * BASE] = low[rows]
            out_ref[block ^ me, :, cols + i * BASE : cols + (i + 1) * BASE] = high[rows]


def first_rotation(where, own, got):
    blocks, half, cols = got.shape
    return pl.pallas_call(
        first_kernel,
        in_specs=[whole(pltpu.SMEM), whole(), whole()],
        out_specs=whole(),
        out_shape=jax.ShapeDtypeStruct((blocks, half, 2 * cols), got.dtype),
        compiler_params=pltpu.CompilerParams(vmem_limit_bytes=VMEM_LIMIT),
        cost_estimate=WORTH,
        name="first_rotation",
    )(where, own, got)


def rotate(order, norm, where_ref, held_ref, got_ref, send_ref, scale_ref, work):
    d1, d2, d3 = order
    place = {}
    for ref, base in ((held_ref, 0), (got_ref, d3)):
        for j, other in enumerate((0, d1, d2, d2 ^ d1)):
            place[base ^ other] = (ref, j)
    cols = held_ref.shape[-1]
    me = where_ref[1]

    def step(unit, carry):
        rows = pl.ds(pl.multiple_of(unit * UNIT, UNIT), UNIT)
        peak = None
        for c in range(0, cols, LANES):
            parts = butterfly(
                place[i][0][place[i][1], rows, c : c + LANES].astype(jnp.float32)
                for i in range(GROUPS)
            )
            for k, part in enumerate(parts):
                work[k, :, c : c + LANES] = part
                part = jnp.abs(part)
                peak = part if peak is None else jnp.maximum(peak, part)
        scale = jnp.max(peak, axis=1, keepdims=True) * norm + 1e-06
        scale_ref[rows, :] = jnp.broadcast_to(scale, (UNIT, EXTRA))
        factor = norm / scale
        for k in range(GROUPS):
            signed = factor * jnp.where(odd_bits(me & k, 3) == 0, 1.0, -1.0).astype(jnp.float32)
            for c in range(0, cols, LANES):
                value = (work[k, :, c : c + LANES] * signed).astype(send_ref.dtype)
                send_ref[rows, k * cols + c : k * cols + c + LANES] = value
        high = scale.astype(jnp.bfloat16).astype(jnp.float32)
        mid = (scale - high).astype(jnp.bfloat16).astype(jnp.float32)
        low = scale - high - mid
        lane = lax.broadcasted_iota(jnp.int32, (UNIT, EXTRA), 1)
        terms = jnp.where(lane == 0, high, jnp.where(lane == 1, mid, low))
        send_ref[rows, GROUPS * cols :] = terms.astype(send_ref.dtype)
        return carry

    lax.fori_loop(0, held_ref.shape[1] // UNIT, step, 0)


def places(where_ref, pieces, half, side):
    core = where_ref[0] if side == 0 else 1 - where_ref[0]
    for j, piece in enumerate(pieces):
        start = (where_ref[2] ^ piece) * (2 * half) + core * half
        yield slice(j * half, (j + 1) * half), pl.ds(pl.multiple_of(start, half), half)


def codes_kernel(order, norm, stored, half, earlier, chained, where_ref, *refs):
    refs = list(refs)

    def take(count):
        taken, refs[:] = refs[:count], refs[count:]
        return taken

    inputs = take(2 if order else 0)
    pairs = [take(2) for _ in stored]
    scales = take(len(earlier))
    take(1 if chained else 0)
    outputs = take(2 if order else 0)
    copies = []
    if stored:
        (out_ref,) = take(1)
        wide = out_ref.shape[1]
        got_scale_refs = take(1 if earlier else len(stored))
        sems = refs[-1]
        for pieces, pair in zip(stored, pairs):
            for side, ref in enumerate(pair):
                for rows, place in places(where_ref, pieces, half, side):
                    copies.append(
                        pltpu.make_async_copy(
                            ref.at[rows, pl.ds(0, wide)], out_ref.at[place], sems.at[len(copies)]
                        )
                    )
    for copy in copies:
        copy.start()
    got_scales = []
    for _, got_ref in pairs:
        terms = got_ref[:, wide:].astype(jnp.float32)
        scale = (terms[:, :1] + terms[:, 1:2]) + terms[:, 2:3]
        got_scales.append(jnp.broadcast_to(scale, (scale.shape[0], EXTRA)))
    if order:
        rotate(order, norm, where_ref, *inputs, *outputs, refs[0])
    if earlier:
        table = refs[0]
        for (pieces, side), ref in zip(earlier, scales):
            for rows, place in places(where_ref, pieces, half, side):
                table[place, :] = ref[rows, :]
        for pieces, scale in zip(stored, got_scales):
            for rows, place in places(where_ref, pieces, half, 1):
                table[place, :] = scale[rows]
        shape = (EXTRA, EXTRA)
        row, lane = (lax.broadcasted_iota(jnp.int32, shape, axis) for axis in range(2))
        (scale_ref,) = got_scale_refs
        for q in range(scale_ref.shape[0]):
            block = table[q * EXTRA : (q + 1) * EXTRA, :]
            line = jnp.sum(jnp.where(row == lane, block, 0.0), axis=0, keepdims=True)
            scale_ref[q : q + 1, :] = line
    elif stored:
        for ref, scale in zip(got_scale_refs, got_scales):
            ref[...] = scale
    for copy in copies:
        copy.wait()


def codes_call(order, norm, inputs, stored, pairs, earlier, scales, out, where, half, full):
    dtype = jnp.bfloat16
    operands = [where, *inputs]
    for pair in pairs:
        operands.extend(pair)
    operands.extend(scales)
    in_specs = [whole(pltpu.SMEM)] + [whole()] * (len(operands) - 1)
    out_specs, out_shape, scratch, aliases = [], [], [], {}
    moved = 0
    if order:
        _, rows, cols = inputs[0].shape
        moved = rows // half
        out_specs += [whole(), whole()]
        out_shape += [
            jax.ShapeDtypeStruct((rows, GROUPS * cols + EXTRA), dtype),
            jax.ShapeDtypeStruct((rows, EXTRA), jnp.float32),
        ]
        scratch.append(pltpu.VMEM((GROUPS, UNIT, cols), jnp.float32))
    if earlier:
        scratch.append(pltpu.VMEM((full, EXTRA), jnp.float32))
    if stored:
        if out is not None:
            aliases = {len(operands): len(out_shape)}
            in_specs.append(whole(pl.ANY))
            operands.append(out)
        out_specs.append(whole(pl.ANY))
        out_shape.append(jax.ShapeDtypeStruct((full, pairs[0][0].shape[1] - EXTRA), dtype))
        heights = [full // EXTRA] if earlier else [own.shape[0] for own, _ in pairs]
        out_specs += [whole()] * len(heights)
        out_shape += [jax.ShapeDtypeStruct((rows, EXTRA), jnp.float32) for rows in heights]
        scratch.append(pltpu.SemaphoreType.DMA((2 * sum(len(pieces) for pieces in stored),)))
    return pl.pallas_call(
        functools.partial(codes_kernel, order, norm, stored, half, earlier, bool(aliases)),
        in_specs=in_specs,
        out_specs=out_specs,
        out_shape=out_shape,
        scratch_shapes=scratch,
        input_output_aliases=aliases,
        compiler_params=pltpu.CompilerParams(vmem_limit_bytes=VMEM_LIMIT),
        cost_estimate=WORTH,
        name=f"rotate{moved}_store{sum(len(pieces) for pieces in stored)}",
    )(*operands)


def local(weight):
    position = lax.axis_index("col")
    core = position % 2
    row = lax.axis_index("row")
    where = jnp.stack([core, position // 2, row])
    rows, cols = weight.shape
    blocks = lax.axis_size("row")
    block = rows // blocks
    half = block // 2
    norm = 1.0 / float(np.sqrt(cols * lax.axis_size("col")))

    weight = weight.reshape(blocks, block, cols)
    send = lax.dynamic_slice_in_dim(weight, (1 - core) * half, half, axis=1)
    own = lax.dynamic_slice_in_dim(weight, core * half, half, axis=1)
    part = first_rotation(where, own, swapped(send, "col", 1))

    token = part

    def after(value):
        return lax.optimization_barrier((value, token))[0]

    pieces = {0: part[0], 1: part[1]}
    held, got, taken = {}, {}, {}
    scales = {}
    codes = None
    for step in PLAN:
        kind, i = step[0], int(step[1])
        if kind == "z":
            token = after(part[i : i + 2])
            pair = swapped(token, "row", i)
            pieces[i], pieces[i + 1] = pair[0], pair[1]
            continue
        names, order = CHUNKS[i] if kind != "r" else ((), ())
        order = [STEPS[name] for name in order]
        if kind == "m":
            token = after(jnp.concatenate([pieces[name] for name in names])[None])
            held[i], got[i] = from_neighbours(token)
            taken[i] = 1
        elif kind == "g":
            turn = taken.get(i, 0)
            taken[i] = turn + 1
            if turn == 0:
                held[i] = jnp.concatenate([pieces[name] for name in names])[None]
            else:
                held[i] = jnp.concatenate([held[i], got[i]])
            token = held[i] = after(held[i])
            got[i] = swapped(token, "col", 2 * order[turn])
        else:
            ready = [int(name) for name in step.partition("r")[2]]
            stored = [CHUNKS[c][0] for c in ready]
            pairs = [(held[c], got[c]) for c in ready]
            earlier = dict(scales) if step == PLAN[-1] else {}
            inputs = ()
            if kind == "k":
                inputs = (held[i], after(got[i]))
            else:
                pairs[-1] = (pairs[-1][0], after(pairs[-1][1]))
            made = codes_call(
                order,
                norm,
                inputs,
                stored,
                pairs,
                list(earlier),
                list(earlier.values()),
                codes,
                where,
                half,
                rows,
            )
            if kind == "k":
                held[i], scales[names, 0], *made = made
                got[i] = swapped(held[i], "col", 1)
                token = held[i]
            if ready:
                codes, *made = made
                for pieces_of, scale in zip(stored, made):
                    scales[pieces_of, 1] = scale

    return codes, made[0].reshape(rows)


def solution(mesh):
    return jax.shard_map(
        local,
        mesh=mesh,
        in_specs=(P("row", "col"),),
        out_specs=(P("row", None), P("row")),
        check_vma=False,
    )
```

time: 293 us -> 104 us (0.35)
  waiting for transfers between devices: 178 us -> 26.9 us
  blocking collectives: 57.5 us -> 0 us
  starting transfers between devices: 8.48 us -> 58.2 us
  local copies, waits for them, and re-layouts: 21.2 us -> 1.45 us
  Pallas kernels: 0 us -> 16.1 us
  between operations: 14 us -> 0.88 us
  other arithmetic: 11 us -> 0.7 us
    all_gather x1 -> x0, waiting for transfers between devices: 107 us -> none  [local(): codes = lax.all_gather(local_codes, 'col', axis=1, tiled=True)]
    ppermute x4 -> x28, waiting for transfers between devices: 70.1 us -> 24.7 us  [swapped(): return lax.ppermute(value, axis, pairs)]
    ppermute x4 -> x28, starting transfers between devices: 8.44 us -> 53.8 us  [swapped(): return lax.ppermute(value, axis, pairs)]
    pmax x1 -> x0, blocking collectives: 35.6 us -> none  [local(): peak = lax.pmax(jnp.max(jnp.abs(rotated), axis=1), 'col')]
    all_to_all x1 -> x0, blocking collectives: 21.9 us -> none  [local(): lax.all_to_all(weight, 'row', split_axis=0, concat_axis=0, tiled=True)]
    unnamed x7 -> x0, local copies, waits for them, and re-layouts: 21.2 us -> none
    pallas_call x0 -> x8, Pallas kernels: none -> 16.1 us  [the longest x7 14.8 us: codes_call(): pl.pallas_call(functools.partial(codes_kernel, order, norm, stored, half,...]
    convert_element_type x4 -> x0, other arithmetic: 9.15 us -> none  [the longest x3 6.22 us: local(): partial_rot.astype(jnp.bfloat16)]
  transfers between devices with their start and end apart: 5 -> 31, of which waited for: 5 -> 14; matrix products, arithmetic and copies ran while one was open for 0% -> 1% of each run, Pallas kernels for 0% -> 9%
where the time goes in v2:
time: 104 us
  starting transfers between devices  58.2 us (56%)
  waiting for transfers between devices  26.9 us (26%)
  Pallas kernels  16.1 us (15%)
  local copies, waits for them, and re-layouts  1.45 us (1%)
    ppermute x28, starting transfers between devices, swapped(): return lax.ppermute(value, axis, pairs)  53.8 us
    ppermute x28, waiting for transfers between devices, swapped(): return lax.ppermute(value, axis, pairs)  24.7 us
    pallas_call x7, Pallas kernels, codes_call(): pl.pallas_call(functools.partial(codes_kernel, order, norm, stored, half,...  14.8 us
    ppermute x3, starting transfers between devices, from_neighbours(): lax.ppermute(value, ('col', 'row'), pairs)  4.42 us
    ppermute x3, waiting for transfers between devices, from_neighbours(): lax.ppermute(value, ('col', 'row'), pairs)  2.22 us
  transfers between devices with their start and end apart: 31, of which 14 were waited for; matrix products, arithmetic and copies ran while one was open for 1% of the time, Pallas kernels for 9%

profile of v2, /device:TPU:1, one launch (start us, length us, event | category | flops | bytes accessed | tf_op | source)
XLA Modules:
  0.0 104.3 jit_solution(949372585942588607)
XLA Ops:
  0.7 1.3 %constant_dynamic-slice_fusion = (bf16[8,32,1024]{2,1,0:T(8,128)(2,1)S(1)}, bf16[8,32,1024]{2,1,0:T(8,128)(2,1)S(1)}) fusion(bf16[8,64,1024]{2,1,0:T(8,128)(2,1)} %bitcast.17, s32[]{:T(128)S(6)} %select_n.20, s32[]{:T(128)S(6)} %select_n.19), kind=kLoop, calls=%fused_computation.19 | loop fusion | bytes 2097160 | tf_op jit(solution)/shard_map/dynamic_slice | solution.py:272
  2.0 1.5 %collective-permute-start = (bf16[8,32,1024]{2,1,0:T(8,128)(2,1)S(1)}, bf16[8,32,1024]{2,1,0:T(8,128)(2,1)S(1)}, u32[]{:S(2)}, u32[]{:S(2)}) collective-permute-start(bf16[8,32,1024]{2,1,0:T(8,128)(2,1)S(1)} %get-tuple-element.101), channel_id=1, source_target_pairs={{0,8},{8,0},{16,24},{24,16},{32,40},{40,32},{48,56},{56,48},{64,72... | collective-permute-start | bytes 1572872 | tf_op jit(solution)/shard_map/ppermute | solution.py:39
  3.5 1.5 %collective-permute-done.got_ref = bf16[8,32,1024]{2,1,0:T(8,128)(2,1)S(1)} collective-permute-done((bf16[8,32,1024]{2,1,0:T(8,128)(2,1)S(1)}, bf16[8,32,1024]{2,1,0:T(8,128)(2,1)S(1)}, u32[]{:S(2)}, u32[]{:S(2)}) %collective-permute-start) | collective-permute-done | bytes 524320 | tf_op jit(solution)/shard_map/ppermute | solution.py:39
  5.0 1.3 %first_rotation.1 = bf16[8,32,2048]{2,1,0:T(8,128)(2,1)S(1)} custom-call(s32[3]{0:T(128)S(1)} %pad_add_fusion.where_ref, bf16[8,32,1024]{2,1,0:T(8,128)(2,1)S(1)} %get-tuple-element.102.own_ref, bf16[8,32,1024]{2,1,0:T(8,128)(2,1)S(1)} %collective-permute-done.got_ref), custom_call_target="tpu_custom_call" | custom-call | flops 20000000000 | bytes 1 | tf_op jit(solution)/shard_map/first_rotation/pallas_call | solution.py:101
  6.4 2.6 %collective-permute-start.3 = (bf16[1,32,2048]{2,1,0:T(8,128)(2,1)S(1)}, bf16[1,32,2048]{2,1,0:T(8,128)(2,1)S(1)}, u32[]{:S(2)}, u32[]{:S(2)}) collective-permute-start(bf16[1,32,2048]{2,1,0:T(8,128)(2,1)S(1)} %get-tuple-element.52), channel_id=1, source_target_pairs={{0,48},{8,56},{16,32},{24,40},{32,16},{40,24},{48,0},{56,8},{64,11... | collective-permute-start | bytes 393224 | tf_op jit(solution)/shard_map/ppermute | solution.py:39
  9.0 3.8 %collective-permute-start.2 = (bf16[2,32,2048]{2,1,0:T(8,128)(2,1)S(1)}, bf16[2,32,2048]{2,1,0:T(8,128)(2,1)S(1)}, u32[]{:S(2)}, u32[]{:S(2)}) collective-permute-start(bf16[2,32,2048]{2,1,0:T(8,128)(2,1)S(1)} %get-tuple-element.51), channel_id=1, source_target_pairs={{0,6},{1,7},{2,4},{3,5},{4,2},{5,3},{6,0},{7,1},{8,14},{9,15},{10,... | collective-permute-start | bytes 786440 | tf_op jit(solution)/shard_map/ppermute | solution.py:39
  12.8 1.3 %collective-permute-start.5 = (bf16[1,32,2048]{2,1,0:T(8,128)(2,1)S(1)}, bf16[1,32,2048]{2,1,0:T(8,128)(2,1)S(1)}, u32[]{:S(2)}, u32[]{:S(2)}) collective-permute-start(bf16[1,32,2048]{2,1,0:T(8,128)(2,1)S(1)} %get-tuple-element.50), channel_id=1, source_target_pairs={{0,1},{1,0},{2,3},{3,2},{4,5},{5,4},{6,7},{7,6},{8,9},{9,8},{10,11... | collective-permute-start | bytes 393224 | tf_op jit(solution)/shard_map/ppermute | solution.py:39
  14.1 1.9 %collective-permute-start.6 = (bf16[1,32,2048]{2,1,0:T(8,128)(2,1)S(1)}, bf16[1,32,2048]{2,1,0:T(8,128)(2,1)S(1)}, u32[]{:S(2)}, u32[]{:S(2)}) collective-permute-start(bf16[1,32,2048]{2,1,0:T(8,128)(2,1)S(1)} %get-tuple-element.50), channel_id=1, source_target_pairs={{0,65},{1,64},{2,67},{3,66},{4,69},{5,68},{6,71},{7,70},{8,73},{9,... | collective-permute-start | bytes 393224 | tf_op jit(solution)/shard_map/ppermute | solution.py:46
  16.9 1.2 %collective-permute-start.7 = (bf16[2,32,2048]{2,1,0:T(8,128)(2,1)S(1)}, bf16[2,32,2048]{2,1,0:T(8,128)(2,1)S(1)}, u32[]{:S(2)}, u32[]{:S(2)}) collective-permute-start(bf16[2,32,2048]{2,1,0:T(8,128)(2,1)S(1)} %get-tuple-element.54), channel_id=1, source_target_pairs={{0,4},{1,5},{2,6},{3,7},{4,0},{5,1},{6,2},{7,3},{8,12},{9,13},{10,... | collective-permute-start | bytes 786440 | tf_op jit(solution)/shard_map/ppermute | solution.py:39
  18.1 1.3 %collective-permute-done.6 = bf16[1,32,2048]{2,1,0:T(8,128)(2,1)S(1)} collective-permute-done((bf16[1,32,2048]{2,1,0:T(8,128)(2,1)S(1)}, bf16[1,32,2048]{2,1,0:T(8,128)(2,1)S(1)}, u32[]{:S(2)}, u32[]{:S(2)}) %collective-permute-start.6) | collective-permute-done | bytes 131104 | tf_op jit(solution)/shard_map/ppermute | solution.py:46
  19.7 1.4 %collective-permute-start.14 = (bf16[1,64,2048]{2,1,0:T(8,128)(2,1)S(1)}, bf16[1,64,2048]{2,1,0:T(8,128)(2,1)S(1)}, u32[]{:S(2)}, u32[]{:S(2)}) collective-permute-start(bf16[1,64,2048]{2,1,0:T(8,128)(2,1)S(1)} %get-tuple-element.56), channel_id=1, source_target_pairs={{0,1},{1,0},{2,3},{3,2},{4,5},{5,4},{6,7},{7,6},{8,9},{9,8},{10,11... | collective-permute-start | bytes 786440 | tf_op jit(solution)/shard_map/ppermute | solution.py:39
  21.1 1.9 %collective-permute-start.15 = (bf16[1,64,2048]{2,1,0:T(8,128)(2,1)S(1)}, bf16[1,64,2048]{2,1,0:T(8,128)(2,1)S(1)}, u32[]{:S(2)}, u32[]{:S(2)}) collective-permute-start(bf16[1,64,2048]{2,1,0:T(8,128)(2,1)S(1)} %get-tuple-element.56), channel_id=1, source_target_pairs={{0,65},{1,64},{2,67},{3,66},{4,69},{5,68},{6,71},{7,70},{8,73},{9,... | collective-permute-start | bytes 786440 | tf_op jit(solution)/shard_map/ppermute | solution.py:46
  23.2 1.2 %collective-permute-done.7 = bf16[2,32,2048]{2,1,0:T(8,128)(2,1)S(1)} collective-permute-done((bf16[2,32,2048]{2,1,0:T(8,128)(2,1)S(1)}, bf16[2,32,2048]{2,1,0:T(8,128)(2,1)S(1)}, u32[]{:S(2)}, u32[]{:S(2)}) %collective-permute-start.7) | collective-permute-done | bytes 262176 | tf_op jit(solution)/shard_map/ppermute | solution.py:39
  26.0 3.8 %collective-permute-done.4 = bf16[1,64,2048]{2,1,0:T(8,128)(2,1)S(1)} collective-permute-done((bf16[1,64,2048]{2,1,0:T(8,128)(2,1)S(1)}, bf16[1,64,2048]{2,1,0:T(8,128)(2,1)S(1)}, u32[]{:S(2)}, u32[]{:S(2)}) %collective-permute-start.4) | collective-permute-done | bytes 262176 | tf_op jit(solution)/shard_map/ppermute | solution.py:39
  30.7 0.9 collective-permute-start.18
  31.6 2.4 %collective-permute-done.11 = bf16[1,32,2048]{2,1,0:T(8,128)(2,1)S(1)} collective-permute-done((bf16[1,32,2048]{2,1,0:T(8,128)(2,1)S(1)}, bf16[1,32,2048]{2,1,0:T(8,128)(2,1)S(1)}, u32[]{:S(2)}, u32[]{:S(2)}) %collective-permute-start.11) | collective-permute-done | bytes 131104 | tf_op jit(solution)/shard_map/ppermute | solution.py:39
  35.4 1.7 %collective-permute-start.23 = (bf16[4,32,2048]{2,1,0:T(8,128)(2,1)S(1)}, bf16[4,32,2048]{2,1,0:T(8,128)(2,1)S(1)}, u32[]{:S(2)}, u32[]{:S(2)}) collective-permute-start(bf16[4,32,2048]{2,1,0:T(8,128)(2,1)S(1)} %pad_maximum_fusion.4.refs_0_), channel_id=1, source_target_pairs={{0,64},{8,72},{16,80},{24,88},{32,96},{40,104},{48,112},{56,120},{... | collective-permute-start | bytes 1572872 | tf_op jit(solution)/shard_map/ppermute | solution.py:39
  37.2 4.1 %collective-permute-done.19 = bf16[2,32,2048]{2,1,0:T(8,128)(2,1)S(1)} collective-permute-done((bf16[2,32,2048]{2,1,0:T(8,128)(2,1)S(1)}, bf16[2,32,2048]{2,1,0:T(8,128)(2,1)S(1)}, u32[]{:S(2)}, u32[]{:S(2)}) %collective-permute-start.19) | collective-permute-done | bytes 262176 | tf_op jit(solution)/shard_map/ppermute | solution.py:39
  42.0 3.3 %collective-permute-start.16 = (bf16[4,64,2048]{2,1,0:T(8,128)(2,1)S(1)}, bf16[4,64,2048]{2,1,0:T(8,128)(2,1)S(1)}, u32[]{:S(2)}, u32[]{:S(2)}) collective-permute-start(bf16[4,64,2048]{2,1,0:T(8,128)(2,1)S(1)} %pad_maximum_fusion.refs_0_), channel_id=1, source_target_pairs={{0,64},{8,72},{16,80},{24,88},{32,96},{40,104},{48,112},{56,120},{... | collective-permute-start | bytes 3145736 | tf_op jit(solution)/shard_map/ppermute | solution.py:39
  46.2 2.2 %collective-permute-done.23.refs_1_ = bf16[4,32,2048]{2,1,0:T(8,128)(2,1)S(1)} collective-permute-done((bf16[4,32,2048]{2,1,0:T(8,128)(2,1)S(1)}, bf16[4,32,2048]{2,1,0:T(8,128)(2,1)S(1)}, u32[]{:S(2)}, u32[]{:S(2)}) %collective-permute-start.23) | collective-permute-done | bytes 524320 | tf_op jit(solution)/shard_map/ppermute | solution.py:39
  49.3 1.1 %rotate1_store0.3 = (bf16[32,16512]{1,0:T(8,128)(2,1)S(1)}, f32[32,128]{1,0:T(8,128)S(1)}) custom-call(s32[3]{0:T(128)S(1)} %pad_add_fusion.where_ref, bf16[4,32,2048]{2,1,0:T(8,128)(2,1)S(1)} %pad_maximum_fusion.4.refs_0_, bf16[4,32,2048]{2,1,0:T(8,128)(2,1)S(1)} %collective-permute-done.23.refs_1_), custom_call_target="tpu_custom_call" | custom-call | flops 20000000000 | bytes 1 | tf_op jit(solution)/shard_map/rotate1_store0/pallas_call | solution.py:247
  50.4 2.5 %collective-permute-done.22.refs_1_ = bf16[4,32,2048]{2,1,0:T(8,128)(2,1)S(1)} collective-permute-done((bf16[4,32,2048]{2,1,0:T(8,128)(2,1)S(1)}, bf16[4,32,2048]{2,1,0:T(8,128)(2,1)S(1)}, u32[]{:S(2)}, u32[]{:S(2)}) %collective-permute-start.22) | collective-permute-done | bytes 524320 | tf_op jit(solution)/shard_map/ppermute | solution.py:39
  53.0 23.8 %collective-permute-start.24 = (bf16[32,16512]{1,0:T(8,128)(2,1)S(1)}, bf16[32,16512]{1,0:T(8,128)(2,1)S(1)}, u32[]{:S(2)}, u32[]{:S(2)}) collective-permute-start(bf16[32,16512]{1,0:T(8,128)(2,1)S(1)} %get-tuple-element.71.refs_2_), channel_id=1, source_target_pairs={{0,8},{8,0},{16,24},{24,16},{32,40},{40,32},{48,56},{56,48},{64,72... | collective-permute-start | bytes 3170312 | tf_op jit(solution)/shard_map/ppermute | solution.py:39
  76.7 1.1 %rotate1_store0.4 = (bf16[32,16512]{1,0:T(8,128)(2,1)S(1)}, f32[32,128]{1,0:T(8,128)S(1)}) custom-call(s32[3]{0:T(128)S(1)} %pad_add_fusion.where_ref, bf16[4,32,2048]{2,1,0:T(8,128)(2,1)S(1)} %pad_maximum_fusion.3.refs_0_, bf16[4,32,2048]{2,1,0:T(8,128)(2,1)S(1)} %collective-permute-done.22.refs_1_), custom_call_target="tpu_custom_call" | custom-call | flops 20000000000 | bytes 1 | tf_op jit(solution)/shard_map/rotate1_store0/pallas_call | solution.py:247
  77.9 1.2 %rotate1_store0.5 = (bf16[32,16512]{1,0:T(8,128)(2,1)S(1)}, f32[32,128]{1,0:T(8,128)S(1)}) custom-call(s32[3]{0:T(128)S(1)} %pad_add_fusion.where_ref, bf16[4,32,2048]{2,1,0:T(8,128)(2,1)S(1)} %pad_maximum_fusion.7.refs_0_, bf16[4,32,2048]{2,1,0:T(8,128)(2,1)S(1)} %collective-permute-done.21.refs_1_), custom_call_target="tpu_custom_call" | custom-call | flops 20000000000 | bytes 1 | tf_op jit(solution)/shard_map/rotate1_store0/pallas_call | solution.py:247
  79.0 3.1 %collective-permute-start.27 = (bf16[32,16512]{1,0:T(8,128)(2,1)S(1)}, bf16[32,16512]{1,0:T(8,128)(2,1)S(1)}, u32[]{:S(2)}, u32[]{:S(2)}) collective-permute-start(bf16[32,16512]{1,0:T(8,128)(2,1)S(1)} %get-tuple-element.75.refs_2_), channel_id=1, source_target_pairs={{0,8},{8,0},{16,24},{24,16},{32,40},{40,32},{48,56},{56,48},{64,72... | collective-permute-start | bytes 3170312 | tf_op jit(solution)/shard_map/ppermute | solution.py:39
  82.1 1.9 %rotate1_store1.1 = (bf16[32,16512]{1,0:T(8,128)(2,1)S(1)}, f32[32,128]{1,0:T(8,128)S(1)}, bf16[512,16384]{1,0:T(8,128)(2,1)}, f32[32,128]{1,0:T(8,128)S(1)}) custom-call(s32[3]{0:T(128)S(1)} %pad_add_fusion.where_ref, bf16[4,32,2048]{2,1,0:T(8,128)(2,1)S(1)} %pad_maximum_fusion.6.refs_0_, bf16[4,32,2048]{2,1,0:T(8,128)(2,1)S(1)} %collective-permute-done.20.refs_1_, ...), custom_call_target="tpu_custom_call" | custom-call | flops 20000000000 | bytes 1 | tf_op jit(solution)/shard_map/rotate1_store1/pallas_call | solution.py:247
  84.0 4.5 %collective-permute-start.28 = (bf16[32,16512]{1,0:T(8,128)(2,1)S(1)}, bf16[32,16512]{1,0:T(8,128)(2,1)S(1)}, u32[]{:S(2)}, u32[]{:S(2)}) collective-permute-start(bf16[32,16512]{1,0:T(8,128)(2,1)S(1)} %get-tuple-element.77.refs_4_), channel_id=1, source_target_pairs={{0,8},{8,0},{16,24},{24,16},{32,40},{40,32},{48,56},{56,48},{64,72... | collective-permute-start | bytes 3170312 | tf_op jit(solution)/shard_map/ppermute | solution.py:39
  88.5 1.8 %rotate2_store0.1 = (bf16[64,16512]{1,0:T(8,128)(2,1)S(1)}, f32[64,128]{1,0:T(8,128)S(1)}) custom-call(s32[3]{0:T(128)S(1)} %pad_add_fusion.where_ref, bf16[4,64,2048]{2,1,0:T(8,128)(2,1)S(1)} %pad_maximum_fusion.refs_0_, bf16[4,64,2048]{2,1,0:T(8,128)(2,1)S(1)} %collective-permute-done.16.refs_1_), custom_call_target="tpu_custom_call" | custom-call | flops 20000000000 | bytes 1 | tf_op jit(solution)/shard_map/rotate2_store0/pallas_call | solution.py:247
  90.8 2.6 %rotate2_store2.1 = (bf16[64,16512]{1,0:T(8,128)(2,1)S(1)}, f32[64,128]{1,0:T(8,128)S(1)}, bf16[512,16384]{1,0:T(8,128)(2,1)}, f32[32,128]{1,0:T(8,128)S(1)}, f32[32,128]{1,0:T(8,128)S(1)}) custom-call(s32[3]{0:T(128)S(1)} %pad_add_fusion.where_ref, bf16[4,64,2048]{2,1,0:T(8,128)(2,1)S(1)} %pad_maximum_fusion.1.refs_0_, ...), custom_call_target="tpu_custom_call", output_to_operand_aliasing={{2}: (7, {})} | custom-call | flops 20000000000 | bytes 1 | tf_op jit(solution)/shard_map/rotate2_store2/pallas_call | solution.py:247
  93.9 5.2 %collective-permute-done.30.refs_5_ = bf16[32,16512]{1,0:T(8,128)(2,1)S(1)} collective-permute-done((bf16[32,16512]{1,0:T(8,128)(2,1)S(1)}, bf16[32,16512]{1,0:T(8,128)(2,1)S(1)}, u32[]{:S(2)}, u32[]{:S(2)}) %collective-permute-start.30) | collective-permute-done | bytes 1056800 | tf_op jit(solution)/shard_map/ppermute | solution.py:39
  99.1 5.2 %rotate0_store5.1 = (bf16[512,16384]{1,0:T(8,128)(2,1)}, f32[4,128]{1,0:T(4,128)}) custom-call(s32[3]{0:T(128)S(1)} %pad_add_fusion.where_ref, bf16[64,16512]{1,0:T(8,128)(2,1)S(1)} %get-tuple-element.79.refs_0_, bf16[64,16512]{1,0:T(8,128)(2,1)S(1)} %collective-permute-done.25.refs_1_, ...), custom_call_target="tpu_custom_call", output_to_operand_aliasing={{0}: (16, {})} | custom-call | flops 20000000000 | bytes 1 | tf_op jit(solution)/shard_map/rotate0_store5/pallas_call | solution.py:247
  (58 shorter events, 9.1 us)
Async XLA Ops:
  2.0 3.0 %collective-permute-start = (bf16[8,32,1024]{2,1,0:T(8,128)(2,1)S(1)}, bf16[8,32,1024]{2,1,0:T(8,128)(2,1)S(1)}, u32[]{:S(2)}, u32[]{:S(2)}) collective-permute-start(bf16[8,32,1024]{2,1,0:T(8,128)(2,1)S(1)} %get-tuple-element.101), channel_id=1, source_target_pairs={{0,8},{8,0},{16,24},{24,16},{32,40},{40,32},{48,56},{56,48},{64,72... | collective-permute-start | bytes 1572872 | tf_op jit(solution)/shard_map/ppermute | solution.py:39
  6.4 9.6 %collective-permute-start.3 = (bf16[1,32,2048]{2,1,0:T(8,128)(2,1)S(1)}, bf16[1,32,2048]{2,1,0:T(8,128)(2,1)S(1)}, u32[]{:S(2)}, u32[]{:S(2)}) collective-permute-start(bf16[1,32,2048]{2,1,0:T(8,128)(2,1)S(1)} %get-tuple-element.52), channel_id=1, source_target_pairs={{0,48},{8,56},{16,32},{24,40},{32,16},{40,24},{48,0},{56,8},{64,11... | collective-permute-start | bytes 393224 | tf_op jit(solution)/shard_map/ppermute | solution.py:39
  9.0 10.4 %collective-permute-start.2 = (bf16[2,32,2048]{2,1,0:T(8,128)(2,1)S(1)}, bf16[2,32,2048]{2,1,0:T(8,128)(2,1)S(1)}, u32[]{:S(2)}, u32[]{:S(2)}) collective-permute-start(bf16[2,32,2048]{2,1,0:T(8,128)(2,1)S(1)} %get-tuple-element.51), channel_id=1, source_target_pairs={{0,6},{1,7},{2,4},{3,5},{4,2},{5,3},{6,0},{7,1},{8,14},{9,15},{10,... | collective-permute-start | bytes 786440 | tf_op jit(solution)/shard_map/ppermute | solution.py:39
  12.8 6.9 %collective-permute-start.1 = (bf16[2,32,2048]{2,1,0:T(8,128)(2,1)S(1)}, bf16[2,32,2048]{2,1,0:T(8,128)(2,1)S(1)}, u32[]{:S(2)}, u32[]{:S(2)}) collective-permute-start(bf16[2,32,2048]{2,1,0:T(8,128)(2,1)S(1)} %get-tuple-element.49), channel_id=1, source_target_pairs={{0,2},{1,3},{2,0},{3,1},{4,6},{5,7},{6,4},{7,5},{8,10},{9,11},{10,... | collective-permute-start | bytes 786440 | tf_op jit(solution)/shard_map/ppermute | solution.py:39
  12.8 4.1 %collective-permute-start.5 = (bf16[1,32,2048]{2,1,0:T(8,128)(2,1)S(1)}, bf16[1,32,2048]{2,1,0:T(8,128)(2,1)S(1)}, u32[]{:S(2)}, u32[]{:S(2)}) collective-permute-start(bf16[1,32,2048]{2,1,0:T(8,128)(2,1)S(1)} %get-tuple-element.50), channel_id=1, source_target_pairs={{0,1},{1,0},{2,3},{3,2},{4,5},{5,4},{6,7},{7,6},{8,9},{9,8},{10,11... | collective-permute-start | bytes 393224 | tf_op jit(solution)/shard_map/ppermute | solution.py:39
  14.1 5.3 %collective-permute-start.6 = (bf16[1,32,2048]{2,1,0:T(8,128)(2,1)S(1)}, bf16[1,32,2048]{2,1,0:T(8,128)(2,1)S(1)}, u32[]{:S(2)}, u32[]{:S(2)}) collective-permute-start(bf16[1,32,2048]{2,1,0:T(8,128)(2,1)S(1)} %get-tuple-element.50), channel_id=1, source_target_pairs={{0,65},{1,64},{2,67},{3,66},{4,69},{5,68},{6,71},{7,70},{8,73},{9,... | collective-permute-start | bytes 393224 | tf_op jit(solution)/shard_map/ppermute | solution.py:46
  16.0 9.2 %collective-permute-start.10 = (bf16[2,32,2048]{2,1,0:T(8,128)(2,1)S(1)}, bf16[2,32,2048]{2,1,0:T(8,128)(2,1)S(1)}, u32[]{:S(2)}, u32[]{:S(2)}) collective-permute-start(bf16[2,32,2048]{2,1,0:T(8,128)(2,1)S(1)} %pad_maximum_fusion.8), channel_id=1, source_target_pairs={{0,16},{8,24},{16,0},{24,8},{32,48},{40,56},{48,32},{56,40},{64,80... | collective-permute-start | bytes 786440 | tf_op jit(solution)/shard_map/ppermute | solution.py:39
  16.9 7.5 %collective-permute-start.7 = (bf16[2,32,2048]{2,1,0:T(8,128)(2,1)S(1)}, bf16[2,32,2048]{2,1,0:T(8,128)(2,1)S(1)}, u32[]{:S(2)}, u32[]{:S(2)}) collective-permute-start(bf16[2,32,2048]{2,1,0:T(8,128)(2,1)S(1)} %get-tuple-element.54), channel_id=1, source_target_pairs={{0,4},{1,5},{2,6},{3,7},{4,0},{5,1},{6,2},{7,3},{8,12},{9,13},{10,... | collective-permute-start | bytes 786440 | tf_op jit(solution)/shard_map/ppermute | solution.py:39
  19.7 10.3 %collective-permute-start.14 = (bf16[1,64,2048]{2,1,0:T(8,128)(2,1)S(1)}, bf16[1,64,2048]{2,1,0:T(8,128)(2,1)S(1)}, u32[]{:S(2)}, u32[]{:S(2)}) collective-permute-start(bf16[1,64,2048]{2,1,0:T(8,128)(2,1)S(1)} %get-tuple-element.56), channel_id=1, source_target_pairs={{0,1},{1,0},{2,3},{3,2},{4,5},{5,4},{6,7},{7,6},{8,9},{9,8},{10,11... | collective-permute-start | bytes 786440 | tf_op jit(solution)/shard_map/ppermute | solution.py:39
  21.1 9.5 %collective-permute-start.15 = (bf16[1,64,2048]{2,1,0:T(8,128)(2,1)S(1)}, bf16[1,64,2048]{2,1,0:T(8,128)(2,1)S(1)}, u32[]{:S(2)}, u32[]{:S(2)}) collective-permute-start(bf16[1,64,2048]{2,1,0:T(8,128)(2,1)S(1)} %get-tuple-element.56), channel_id=1, source_target_pairs={{0,65},{1,64},{2,67},{3,66},{4,69},{5,68},{6,71},{7,70},{8,73},{9,... | collective-permute-start | bytes 786440 | tf_op jit(solution)/shard_map/ppermute | solution.py:46
  23.0 6.7 %collective-permute-start.4 = (bf16[1,64,2048]{2,1,0:T(8,128)(2,1)S(1)}, bf16[1,64,2048]{2,1,0:T(8,128)(2,1)S(1)}, u32[]{:S(2)}, u32[]{:S(2)}) collective-permute-start(bf16[1,64,2048]{2,1,0:T(8,128)(2,1)S(1)} %get-tuple-element.55), channel_id=1, source_target_pairs={{0,48},{8,56},{16,32},{24,40},{32,16},{40,24},{48,0},{56,8},{64,11... | collective-permute-start | bytes 786440 | tf_op jit(solution)/shard_map/ppermute | solution.py:39
  24.4 6.2 %collective-permute-start.13 = (bf16[1,32,2048]{2,1,0:T(8,128)(2,1)S(1)}, bf16[1,32,2048]{2,1,0:T(8,128)(2,1)S(1)}, u32[]{:S(2)}, u32[]{:S(2)}) collective-permute-start(bf16[1,32,2048]{2,1,0:T(8,128)(2,1)S(1)} %get-tuple-element.57), channel_id=1, source_target_pairs={{0,16},{8,24},{16,0},{24,8},{32,48},{40,56},{48,32},{56,40},{64,80... | collective-permute-start | bytes 393224 | tf_op jit(solution)/shard_map/ppermute | solution.py:39
  25.2 10.2 %collective-permute-start.9 = (bf16[2,32,2048]{2,1,0:T(8,128)(2,1)S(1)}, bf16[2,32,2048]{2,1,0:T(8,128)(2,1)S(1)}, u32[]{:S(2)}, u32[]{:S(2)}) collective-permute-start(bf16[2,32,2048]{2,1,0:T(8,128)(2,1)S(1)} %pad_maximum_fusion.9), channel_id=1, source_target_pairs={{0,48},{8,56},{16,32},{24,40},{32,16},{40,24},{48,0},{56,8},{64,11... | collective-permute-start | bytes 786440 | tf_op jit(solution)/shard_map/ppermute | solution.py:39
  29.8 4.2 %collective-permute-start.11 = (bf16[1,32,2048]{2,1,0:T(8,128)(2,1)S(1)}, bf16[1,32,2048]{2,1,0:T(8,128)(2,1)S(1)}, u32[]{:S(2)}, u32[]{:S(2)}) collective-permute-start(bf16[1,32,2048]{2,1,0:T(8,128)(2,1)S(1)} %get-tuple-element.60), channel_id=1, source_target_pairs={{0,1},{1,0},{2,3},{3,2},{4,5},{5,4},{6,7},{7,6},{8,9},{9,8},{10,11... | collective-permute-start | bytes 393224 | tf_op jit(solution)/shard_map/ppermute | solution.py:39
  30.0 5.3 %collective-permute-start.12 = (bf16[1,32,2048]{2,1,0:T(8,128)(2,1)S(1)}, bf16[1,32,2048]{2,1,0:T(8,128)(2,1)S(1)}, u32[]{:S(2)}, u32[]{:S(2)}) collective-permute-start(bf16[1,32,2048]{2,1,0:T(8,128)(2,1)S(1)} %get-tuple-element.60), channel_id=1, source_target_pairs={{0,65},{1,64},{2,67},{3,66},{4,69},{5,68},{6,71},{7,70},{8,73},{9,... | collective-permute-start | bytes 393224 | tf_op jit(solution)/shard_map/ppermute | solution.py:46
  30.6 11.2 %collective-permute-start.8 = (bf16[2,64,2048]{2,1,0:T(8,128)(2,1)S(1)}, bf16[2,64,2048]{2,1,0:T(8,128)(2,1)S(1)}, u32[]{:S(2)}, u32[]{:S(2)}) collective-permute-start(bf16[2,64,2048]{2,1,0:T(8,128)(2,1)S(1)} %pad_maximum_fusion.2), channel_id=1, source_target_pairs={{0,16},{8,24},{16,0},{24,8},{32,48},{40,56},{48,32},{56,40},{64,80... | collective-permute-start | bytes 1572872 | tf_op jit(solution)/shard_map/ppermute | solution.py:39
  30.7 15.4 %collective-permute-start.18 = (bf16[2,64,2048]{2,1,0:T(8,128)(2,1)S(1)}, bf16[2,64,2048]{2,1,0:T(8,128)(2,1)S(1)}, u32[]{:S(2)}, u32[]{:S(2)}) collective-permute-start(bf16[2,64,2048]{2,1,0:T(8,128)(2,1)S(1)} %pad_maximum_fusion.5), channel_id=1, source_target_pairs={{0,48},{8,56},{16,32},{24,40},{32,16},{40,24},{48,0},{56,8},{64,11... | collective-permute-start | bytes 1572872 | tf_op jit(solution)/shard_map/ppermute | solution.py:39
  34.0 7.3 %collective-permute-start.19 = (bf16[2,32,2048]{2,1,0:T(8,128)(2,1)S(1)}, bf16[2,32,2048]{2,1,0:T(8,128)(2,1)S(1)}, u32[]{:S(2)}, u32[]{:S(2)}) collective-permute-start(bf16[2,32,2048]{2,1,0:T(8,128)(2,1)S(1)} %pad_maximum_fusion.11), channel_id=1, source_target_pairs={{0,64},{8,72},{16,80},{24,88},{32,96},{40,104},{48,112},{56,120},{... | collective-permute-start | bytes 786440 | tf_op jit(solution)/shard_map/ppermute | solution.py:39
  35.3 6.4 %collective-permute-start.17 = (bf16[2,32,2048]{2,1,0:T(8,128)(2,1)S(1)}, bf16[2,32,2048]{2,1,0:T(8,128)(2,1)S(1)}, u32[]{:S(2)}, u32[]{:S(2)}) collective-permute-start(bf16[2,32,2048]{2,1,0:T(8,128)(2,1)S(1)} %pad_maximum_fusion.10), channel_id=1, source_target_pairs={{0,16},{8,24},{16,0},{24,8},{32,48},{40,56},{48,32},{56,40},{64,80... | collective-permute-start | bytes 786440 | tf_op jit(solution)/shard_map/ppermute | solution.py:39
  35.4 13.0 %collective-permute-start.23 = (bf16[4,32,2048]{2,1,0:T(8,128)(2,1)S(1)}, bf16[4,32,2048]{2,1,0:T(8,128)(2,1)S(1)}, u32[]{:S(2)}, u32[]{:S(2)}) collective-permute-start(bf16[4,32,2048]{2,1,0:T(8,128)(2,1)S(1)} %pad_maximum_fusion.4.refs_0_), channel_id=1, source_target_pairs={{0,64},{8,72},{16,80},{24,88},{32,96},{40,104},{48,112},{56,120},{... | collective-permute-start | bytes 1572872 | tf_op jit(solution)/shard_map/ppermute | solution.py:39
  41.3 11.7 %collective-permute-start.22 = (bf16[4,32,2048]{2,1,0:T(8,128)(2,1)S(1)}, bf16[4,32,2048]{2,1,0:T(8,128)(2,1)S(1)}, u32[]{:S(2)}, u32[]{:S(2)}) collective-permute-start(bf16[4,32,2048]{2,1,0:T(8,128)(2,1)S(1)} %pad_maximum_fusion.3.refs_0_), channel_id=1, source_target_pairs={{0,16},{8,24},{16,0},{24,8},{32,48},{40,56},{48,32},{56,40},{64,80... | collective-permute-start | bytes 1572872 | tf_op jit(solution)/shard_map/ppermute | solution.py:39
  42.0 46.5 %collective-permute-start.16 = (bf16[4,64,2048]{2,1,0:T(8,128)(2,1)S(1)}, bf16[4,64,2048]{2,1,0:T(8,128)(2,1)S(1)}, u32[]{:S(2)}, u32[]{:S(2)}) collective-permute-start(bf16[4,64,2048]{2,1,0:T(8,128)(2,1)S(1)} %pad_maximum_fusion.refs_0_), channel_id=1, source_target_pairs={{0,64},{8,72},{16,80},{24,88},{32,96},{40,104},{48,112},{56,120},{... | collective-permute-start | bytes 3145736 | tf_op jit(solution)/shard_map/ppermute | solution.py:39
  45.2 32.7 %collective-permute-start.21 = (bf16[4,32,2048]{2,1,0:T(8,128)(2,1)S(1)}, bf16[4,32,2048]{2,1,0:T(8,128)(2,1)S(1)}, u32[]{:S(2)}, u32[]{:S(2)}) collective-permute-start(bf16[4,32,2048]{2,1,0:T(8,128)(2,1)S(1)} %pad_maximum_fusion.7.refs_0_), channel_id=1, source_target_pairs={{0,48},{8,56},{16,32},{24,40},{32,16},{40,24},{48,0},{56,8},{64,11... | collective-permute-start | bytes 1572872 | tf_op jit(solution)/shard_map/ppermute | solution.py:39
  46.1 44.2 %collective-permute-start.26 = (bf16[4,64,2048]{2,1,0:T(8,128)(2,1)S(1)}, bf16[4,64,2048]{2,1,0:T(8,128)(2,1)S(1)}, u32[]{:S(2)}, u32[]{:S(2)}) collective-permute-start(bf16[4,64,2048]{2,1,0:T(8,128)(2,1)S(1)} %pad_maximum_fusion.1.refs_0_), channel_id=1, source_target_pairs={{0,16},{8,24},{16,0},{24,8},{32,48},{40,56},{48,32},{56,40},{64,80... | collective-permute-start | bytes 3145736 | tf_op jit(solution)/shard_map/ppermute | solution.py:39
  48.5 33.6 %collective-permute-start.20 = (bf16[4,32,2048]{2,1,0:T(8,128)(2,1)S(1)}, bf16[4,32,2048]{2,1,0:T(8,128)(2,1)S(1)}, u32[]{:S(2)}, u32[]{:S(2)}) collective-permute-start(bf16[4,32,2048]{2,1,0:T(8,128)(2,1)S(1)} %pad_maximum_fusion.6.refs_0_), channel_id=1, source_target_pairs={{0,48},{8,56},{16,32},{24,40},{32,16},{40,24},{48,0},{56,8},{64,11... | collective-permute-start | bytes 1572872 | tf_op jit(solution)/shard_map/ppermute | solution.py:39
  53.0 29.1 %collective-permute-start.24 = (bf16[32,16512]{1,0:T(8,128)(2,1)S(1)}, bf16[32,16512]{1,0:T(8,128)(2,1)S(1)}, u32[]{:S(2)}, u32[]{:S(2)}) collective-permute-start(bf16[32,16512]{1,0:T(8,128)(2,1)S(1)} %get-tuple-element.71.refs_2_), channel_id=1, source_target_pairs={{0,8},{8,0},{16,24},{24,16},{32,40},{40,32},{48,56},{56,48},{64,72... | collective-permute-start | bytes 3170312 | tf_op jit(solution)/shard_map/ppermute | solution.py:39
  79.0 11.3 %collective-permute-start.27 = (bf16[32,16512]{1,0:T(8,128)(2,1)S(1)}, bf16[32,16512]{1,0:T(8,128)(2,1)S(1)}, u32[]{:S(2)}, u32[]{:S(2)}) collective-permute-start(bf16[32,16512]{1,0:T(8,128)(2,1)S(1)} %get-tuple-element.75.refs_2_), channel_id=1, source_target_pairs={{0,8},{8,0},{16,24},{24,16},{32,40},{40,32},{48,56},{56,48},{64,72... | collective-permute-start | bytes 3170312 | tf_op jit(solution)/shard_map/ppermute | solution.py:39
  84.0 6.8 %collective-permute-start.28 = (bf16[32,16512]{1,0:T(8,128)(2,1)S(1)}, bf16[32,16512]{1,0:T(8,128)(2,1)S(1)}, u32[]{:S(2)}, u32[]{:S(2)}) collective-permute-start(bf16[32,16512]{1,0:T(8,128)(2,1)S(1)} %get-tuple-element.77.refs_4_), channel_id=1, source_target_pairs={{0,8},{8,0},{16,24},{24,16},{32,40},{40,32},{48,56},{56,48},{64,72... | collective-permute-start | bytes 3170312 | tf_op jit(solution)/shard_map/ppermute | solution.py:39
  90.2 8.9 %collective-permute-start.25 = (bf16[64,16512]{1,0:T(8,128)(2,1)S(1)}, bf16[64,16512]{1,0:T(8,128)(2,1)S(1)}, u32[]{:S(2)}, u32[]{:S(2)}) collective-permute-start(bf16[64,16512]{1,0:T(8,128)(2,1)S(1)} %get-tuple-element.79.refs_0_), channel_id=1, source_target_pairs={{0,8},{8,0},{16,24},{24,16},{32,40},{40,32},{48,56},{56,48},{64,72... | collective-permute-start | bytes 6340616 | tf_op jit(solution)/shard_map/ppermute | solution.py:39
  93.4 5.8 %collective-permute-start.29 = (bf16[64,16512]{1,0:T(8,128)(2,1)S(1)}, bf16[64,16512]{1,0:T(8,128)(2,1)S(1)}, u32[]{:S(2)}, u32[]{:S(2)}) collective-permute-start(bf16[64,16512]{1,0:T(8,128)(2,1)S(1)} %get-tuple-element.82.refs_2_), channel_id=1, source_target_pairs={{0,8},{8,0},{16,24},{24,16},{32,40},{40,32},{48,56},{56,48},{64,72... | collective-permute-start | bytes 6340616 | tf_op jit(solution)/shard_map/ppermute | solution.py:39
  93.8 5.3 %collective-permute-start.30 = (bf16[32,16512]{1,0:T(8,128)(2,1)S(1)}, bf16[32,16512]{1,0:T(8,128)(2,1)S(1)}, u32[]{:S(2)}, u32[]{:S(2)}) collective-permute-start(bf16[32,16512]{1,0:T(8,128)(2,1)S(1)} %get-tuple-element.73.refs_4_), channel_id=1, source_target_pairs={{0,8},{8,0},{16,24},{24,16},{32,40},{40,32},{48,56},{56,48},{64,72... | collective-permute-start | bytes 3170312 | tf_op jit(solution)/shard_map/ppermute | solution.py:39

commit v3 on v2

--- a/solution.py
+++ b/solution.py
@@ -20,7 +20,7 @@
 
 
 CHUNKS = (
-    ((0,), "bay"),
+    ((0,), "aby"),
     ((2, 6), "bay"),
     ((1,), "yba"),
     ((4,), "ayb"),
@@ -29,8 +29,9 @@
 )
 
 PLAN = (
-    "z2", "m2", "z6", "g0", "g0", "z4", "g1", "m4", "g3", "g2", "g1", "m5", "g4", "g3", "g5",
-    "g0", "g2", "g1", "g3", "g4", "g5", "k0", "k2", "k3", "k5r0", "k1", "k4r35", "r142",
+    "z2", "m2", "z6", "z4", "g1", "g0", "g1", "g0", "m4", "g3", "m5", "g2", "g3", "g5", "g4",
+    "g0", "g2", "g3", "g4", "g1", "g5", "k0", "k2o0", "k5o2", "k3o5", "k4o3r20", "k1o4r35",
+    "o1r4", "r1",
 )
 
 
@@ -164,39 +165,39 @@
         return taken
 
     inputs = take(2 if order else 0)
-    pairs = [take(2) for _ in stored]
+    code_refs = take(len(stored))
     scales = take(len(earlier))
     take(1 if chained else 0)
     outputs = take(2 if order else 0)
-    copies = []
+    copies, got_scales = [], []
     if stored:
         (out_ref,) = take(1)
         wide = out_ref.shape[1]
-        got_scale_refs = take(1 if earlier else len(stored))
         sems = refs[-1]
-        for pieces, pair in zip(stored, pairs):
-            for side, ref in enumerate(pair):
-                for rows, place in places(where_ref, pieces, half, side):
-                    copies.append(
-                        pltpu.make_async_copy(
-                            ref.at[rows, pl.ds(0, wide)], out_ref.at[place], sems.at[len(copies)]
-                        )
+        for (pieces, side), ref in zip(stored, code_refs):
+            for rows, place in places(where_ref, pieces, half, side):
+                copies.append(
+                    pltpu.make_async_copy(
+                        ref.at[rows, pl.ds(0, wide)], out_ref.at[place], sems.at[len(copies)]
                     )
-    for copy in copies:
-        copy.start()
-    got_scales = []
-    for _, got_ref in pairs:
-        terms = got_ref[:, wide:].astype(jnp.float32)
-        scale = (terms[:, :1] + terms[:, 1:2]) + terms[:, 2:3]
-        got_scales.append(jnp.broadcast_to(scale, (scale.shape[0], EXTRA)))
+                )
+        for copy in copies:
+            copy.start()
+        for (pieces, side), ref in zip(stored, code_refs):
+            if side == 1:
+                terms = ref[:, wide:].astype(jnp.float32)
+                scale = (terms[:, :1] + terms[:, 1:2]) + terms[:, 2:3]
+                scale = jnp.broadcast_to(scale, (scale.shape[0], EXTRA))
+                got_scales.append((pieces, scale))
+    got_scale_refs = take(1 if earlier else len(got_scales))
     if order:
-        rotate(order, norm, where_ref, *inputs, *outputs, refs[0])
+        rotate(order, norm, where_ref, *inputs, *outputs, *take(1))
     if earlier:
-        table = refs[0]
+        (table,) = take(1)
         for (pieces, side), ref in zip(earlier, scales):
             for rows, place in places(where_ref, pieces, half, side):
                 table[place, :] = ref[rows, :]
-        for pieces, scale in zip(stored, got_scales):
+        for pieces, scale in got_scales:
             for rows, place in places(where_ref, pieces, half, 1):
                 table[place, :] = scale[rows]
         shape = (EXTRA, EXTRA)
@@ -206,19 +207,16 @@
             block = table[q * EXTRA : (q + 1) * EXTRA, :]
             line = jnp.sum(jnp.where(row == lane, block, 0.0), axis=0, keepdims=True)
             scale_ref[q : q + 1, :] = line
-    elif stored:
-        for ref, scale in zip(got_scale_refs, got_scales):
+    else:
+        for ref, (_, scale) in zip(got_scale_refs, got_scales):
             ref[...] = scale
     for copy in copies:
         copy.wait()
 
 
-def codes_call(order, norm, inputs, stored, pairs, earlier, scales, out, where, half, full):
+def codes_call(order, norm, inputs, stored, parts, earlier, scales, out, where, half, full):
     dtype = jnp.bfloat16
-    operands = [where, *inputs]
-    for pair in pairs:
-        operands.extend(pair)
-    operands.extend(scales)
+    operands = [where, *inputs, *parts, *scales]
     in_specs = [whole(pltpu.SMEM)] + [whole()] * (len(operands) - 1)
     out_specs, out_shape, scratch, aliases = [], [], [], {}
     moved = 0
@@ -239,11 +237,13 @@
             in_specs.append(whole(pl.ANY))
             operands.append(out)
         out_specs.append(whole(pl.ANY))
-        out_shape.append(jax.ShapeDtypeStruct((full, pairs[0][0].shape[1] - EXTRA), dtype))
-        heights = [full // EXTRA] if earlier else [own.shape[0] for own, _ in pairs]
-        out_specs += [whole()] * len(heights)
-        out_shape += [jax.ShapeDtypeStruct((rows, EXTRA), jnp.float32) for rows in heights]
-        scratch.append(pltpu.SemaphoreType.DMA((2 * sum(len(pieces) for pieces in stored),)))
+        out_shape.append(jax.ShapeDtypeStruct((full, parts[0].shape[1] - EXTRA), dtype))
+        scratch.append(pltpu.SemaphoreType.DMA((sum(len(pieces) for pieces, _ in stored),)))
+    heights = [part.shape[0] for part, (_, side) in zip(parts, stored) if side == 1]
+    if earlier:
+        heights = [full // EXTRA]
+    out_specs += [whole()] * len(heights)
+    out_shape += [jax.ShapeDtypeStruct((height, EXTRA), jnp.float32) for height in heights]
     return pl.pallas_call(
         functools.partial(codes_kernel, order, norm, stored, half, earlier, bool(aliases)),
         in_specs=in_specs,
@@ -253,7 +253,7 @@
         input_output_aliases=aliases,
         compiler_params=pltpu.CompilerParams(vmem_limit_bytes=VMEM_LIMIT),
         cost_estimate=WORTH,
-        name=f"rotate{moved}_store{sum(len(pieces) for pieces in stored)}",
+        name=f"rotate{moved}_store{sum(len(pieces) for pieces, _ in stored)}",
     )(*operands)
 
 
@@ -283,13 +283,13 @@
     scales = {}
     codes = None
     for step in PLAN:
-        kind, i = step[0], int(step[1])
+        kind, i = step[0], int(step[1:2])
         if kind == "z":
             token = after(part[i : i + 2])
             pair = swapped(token, "row", i)
             pieces[i], pieces[i + 1] = pair[0], pair[1]
             continue
-        names, order = CHUNKS[i] if kind != "r" else ((), ())
+        names, order = CHUNKS[i] if kind not in "or" else ((), ())
         order = [STEPS[name] for name in order]
         if kind == "m":
             token = after(jnp.concatenate([pieces[name] for name in names])[None])
@@ -305,21 +305,26 @@
             token = held[i] = after(held[i])
             got[i] = swapped(token, "col", 2 * order[turn])
         else:
-            ready = [int(name) for name in step.partition("r")[2]]
-            stored = [CHUNKS[c][0] for c in ready]
-            pairs = [(held[c], got[c]) for c in ready]
+            named, side = [], 0
+            for letter in step[2 * (kind == "k") :]:
+                if letter in "or":
+                    side = "or".index(letter)
+                else:
+                    named.append((int(letter), side))
+            stored = [(CHUNKS[c][0], side) for c, side in named]
+            parts = [(held, got)[side][c] for c, side in named]
             earlier = dict(scales) if step == PLAN[-1] else {}
             inputs = ()
             if kind == "k":
                 inputs = (held[i], after(got[i]))
             else:
-                pairs[-1] = (pairs[-1][0], after(pairs[-1][1]))
+                parts[-1] = after(parts[-1])
             made = codes_call(
                 order,
                 norm,
                 inputs,
                 stored,
-                pairs,
+                parts,
                 list(earlier),
                 list(earlier.values()),
                 codes,
@@ -331,9 +336,10 @@
                 held[i], scales[names, 0], *made = made
                 got[i] = swapped(held[i], "col", 1)
                 token = held[i]
-            if ready:
+            if stored:
                 codes, *made = made
-                for pieces_of, scale in zip(stored, made):
+                got_pieces = [pieces_of for pieces_of, side in stored if side == 1]
+                for pieces_of, scale in zip(got_pieces, made):
                     scales[pieces_of, 1] = scale
 
     return codes, made[0].reshape(rows)

time: 104 us -> 98.9 us (0.951)
  waiting for transfers between devices: 26.9 us -> 19.9 us
    ppermute x28, waiting for transfers between devices: 24.7 us -> 19.2 us  [swapped(): return lax.ppermute(value, axis, pairs)]
    ppermute x3, waiting for transfers between devices: 2.22 us -> 0.72 us  [from_neighbours(): lax.ppermute(value, ('col', 'row'), pairs)]
    pallas_call x7 -> x8, Pallas kernels: 14.8 us -> 15.6 us  [codes_call(): pl.pallas_call(functools.partial(codes_kernel, order, norm, stored, half,...]
  transfers between devices with their start and end apart: 31 -> 31, of which waited for: 14 -> 13; matrix products, arithmetic and copies ran while one was open for 1% -> 1% of each run, Pallas kernels for 9% -> 13%
where the time goes in v3:
time: 98.9 us; the launch traced here: 98.8 us
  starting transfers between devices  59 us (60%)
  waiting for transfers between devices  19.9 us (20%)
  Pallas kernels  16.9 us (17%)
  local copies, waits for them, and re-layouts  1.44 us (1%)
    ppermute x28, starting transfers between devices, swapped(): return lax.ppermute(value, axis, pairs)  53.7 us
    ppermute x28, waiting for transfers between devices, swapped(): return lax.ppermute(value, axis, pairs)  19.2 us
    pallas_call x8, Pallas kernels, codes_call(): pl.pallas_call(functools.partial(codes_kernel, order, norm, stored, half,...  15.6 us
    ppermute x3, starting transfers between devices, from_neighbours(): lax.ppermute(value, ('col', 'row'), pairs)  5.29 us
  transfers between devices with their start and end apart: 31, of which 13 were waited for; matrix products, arithmetic and copies ran while one was open for 1% of the time, Pallas kernels for 13%

profile of v3, /device:TPU:1, one launch (start us, length us, event | category | flops | bytes accessed | tf_op | source)
XLA Modules:
  0.0 98.8 jit_solution(17917381223644982656)
XLA Ops:
  0.7 1.3 %constant_dynamic-slice_fusion = (bf16[8,32,1024]{2,1,0:T(8,128)(2,1)S(1)}, bf16[8,32,1024]{2,1,0:T(8,128)(2,1)S(1)}) fusion(bf16[8,64,1024]{2,1,0:T(8,128)(2,1)} %bitcast.17, s32[]{:T(128)S(6)} %select_n.20, s32[]{:T(128)S(6)} %select_n.19), kind=kLoop, calls=%fused_computation.19 | loop fusion | bytes 2097160 | tf_op jit(solution)/shard_map/dynamic_slice | solution.py:272
  2.0 1.5 %collective-permute-start = (bf16[8,32,1024]{2,1,0:T(8,128)(2,1)S(1)}, bf16[8,32,1024]{2,1,0:T(8,128)(2,1)S(1)}, u32[]{:S(2)}, u32[]{:S(2)}) collective-permute-start(bf16[8,32,1024]{2,1,0:T(8,128)(2,1)S(1)} %get-tuple-element.115), channel_id=1, source_target_pairs={{0,8},{8,0},{16,24},{24,16},{32,40},{40,32},{48,56},{56,48},{64,72... | collective-permute-start | bytes 1572872 | tf_op jit(solution)/shard_map/ppermute | solution.py:40
  3.5 1.5 %collective-permute-done.got_ref = bf16[8,32,1024]{2,1,0:T(8,128)(2,1)S(1)} collective-permute-done((bf16[8,32,1024]{2,1,0:T(8,128)(2,1)S(1)}, bf16[8,32,1024]{2,1,0:T(8,128)(2,1)S(1)}, u32[]{:S(2)}, u32[]{:S(2)}) %collective-permute-start) | collective-permute-done | bytes 524320 | tf_op jit(solution)/shard_map/ppermute | solution.py:40
  5.0 1.3 %first_rotation.1 = bf16[8,32,2048]{2,1,0:T(8,128)(2,1)S(1)} custom-call(s32[3]{0:T(128)S(1)} %pad_add_fusion.where_ref, bf16[8,32,1024]{2,1,0:T(8,128)(2,1)S(1)} %get-tuple-element.116.own_ref, bf16[8,32,1024]{2,1,0:T(8,128)(2,1)S(1)} %collective-permute-done.got_ref), custom_call_target="tpu_custom_call" | custom-call | flops 20000000000 | bytes 1 | tf_op jit(solution)/shard_map/first_rotation/pallas_call | solution.py:102
  6.4 3.9 %collective-permute-start.2 = (bf16[2,32,2048]{2,1,0:T(8,128)(2,1)S(1)}, bf16[2,32,2048]{2,1,0:T(8,128)(2,1)S(1)}, u32[]{:S(2)}, u32[]{:S(2)}) collective-permute-start(bf16[2,32,2048]{2,1,0:T(8,128)(2,1)S(1)} %get-tuple-element.58), channel_id=1, source_target_pairs={{0,6},{1,7},{2,4},{3,5},{4,2},{5,3},{6,0},{7,1},{8,14},{9,15},{10,... | collective-permute-start | bytes 786440 | tf_op jit(solution)/shard_map/ppermute | solution.py:40
  10.3 1.3 %collective-permute-start.12 = (bf16[1,32,2048]{2,1,0:T(8,128)(2,1)S(1)}, bf16[1,32,2048]{2,1,0:T(8,128)(2,1)S(1)}, u32[]{:S(2)}, u32[]{:S(2)}) collective-permute-start(bf16[1,32,2048]{2,1,0:T(8,128)(2,1)S(1)} %get-tuple-element.57), channel_id=1, source_target_pairs={{0,1},{1,0},{2,3},{3,2},{4,5},{5,4},{6,7},{7,6},{8,9},{9,8},{10,11... | collective-permute-start | bytes 393224 | tf_op jit(solution)/shard_map/ppermute | solution.py:40
  11.6 1.9 %collective-permute-start.13 = (bf16[1,32,2048]{2,1,0:T(8,128)(2,1)S(1)}, bf16[1,32,2048]{2,1,0:T(8,128)(2,1)S(1)}, u32[]{:S(2)}, u32[]{:S(2)}) collective-permute-start(bf16[1,32,2048]{2,1,0:T(8,128)(2,1)S(1)} %get-tuple-element.57), channel_id=1, source_target_pairs={{0,65},{1,64},{2,67},{3,66},{4,69},{5,68},{6,71},{7,70},{8,73},{9,... | collective-permute-start | bytes 393224 | tf_op jit(solution)/shard_map/ppermute | solution.py:47
  14.8 1.9 %collective-permute-done.2 = bf16[2,32,2048]{2,1,0:T(8,128)(2,1)S(1)} collective-permute-done((bf16[2,32,2048]{2,1,0:T(8,128)(2,1)S(1)}, bf16[2,32,2048]{2,1,0:T(8,128)(2,1)S(1)}, u32[]{:S(2)}, u32[]{:S(2)}) %collective-permute-start.2) | collective-permute-done | bytes 262176 | tf_op jit(solution)/shard_map/ppermute | solution.py:40
  17.6 2.6 %collective-permute-start.3 = (bf16[1,64,2048]{2,1,0:T(8,128)(2,1)S(1)}, bf16[1,64,2048]{2,1,0:T(8,128)(2,1)S(1)}, u32[]{:S(2)}, u32[]{:S(2)}) collective-permute-start(bf16[1,64,2048]{2,1,0:T(8,128)(2,1)S(1)} %get-tuple-element.60), channel_id=1, source_target_pairs={{0,48},{8,56},{16,32},{24,40},{32,16},{40,24},{48,0},{56,8},{64,11... | collective-permute-start | bytes 786440 | tf_op jit(solution)/shard_map/ppermute | solution.py:40
  20.1 2.9 %collective-permute-done.8 = bf16[2,32,2048]{2,1,0:T(8,128)(2,1)S(1)} collective-permute-done((bf16[2,32,2048]{2,1,0:T(8,128)(2,1)S(1)}, bf16[2,32,2048]{2,1,0:T(8,128)(2,1)S(1)}, u32[]{:S(2)}, u32[]{:S(2)}) %collective-permute-start.8) | collective-permute-done | bytes 262176 | tf_op jit(solution)/shard_map/ppermute | solution.py:40
  24.6 3.0 %collective-permute-start.10 = (bf16[1,32,2048]{2,1,0:T(8,128)(2,1)S(1)}, bf16[1,32,2048]{2,1,0:T(8,128)(2,1)S(1)}, u32[]{:S(2)}, u32[]{:S(2)}) collective-permute-start(bf16[1,32,2048]{2,1,0:T(8,128)(2,1)S(1)} %get-tuple-element.66), channel_id=1, source_target_pairs={{0,65},{1,64},{2,67},{3,66},{4,69},{5,68},{6,71},{7,70},{8,73},{9,... | collective-permute-start | bytes 393224 | tf_op jit(solution)/shard_map/ppermute | solution.py:47
  27.5 2.1 %collective-permute-start.17 = (bf16[2,32,2048]{2,1,0:T(8,128)(2,1)S(1)}, bf16[2,32,2048]{2,1,0:T(8,128)(2,1)S(1)}, u32[]{:S(2)}, u32[]{:S(2)}) collective-permute-start(bf16[2,32,2048]{2,1,0:T(8,128)(2,1)S(1)} %pad_maximum_fusion.8), channel_id=1, source_target_pairs={{0,48},{8,56},{16,32},{24,40},{32,16},{40,24},{48,0},{56,8},{64,11... | collective-permute-start | bytes 786440 | tf_op jit(solution)/shard_map/ppermute | solution.py:40
  29.6 1.5 %collective-permute-start.6 = (bf16[1,64,2048]{2,1,0:T(8,128)(2,1)S(1)}, bf16[1,64,2048]{2,1,0:T(8,128)(2,1)S(1)}, u32[]{:S(2)}, u32[]{:S(2)}) collective-permute-start(bf16[1,64,2048]{2,1,0:T(8,128)(2,1)S(1)} %get-tuple-element.64), channel_id=1, source_target_pairs={{0,1},{1,0},{2,3},{3,2},{4,5},{5,4},{6,7},{7,6},{8,9},{9,8},{10,11... | collective-permute-start | bytes 786440 | tf_op jit(solution)/shard_map/ppermute | solution.py:40
  32.1 1.6 %collective-permute-start.16 = (bf16[2,32,2048]{2,1,0:T(8,128)(2,1)S(1)}, bf16[2,32,2048]{2,1,0:T(8,128)(2,1)S(1)}, u32[]{:S(2)}, u32[]{:S(2)}) collective-permute-start(bf16[2,32,2048]{2,1,0:T(8,128)(2,1)S(1)} %pad_maximum_fusion.11), channel_id=1, source_target_pairs={{0,48},{8,56},{16,32},{24,40},{32,16},{40,24},{48,0},{56,8},{64,11... | collective-permute-start | bytes 786440 | tf_op jit(solution)/shard_map/ppermute | solution.py:40
  33.7 2.0 %collective-permute-done.6 = bf16[1,64,2048]{2,1,0:T(8,128)(2,1)S(1)} collective-permute-done((bf16[1,64,2048]{2,1,0:T(8,128)(2,1)S(1)}, bf16[1,64,2048]{2,1,0:T(8,128)(2,1)S(1)}, u32[]{:S(2)}, u32[]{:S(2)}) %collective-permute-start.6) | collective-permute-done | bytes 262176 | tf_op jit(solution)/shard_map/ppermute | solution.py:40
  35.8 1.3 %collective-permute-start.15 = (bf16[2,32,2048]{2,1,0:T(8,128)(2,1)S(1)}, bf16[2,32,2048]{2,1,0:T(8,128)(2,1)S(1)}, u32[]{:S(2)}, u32[]{:S(2)}) collective-permute-start(bf16[2,32,2048]{2,1,0:T(8,128)(2,1)S(1)} %pad_maximum_fusion.10), channel_id=1, source_target_pairs={{0,64},{8,72},{16,80},{24,88},{32,96},{40,104},{48,112},{56,120},{... | collective-permute-start | bytes 786440 | tf_op jit(solution)/shard_map/ppermute | solution.py:40
  37.8 1.3 %collective-permute-start.21 = (bf16[2,32,2048]{2,1,0:T(8,128)(2,1)S(1)}, bf16[2,32,2048]{2,1,0:T(8,128)(2,1)S(1)}, u32[]{:S(2)}, u32[]{:S(2)}) collective-permute-start(bf16[2,32,2048]{2,1,0:T(8,128)(2,1)S(1)} %pad_maximum_fusion.9), channel_id=1, source_target_pairs={{0,16},{8,24},{16,0},{24,8},{32,48},{40,56},{48,32},{56,40},{64,80... | collective-permute-start | bytes 786440 | tf_op jit(solution)/shard_map/ppermute | solution.py:40
  39.2 1.3 %collective-permute-start.14 = (bf16[2,64,2048]{2,1,0:T(8,128)(2,1)S(1)}, bf16[2,64,2048]{2,1,0:T(8,128)(2,1)S(1)}, u32[]{:S(2)}, u32[]{:S(2)}) collective-permute-start(bf16[2,64,2048]{2,1,0:T(8,128)(2,1)S(1)} %pad_maximum_fusion.3), channel_id=1, source_target_pairs={{0,48},{8,56},{16,32},{24,40},{32,16},{40,24},{48,0},{56,8},{64,11... | collective-permute-start | bytes 1572872 | tf_op jit(solution)/shard_map/ppermute | solution.py:40
  41.1 2.1 %collective-permute-start.24 = (bf16[4,32,2048]{2,1,0:T(8,128)(2,1)S(1)}, bf16[4,32,2048]{2,1,0:T(8,128)(2,1)S(1)}, u32[]{:S(2)}, u32[]{:S(2)}) collective-permute-start(bf16[4,32,2048]{2,1,0:T(8,128)(2,1)S(1)} %pad_maximum_fusion.6.refs_0_), channel_id=1, source_target_pairs={{0,64},{8,72},{16,80},{24,88},{32,96},{40,104},{48,112},{56,120},{... | collective-permute-start | bytes 1572872 | tf_op jit(solution)/shard_map/ppermute | solution.py:40
  44.3 1.8 %collective-permute-done.21 = bf16[2,32,2048]{2,1,0:T(8,128)(2,1)S(1)} collective-permute-done((bf16[2,32,2048]{2,1,0:T(8,128)(2,1)S(1)}, bf16[2,32,2048]{2,1,0:T(8,128)(2,1)S(1)}, u32[]{:S(2)}, u32[]{:S(2)}) %collective-permute-start.21) | collective-permute-done | bytes 262176 | tf_op jit(solution)/shard_map/ppermute | solution.py:40
  47.4 3.5 %collective-permute-done.14 = bf16[2,64,2048]{2,1,0:T(8,128)(2,1)S(1)} collective-permute-done((bf16[2,64,2048]{2,1,0:T(8,128)(2,1)S(1)}, bf16[2,64,2048]{2,1,0:T(8,128)(2,1)S(1)}, u32[]{:S(2)}, u32[]{:S(2)}) %collective-permute-start.14) | collective-permute-done | bytes 524320 | tf_op jit(solution)/shard_map/ppermute | solution.py:40
  51.8 1.8 %collective-permute-done.24.refs_1_ = bf16[4,32,2048]{2,1,0:T(8,128)(2,1)S(1)} collective-permute-done((bf16[4,32,2048]{2,1,0:T(8,128)(2,1)S(1)}, bf16[4,32,2048]{2,1,0:T(8,128)(2,1)S(1)}, u32[]{:S(2)}, u32[]{:S(2)}) %collective-permute-start.24) | collective-permute-done | bytes 524320 | tf_op jit(solution)/shard_map/ppermute | solution.py:40
  53.5 1.5 %collective-permute-start.22 = (bf16[4,32,2048]{2,1,0:T(8,128)(2,1)S(1)}, bf16[4,32,2048]{2,1,0:T(8,128)(2,1)S(1)}, u32[]{:S(2)}, u32[]{:S(2)}) collective-permute-start(bf16[4,32,2048]{2,1,0:T(8,128)(2,1)S(1)} %pad_maximum_fusion.7.refs_0_), channel_id=1, source_target_pairs={{0,48},{8,56},{16,32},{24,40},{32,16},{40,24},{48,0},{56,8},{64,11... | collective-permute-start | bytes 1572872 | tf_op jit(solution)/shard_map/ppermute | solution.py:40
  56.2 19.9 %collective-permute-start.26 = (bf16[32,16512]{1,0:T(8,128)(2,1)S(1)}, bf16[32,16512]{1,0:T(8,128)(2,1)S(1)}, u32[]{:S(2)}, u32[]{:S(2)}) collective-permute-start(bf16[32,16512]{1,0:T(8,128)(2,1)S(1)} %get-tuple-element.78.refs_2_), channel_id=1, source_target_pairs={{0,8},{8,0},{16,24},{24,16},{32,40},{40,32},{48,56},{56,48},{64,72... | collective-permute-start | bytes 3170312 | tf_op jit(solution)/shard_map/ppermute | solution.py:40
  76.1 1.5 %rotate1_store1.3 = (bf16[32,16512]{1,0:T(8,128)(2,1)S(1)}, f32[32,128]{1,0:T(8,128)S(1)}, bf16[512,16384]{1,0:T(8,128)(2,1)}) custom-call(s32[3]{0:T(128)S(1)} %pad_add_fusion.where_ref, bf16[4,32,2048]{2,1,0:T(8,128)(2,1)S(1)} %pad_maximum_fusion.5.refs_0_, bf16[4,32,2048]{2,1,0:T(8,128)(2,1)S(1)} %collective-permute-done.23.refs_1_, ...), custom_call_target="tpu_custom_call" | custom-call | flops 20000000000 | bytes 1 | tf_op jit(solution)/shard_map/rotate1_store1/pallas_call | solution.py:247
  77.6 5.4 %collective-permute-start.25 = (bf16[32,16512]{1,0:T(8,128)(2,1)S(1)}, bf16[32,16512]{1,0:T(8,128)(2,1)S(1)}, u32[]{:S(2)}, u32[]{:S(2)}) collective-permute-start(bf16[32,16512]{1,0:T(8,128)(2,1)S(1)} %get-tuple-element.80.refs_2_), channel_id=1, source_target_pairs={{0,8},{8,0},{16,24},{24,16},{32,40},{40,32},{48,56},{56,48},{64,72... | collective-permute-start | bytes 3170312 | tf_op jit(solution)/shard_map/ppermute | solution.py:40
  83.0 1.5 %rotate1_store1.4 = (bf16[32,16512]{1,0:T(8,128)(2,1)S(1)}, f32[32,128]{1,0:T(8,128)S(1)}, bf16[512,16384]{1,0:T(8,128)(2,1)}) custom-call(s32[3]{0:T(128)S(1)} %pad_add_fusion.where_ref, bf16[4,32,2048]{2,1,0:T(8,128)(2,1)S(1)} %pad_maximum_fusion.7.refs_0_, ...), custom_call_target="tpu_custom_call", output_to_operand_aliasing={{2}: (4, {})} | custom-call | flops 20000000000 | bytes 1 | tf_op jit(solution)/shard_map/rotate1_store1/pallas_call | solution.py:247
  84.7 1.5 %rotate1_store1.5 = (bf16[32,16512]{1,0:T(8,128)(2,1)S(1)}, f32[32,128]{1,0:T(8,128)S(1)}, bf16[512,16384]{1,0:T(8,128)(2,1)}) custom-call(s32[3]{0:T(128)S(1)} %pad_add_fusion.where_ref, bf16[4,32,2048]{2,1,0:T(8,128)(2,1)S(1)} %pad_maximum_fusion.4.refs_0_, ...), custom_call_target="tpu_custom_call", output_to_operand_aliasing={{2}: (4, {})} | custom-call | flops 20000000000 | bytes 1 | tf_op jit(solution)/shard_map/rotate1_store1/pallas_call | solution.py:247
  86.8 2.2 %rotate2_store3.1 = (bf16[64,16512]{1,0:T(8,128)(2,1)S(1)}, f32[64,128]{1,0:T(8,128)S(1)}, bf16[512,16384]{1,0:T(8,128)(2,1)}, f32[32,128]{1,0:T(8,128)S(1)}, f32[32,128]{1,0:T(8,128)S(1)}) custom-call(s32[3]{0:T(128)S(1)} %pad_add_fusion.where_ref, bf16[4,64,2048]{2,1,0:T(8,128)(2,1)S(1)} %pad_maximum_fusion.1.refs_0_, ...), custom_call_target="tpu_custom_call", output_to_operand_aliasing={{2}: (6, {})} | custom-call | flops 20000000000 | bytes 1 | tf_op jit(solution)/shard_map/rotate2_store3/pallas_call | solution.py:247
  89.2 2.6 %rotate2_store4.1 = (bf16[64,16512]{1,0:T(8,128)(2,1)S(1)}, f32[64,128]{1,0:T(8,128)S(1)}, bf16[512,16384]{1,0:T(8,128)(2,1)}, f32[32,128]{1,0:T(8,128)S(1)}, f32[32,128]{1,0:T(8,128)S(1)}) custom-call(s32[3]{0:T(128)S(1)} %pad_add_fusion.where_ref, bf16[4,64,2048]{2,1,0:T(8,128)(2,1)S(1)} %pad_maximum_fusion.refs_0_, ...), custom_call_target="tpu_custom_call", output_to_operand_aliasing={{2}: (6, {})} | custom-call | flops 20000000000 | bytes 1 | tf_op jit(solution)/shard_map/rotate2_store4/pallas_call | solution.py:247
  93.3 2.6 %rotate0_store4.1 = (bf16[512,16384]{1,0:T(8,128)(2,1)}, f32[64,128]{1,0:T(8,128)S(1)}) custom-call(s32[3]{0:T(128)S(1)} %pad_add_fusion.where_ref, bf16[64,16512]{1,0:T(8,128)(2,1)S(1)} %get-tuple-element.92.refs_0_, bf16[64,16512]{1,0:T(8,128)(2,1)S(1)} %collective-permute-done.30.refs_1_, ...), custom_call_target="tpu_custom_call", output_to_operand_aliasing={{0}: (3, {})} | custom-call | flops 20000000000 | bytes 1 | tf_op jit(solution)/shard_map/rotate0_store4/pallas_call | solution.py:247
  96.3 2.5 %rotate0_store2.1 = (bf16[512,16384]{1,0:T(8,128)(2,1)}, f32[4,128]{1,0:T(4,128)}) custom-call(s32[3]{0:T(128)S(1)} %pad_add_fusion.where_ref, bf16[64,16512]{1,0:T(8,128)(2,1)S(1)} %collective-permute-done.29.refs_0_, f32[32,128]{1,0:T(8,128)S(1)} %get-tuple-element.94.refs_1_, ...), custom_call_target="tpu_custom_call", output_to_operand_aliasing={{0}: (13, {})} | custom-call | flops 20000000000 | bytes 1 | tf_op jit(solution)/shard_map/rotate0_store2/pallas_call | solution.py:247
  (59 shorter events, 13.4 us)
Async XLA Ops:
  2.0 3.0 %collective-permute-start = (bf16[8,32,1024]{2,1,0:T(8,128)(2,1)S(1)}, bf16[8,32,1024]{2,1,0:T(8,128)(2,1)S(1)}, u32[]{:S(2)}, u32[]{:S(2)}) collective-permute-start(bf16[8,32,1024]{2,1,0:T(8,128)(2,1)S(1)} %get-tuple-element.115), channel_id=1, source_target_pairs={{0,8},{8,0},{16,24},{24,16},{32,40},{40,32},{48,56},{56,48},{64,72... | collective-permute-start | bytes 1572872 | tf_op jit(solution)/shard_map/ppermute | solution.py:40
  6.4 10.3 %collective-permute-start.2 = (bf16[2,32,2048]{2,1,0:T(8,128)(2,1)S(1)}, bf16[2,32,2048]{2,1,0:T(8,128)(2,1)S(1)}, u32[]{:S(2)}, u32[]{:S(2)}) collective-permute-start(bf16[2,32,2048]{2,1,0:T(8,128)(2,1)S(1)} %get-tuple-element.58), channel_id=1, source_target_pairs={{0,6},{1,7},{2,4},{3,5},{4,2},{5,3},{6,0},{7,1},{8,14},{9,15},{10,... | collective-permute-start | bytes 786440 | tf_op jit(solution)/shard_map/ppermute | solution.py:40
  10.3 7.2 %collective-permute-start.1 = (bf16[2,32,2048]{2,1,0:T(8,128)(2,1)S(1)}, bf16[2,32,2048]{2,1,0:T(8,128)(2,1)S(1)}, u32[]{:S(2)}, u32[]{:S(2)}) collective-permute-start(bf16[2,32,2048]{2,1,0:T(8,128)(2,1)S(1)} %get-tuple-element.56), channel_id=1, source_target_pairs={{0,2},{1,3},{2,0},{3,1},{4,6},{5,7},{6,4},{7,5},{8,10},{9,11},{10,... | collective-permute-start | bytes 786440 | tf_op jit(solution)/shard_map/ppermute | solution.py:40
  10.3 14.2 %collective-permute-start.12 = (bf16[1,32,2048]{2,1,0:T(8,128)(2,1)S(1)}, bf16[1,32,2048]{2,1,0:T(8,128)(2,1)S(1)}, u32[]{:S(2)}, u32[]{:S(2)}) collective-permute-start(bf16[1,32,2048]{2,1,0:T(8,128)(2,1)S(1)} %get-tuple-element.57), channel_id=1, source_target_pairs={{0,1},{1,0},{2,3},{3,2},{4,5},{5,4},{6,7},{7,6},{8,9},{9,8},{10,11... | collective-permute-start | bytes 393224 | tf_op jit(solution)/shard_map/ppermute | solution.py:40
  11.6 12.9 %collective-permute-start.13 = (bf16[1,32,2048]{2,1,0:T(8,128)(2,1)S(1)}, bf16[1,32,2048]{2,1,0:T(8,128)(2,1)S(1)}, u32[]{:S(2)}, u32[]{:S(2)}) collective-permute-start(bf16[1,32,2048]{2,1,0:T(8,128)(2,1)S(1)} %get-tuple-element.57), channel_id=1, source_target_pairs={{0,65},{1,64},{2,67},{3,66},{4,69},{5,68},{6,71},{7,70},{8,73},{9,... | collective-permute-start | bytes 393224 | tf_op jit(solution)/shard_map/ppermute | solution.py:47
  13.5 9.5 %collective-permute-start.8 = (bf16[2,32,2048]{2,1,0:T(8,128)(2,1)S(1)}, bf16[2,32,2048]{2,1,0:T(8,128)(2,1)S(1)}, u32[]{:S(2)}, u32[]{:S(2)}) collective-permute-start(bf16[2,32,2048]{2,1,0:T(8,128)(2,1)S(1)} %get-tuple-element.59), channel_id=1, source_target_pairs={{0,4},{1,5},{2,6},{3,7},{4,0},{5,1},{6,2},{7,3},{8,12},{9,13},{10,... | collective-permute-start | bytes 786440 | tf_op jit(solution)/shard_map/ppermute | solution.py:40
  17.6 6.5 %collective-permute-start.3 = (bf16[1,64,2048]{2,1,0:T(8,128)(2,1)S(1)}, bf16[1,64,2048]{2,1,0:T(8,128)(2,1)S(1)}, u32[]{:S(2)}, u32[]{:S(2)}) collective-permute-start(bf16[1,64,2048]{2,1,0:T(8,128)(2,1)S(1)} %get-tuple-element.60), channel_id=1, source_target_pairs={{0,48},{8,56},{16,32},{24,40},{32,16},{40,24},{48,0},{56,8},{64,11... | collective-permute-start | bytes 786440 | tf_op jit(solution)/shard_map/ppermute | solution.py:40
  20.1 3.9 %collective-permute-start.5 = (bf16[1,32,2048]{2,1,0:T(8,128)(2,1)S(1)}, bf16[1,32,2048]{2,1,0:T(8,128)(2,1)S(1)}, u32[]{:S(2)}, u32[]{:S(2)}) collective-permute-start(bf16[1,32,2048]{2,1,0:T(8,128)(2,1)S(1)} %get-tuple-element.61), channel_id=1, source_target_pairs={{0,16},{8,24},{16,0},{24,8},{32,48},{40,56},{48,32},{56,40},{64,80... | collective-permute-start | bytes 393224 | tf_op jit(solution)/shard_map/ppermute | solution.py:40
  24.2 6.9 %collective-permute-start.11 = (bf16[1,32,2048]{2,1,0:T(8,128)(2,1)S(1)}, bf16[1,32,2048]{2,1,0:T(8,128)(2,1)S(1)}, u32[]{:S(2)}, u32[]{:S(2)}) collective-permute-start(bf16[1,32,2048]{2,1,0:T(8,128)(2,1)S(1)} %get-tuple-element.65), channel_id=1, source_target_pairs={{0,16},{8,24},{16,0},{24,8},{32,48},{40,56},{48,32},{56,40},{64,80... | collective-permute-start | bytes 393224 | tf_op jit(solution)/shard_map/ppermute | solution.py:40
  24.6 7.0 %collective-permute-start.10 = (bf16[1,32,2048]{2,1,0:T(8,128)(2,1)S(1)}, bf16[1,32,2048]{2,1,0:T(8,128)(2,1)S(1)}, u32[]{:S(2)}, u32[]{:S(2)}) collective-permute-start(bf16[1,32,2048]{2,1,0:T(8,128)(2,1)S(1)} %get-tuple-element.66), channel_id=1, source_target_pairs={{0,65},{1,64},{2,67},{3,66},{4,69},{5,68},{6,71},{7,70},{8,73},{9,... | collective-permute-start | bytes 393224 | tf_op jit(solution)/shard_map/ppermute | solution.py:47
  27.5 4.6 %collective-permute-start.9 = (bf16[1,32,2048]{2,1,0:T(8,128)(2,1)S(1)}, bf16[1,32,2048]{2,1,0:T(8,128)(2,1)S(1)}, u32[]{:S(2)}, u32[]{:S(2)}) collective-permute-start(bf16[1,32,2048]{2,1,0:T(8,128)(2,1)S(1)} %get-tuple-element.66), channel_id=1, source_target_pairs={{0,1},{1,0},{2,3},{3,2},{4,5},{5,4},{6,7},{7,6},{8,9},{9,8},{10,11... | collective-permute-start | bytes 393224 | tf_op jit(solution)/shard_map/ppermute | solution.py:40
  27.5 11.6 %collective-permute-start.17 = (bf16[2,32,2048]{2,1,0:T(8,128)(2,1)S(1)}, bf16[2,32,2048]{2,1,0:T(8,128)(2,1)S(1)}, u32[]{:S(2)}, u32[]{:S(2)}) collective-permute-start(bf16[2,32,2048]{2,1,0:T(8,128)(2,1)S(1)} %pad_maximum_fusion.8), channel_id=1, source_target_pairs={{0,48},{8,56},{16,32},{24,40},{32,16},{40,24},{48,0},{56,8},{64,11... | collective-permute-start | bytes 786440 | tf_op jit(solution)/shard_map/ppermute | solution.py:40
  29.6 6.2 %collective-permute-start.6 = (bf16[1,64,2048]{2,1,0:T(8,128)(2,1)S(1)}, bf16[1,64,2048]{2,1,0:T(8,128)(2,1)S(1)}, u32[]{:S(2)}, u32[]{:S(2)}) collective-permute-start(bf16[1,64,2048]{2,1,0:T(8,128)(2,1)S(1)} %get-tuple-element.64), channel_id=1, source_target_pairs={{0,1},{1,0},{2,3},{3,2},{4,5},{5,4},{6,7},{7,6},{8,9},{9,8},{10,11... | collective-permute-start | bytes 786440 | tf_op jit(solution)/shard_map/ppermute | solution.py:40
  31.1 6.7 %collective-permute-start.7 = (bf16[1,64,2048]{2,1,0:T(8,128)(2,1)S(1)}, bf16[1,64,2048]{2,1,0:T(8,128)(2,1)S(1)}, u32[]{:S(2)}, u32[]{:S(2)}) collective-permute-start(bf16[1,64,2048]{2,1,0:T(8,128)(2,1)S(1)} %get-tuple-element.64), channel_id=1, source_target_pairs={{0,65},{1,64},{2,67},{3,66},{4,69},{5,68},{6,71},{7,70},{8,73},{9,... | collective-permute-start | bytes 786440 | tf_op jit(solution)/shard_map/ppermute | solution.py:47
  31.5 15.8 %collective-permute-start.4 = (bf16[2,64,2048]{2,1,0:T(8,128)(2,1)S(1)}, bf16[2,64,2048]{2,1,0:T(8,128)(2,1)S(1)}, u32[]{:S(2)}, u32[]{:S(2)}) collective-permute-start(bf16[2,64,2048]{2,1,0:T(8,128)(2,1)S(1)} %pad_maximum_fusion.2), channel_id=1, source_target_pairs={{0,16},{8,24},{16,0},{24,8},{32,48},{40,56},{48,32},{56,40},{64,80... | collective-permute-start | bytes 1572872 | tf_op jit(solution)/shard_map/ppermute | solution.py:40
  32.1 9.0 %collective-permute-start.16 = (bf16[2,32,2048]{2,1,0:T(8,128)(2,1)S(1)}, bf16[2,32,2048]{2,1,0:T(8,128)(2,1)S(1)}, u32[]{:S(2)}, u32[]{:S(2)}) collective-permute-start(bf16[2,32,2048]{2,1,0:T(8,128)(2,1)S(1)} %pad_maximum_fusion.11), channel_id=1, source_target_pairs={{0,48},{8,56},{16,32},{24,40},{32,16},{40,24},{48,0},{56,8},{64,11... | collective-permute-start | bytes 786440 | tf_op jit(solution)/shard_map/ppermute | solution.py:40
  35.8 7.5 %collective-permute-start.15 = (bf16[2,32,2048]{2,1,0:T(8,128)(2,1)S(1)}, bf16[2,32,2048]{2,1,0:T(8,128)(2,1)S(1)}, u32[]{:S(2)}, u32[]{:S(2)}) collective-permute-start(bf16[2,32,2048]{2,1,0:T(8,128)(2,1)S(1)} %pad_maximum_fusion.10), channel_id=1, source_target_pairs={{0,64},{8,72},{16,80},{24,88},{32,96},{40,104},{48,112},{56,120},{... | collective-permute-start | bytes 786440 | tf_op jit(solution)/shard_map/ppermute | solution.py:40
  37.8 8.3 %collective-permute-start.21 = (bf16[2,32,2048]{2,1,0:T(8,128)(2,1)S(1)}, bf16[2,32,2048]{2,1,0:T(8,128)(2,1)S(1)}, u32[]{:S(2)}, u32[]{:S(2)}) collective-permute-start(bf16[2,32,2048]{2,1,0:T(8,128)(2,1)S(1)} %pad_maximum_fusion.9), channel_id=1, source_target_pairs={{0,16},{8,24},{16,0},{24,8},{32,48},{40,56},{48,32},{56,40},{64,80... | collective-permute-start | bytes 786440 | tf_op jit(solution)/shard_map/ppermute | solution.py:40
  39.2 11.7 %collective-permute-start.14 = (bf16[2,64,2048]{2,1,0:T(8,128)(2,1)S(1)}, bf16[2,64,2048]{2,1,0:T(8,128)(2,1)S(1)}, u32[]{:S(2)}, u32[]{:S(2)}) collective-permute-start(bf16[2,64,2048]{2,1,0:T(8,128)(2,1)S(1)} %pad_maximum_fusion.3), channel_id=1, source_target_pairs={{0,48},{8,56},{16,32},{24,40},{32,16},{40,24},{48,0},{56,8},{64,11... | collective-permute-start | bytes 1572872 | tf_op jit(solution)/shard_map/ppermute | solution.py:40
  41.1 12.5 %collective-permute-start.24 = (bf16[4,32,2048]{2,1,0:T(8,128)(2,1)S(1)}, bf16[4,32,2048]{2,1,0:T(8,128)(2,1)S(1)}, u32[]{:S(2)}, u32[]{:S(2)}) collective-permute-start(bf16[4,32,2048]{2,1,0:T(8,128)(2,1)S(1)} %pad_maximum_fusion.6.refs_0_), channel_id=1, source_target_pairs={{0,64},{8,72},{16,80},{24,88},{32,96},{40,104},{48,112},{56,120},{... | collective-permute-start | bytes 1572872 | tf_op jit(solution)/shard_map/ppermute | solution.py:40
  43.2 13.0 %collective-permute-start.23 = (bf16[4,32,2048]{2,1,0:T(8,128)(2,1)S(1)}, bf16[4,32,2048]{2,1,0:T(8,128)(2,1)S(1)}, u32[]{:S(2)}, u32[]{:S(2)}) collective-permute-start(bf16[4,32,2048]{2,1,0:T(8,128)(2,1)S(1)} %pad_maximum_fusion.5.refs_0_), channel_id=1, source_target_pairs={{0,16},{8,24},{16,0},{24,8},{32,48},{40,56},{48,32},{56,40},{64,80... | collective-permute-start | bytes 1572872 | tf_op jit(solution)/shard_map/ppermute | solution.py:40
  46.1 38.4 %collective-permute-start.20 = (bf16[4,32,2048]{2,1,0:T(8,128)(2,1)S(1)}, bf16[4,32,2048]{2,1,0:T(8,128)(2,1)S(1)}, u32[]{:S(2)}, u32[]{:S(2)}) collective-permute-start(bf16[4,32,2048]{2,1,0:T(8,128)(2,1)S(1)} %pad_maximum_fusion.4.refs_0_), channel_id=1, source_target_pairs={{0,48},{8,56},{16,32},{24,40},{32,16},{40,24},{48,0},{56,8},{64,11... | collective-permute-start | bytes 1572872 | tf_op jit(solution)/shard_map/ppermute | solution.py:40
  51.0 35.2 %collective-permute-start.19 = (bf16[4,64,2048]{2,1,0:T(8,128)(2,1)S(1)}, bf16[4,64,2048]{2,1,0:T(8,128)(2,1)S(1)}, u32[]{:S(2)}, u32[]{:S(2)}) collective-permute-start(bf16[4,64,2048]{2,1,0:T(8,128)(2,1)S(1)} %pad_maximum_fusion.1.refs_0_), channel_id=1, source_target_pairs={{0,16},{8,24},{16,0},{24,8},{32,48},{40,56},{48,32},{56,40},{64,80... | collective-permute-start | bytes 3145736 | tf_op jit(solution)/shard_map/ppermute | solution.py:40
  51.1 38.1 %collective-permute-start.18 = (bf16[4,64,2048]{2,1,0:T(8,128)(2,1)S(1)}, bf16[4,64,2048]{2,1,0:T(8,128)(2,1)S(1)}, u32[]{:S(2)}, u32[]{:S(2)}) collective-permute-start(bf16[4,64,2048]{2,1,0:T(8,128)(2,1)S(1)} %pad_maximum_fusion.refs_0_), channel_id=1, source_target_pairs={{0,64},{8,72},{16,80},{24,88},{32,96},{40,104},{48,112},{56,120},{... | collective-permute-start | bytes 3145736 | tf_op jit(solution)/shard_map/ppermute | solution.py:40
  53.5 24.1 %collective-permute-start.22 = (bf16[4,32,2048]{2,1,0:T(8,128)(2,1)S(1)}, bf16[4,32,2048]{2,1,0:T(8,128)(2,1)S(1)}, u32[]{:S(2)}, u32[]{:S(2)}) collective-permute-start(bf16[4,32,2048]{2,1,0:T(8,128)(2,1)S(1)} %pad_maximum_fusion.7.refs_0_), channel_id=1, source_target_pairs={{0,48},{8,56},{16,32},{24,40},{32,16},{40,24},{48,0},{56,8},{64,11... | collective-permute-start | bytes 1572872 | tf_op jit(solution)/shard_map/ppermute | solution.py:40
  56.2 30.6 %collective-permute-start.26 = (bf16[32,16512]{1,0:T(8,128)(2,1)S(1)}, bf16[32,16512]{1,0:T(8,128)(2,1)S(1)}, u32[]{:S(2)}, u32[]{:S(2)}) collective-permute-start(bf16[32,16512]{1,0:T(8,128)(2,1)S(1)} %get-tuple-element.78.refs_2_), channel_id=1, source_target_pairs={{0,8},{8,0},{16,24},{24,16},{32,40},{40,32},{48,56},{56,48},{64,72... | collective-permute-start | bytes 3170312 | tf_op jit(solution)/shard_map/ppermute | solution.py:40
  77.6 9.2 %collective-permute-start.25 = (bf16[32,16512]{1,0:T(8,128)(2,1)S(1)}, bf16[32,16512]{1,0:T(8,128)(2,1)S(1)}, u32[]{:S(2)}, u32[]{:S(2)}) collective-permute-start(bf16[32,16512]{1,0:T(8,128)(2,1)S(1)} %get-tuple-element.80.refs_2_), channel_id=1, source_target_pairs={{0,8},{8,0},{16,24},{24,16},{32,40},{40,32},{48,56},{56,48},{64,72... | collective-permute-start | bytes 3170312 | tf_op jit(solution)/shard_map/ppermute | solution.py:40
  84.6 4.6 %collective-permute-start.28 = (bf16[32,16512]{1,0:T(8,128)(2,1)S(1)}, bf16[32,16512]{1,0:T(8,128)(2,1)S(1)}, u32[]{:S(2)}, u32[]{:S(2)}) collective-permute-start(bf16[32,16512]{1,0:T(8,128)(2,1)S(1)} %get-tuple-element.83.refs_2_), channel_id=1, source_target_pairs={{0,8},{8,0},{16,24},{24,16},{32,40},{40,32},{48,56},{56,48},{64,72... | collective-permute-start | bytes 3170312 | tf_op jit(solution)/shard_map/ppermute | solution.py:40
  86.2 2.9 %collective-permute-start.27 = (bf16[32,16512]{1,0:T(8,128)(2,1)S(1)}, bf16[32,16512]{1,0:T(8,128)(2,1)S(1)}, u32[]{:S(2)}, u32[]{:S(2)}) collective-permute-start(bf16[32,16512]{1,0:T(8,128)(2,1)S(1)} %get-tuple-element.86.refs_2_), channel_id=1, source_target_pairs={{0,8},{8,0},{16,24},{24,16},{32,40},{40,32},{48,56},{56,48},{64,72... | collective-permute-start | bytes 3170312 | tf_op jit(solution)/shard_map/ppermute | solution.py:40
  89.0 4.3 %collective-permute-start.30 = (bf16[64,16512]{1,0:T(8,128)(2,1)S(1)}, bf16[64,16512]{1,0:T(8,128)(2,1)S(1)}, u32[]{:S(2)}, u32[]{:S(2)}) collective-permute-start(bf16[64,16512]{1,0:T(8,128)(2,1)S(1)} %get-tuple-element.89.refs_2_), channel_id=1, source_target_pairs={{0,8},{8,0},{16,24},{24,16},{32,40},{40,32},{48,56},{56,48},{64,72... | collective-permute-start | bytes 6340616 | tf_op jit(solution)/shard_map/ppermute | solution.py:40
  91.8 4.6 %collective-permute-start.29 = (bf16[64,16512]{1,0:T(8,128)(2,1)S(1)}, bf16[64,16512]{1,0:T(8,128)(2,1)S(1)}, u32[]{:S(2)}, u32[]{:S(2)}) collective-permute-start(bf16[64,16512]{1,0:T(8,128)(2,1)S(1)} %get-tuple-element.92.refs_0_), channel_id=1, source_target_pairs={{0,8},{8,0},{16,24},{24,16},{32,40},{40,32},{48,56},{56,48},{64,72... | collective-permute-start | bytes 6340616 | tf_op jit(solution)/shard_map/ppermute | solution.py:40

commit v4 on v3

--- a/solution.py
+++ b/solution.py
@@ -29,9 +29,9 @@
 )
 
 PLAN = (
-    "z2", "m2", "z6", "z4", "g1", "g0", "g1", "g0", "m4", "g3", "m5", "g2", "g3", "g5", "g4",
-    "g0", "g2", "g3", "g4", "g1", "g5", "k0", "k2o0", "k5o2", "k3o5", "k4o3r20", "k1o4r35",
-    "o1r4", "r1",
+    "z2", "m2", "z6", "z4", "g1", "g0", "g1", "g0", "m4", "g3", "m5", "g3", "g2", "g5", "g4",
+    "g2", "g0", "g3", "g1", "g4", "g5", "k0", "k2o0", "k5o2", "k3o5", "k1o3r02", "k4o1r53",
+    "o4r1", "r4",
 )
 
 

time: 98.9 us -> 94.9 us (0.960)
  starting transfers between devices: 59 us -> 56.4 us
  waiting for transfers between devices: 19.9 us -> 18.2 us
    ppermute x28, starting transfers between devices: 53.7 us -> 52 us  [swapped(): return lax.ppermute(value, axis, pairs)]
    ppermute x28, waiting for transfers between devices: 19.2 us -> 18.2 us  [swapped(): return lax.ppermute(value, axis, pairs)]
  transfers between devices with their start and end apart: 31 -> 31, of which waited for: 13 -> 13; matrix products, arithmetic and copies ran while one was open for 1% -> 1% of each run, Pallas kernels for 13% -> 14%
where the time goes in v4:
time: 94.9 us; the launch traced here: 94.6 us
  starting transfers between devices  56.4 us (59%)
  waiting for transfers between devices  18.2 us (19%)
  Pallas kernels  16.9 us (18%)
  local copies, waits for them, and re-layouts  1.44 us (2%)
    ppermute x28, starting transfers between devices, swapped(): return lax.ppermute(value, axis, pairs)  52 us
    ppermute x28, waiting for transfers between devices, swapped(): return lax.ppermute(value, axis, pairs)  18.2 us
    pallas_call x8, Pallas kernels, codes_call(): pl.pallas_call(functools.partial(codes_kernel, order, norm, stored, half,...  15.6 us
    ppermute x3, starting transfers between devices, from_neighbours(): lax.ppermute(value, ('col', 'row'), pairs)  4.41 us
  transfers between devices with their start and end apart: 31, of which 13 were waited for; matrix products, arithmetic and copies ran while one was open for 1% of the time, Pallas kernels for 14%

profile of v4, /device:TPU:1, one launch (start us, length us, event | category | flops | bytes accessed | tf_op | source)
XLA Modules:
  0.0 94.6 jit_solution(6130781074930587722)
XLA Ops:
  0.7 1.3 %constant_dynamic-slice_fusion = (bf16[8,32,1024]{2,1,0:T(8,128)(2,1)S(1)}, bf16[8,32,1024]{2,1,0:T(8,128)(2,1)S(1)}) fusion(bf16[8,64,1024]{2,1,0:T(8,128)(2,1)} %bitcast.17, s32[]{:T(128)S(6)} %select_n.20, s32[]{:T(128)S(6)} %select_n.19), kind=kLoop, calls=%fused_computation.19 | loop fusion | bytes 2097160 | tf_op jit(solution)/shard_map/dynamic_slice | solution.py:272
  2.0 1.5 %collective-permute-start = (bf16[8,32,1024]{2,1,0:T(8,128)(2,1)S(1)}, bf16[8,32,1024]{2,1,0:T(8,128)(2,1)S(1)}, u32[]{:S(2)}, u32[]{:S(2)}) collective-permute-start(bf16[8,32,1024]{2,1,0:T(8,128)(2,1)S(1)} %get-tuple-element.115), channel_id=1, source_target_pairs={{0,8},{8,0},{16,24},{24,16},{32,40},{40,32},{48,56},{56,48},{64,72... | collective-permute-start | bytes 1572872 | tf_op jit(solution)/shard_map/ppermute | solution.py:40
  3.5 1.5 %collective-permute-done.got_ref = bf16[8,32,1024]{2,1,0:T(8,128)(2,1)S(1)} collective-permute-done((bf16[8,32,1024]{2,1,0:T(8,128)(2,1)S(1)}, bf16[8,32,1024]{2,1,0:T(8,128)(2,1)S(1)}, u32[]{:S(2)}, u32[]{:S(2)}) %collective-permute-start) | collective-permute-done | bytes 524320 | tf_op jit(solution)/shard_map/ppermute | solution.py:40
  5.0 1.3 %first_rotation.1 = bf16[8,32,2048]{2,1,0:T(8,128)(2,1)S(1)} custom-call(s32[3]{0:T(128)S(1)} %pad_add_fusion.where_ref, bf16[8,32,1024]{2,1,0:T(8,128)(2,1)S(1)} %get-tuple-element.116.own_ref, bf16[8,32,1024]{2,1,0:T(8,128)(2,1)S(1)} %collective-permute-done.got_ref), custom_call_target="tpu_custom_call" | custom-call | flops 20000000000 | bytes 1 | tf_op jit(solution)/shard_map/first_rotation/pallas_call | solution.py:102
  6.4 3.9 %collective-permute-start.2 = (bf16[2,32,2048]{2,1,0:T(8,128)(2,1)S(1)}, bf16[2,32,2048]{2,1,0:T(8,128)(2,1)S(1)}, u32[]{:S(2)}, u32[]{:S(2)}) collective-permute-start(bf16[2,32,2048]{2,1,0:T(8,128)(2,1)S(1)} %get-tuple-element.58), channel_id=1, source_target_pairs={{0,6},{1,7},{2,4},{3,5},{4,2},{5,3},{6,0},{7,1},{8,14},{9,15},{10,... | collective-permute-start | bytes 786440 | tf_op jit(solution)/shard_map/ppermute | solution.py:40
  10.3 1.3 %collective-permute-start.10 = (bf16[1,32,2048]{2,1,0:T(8,128)(2,1)S(1)}, bf16[1,32,2048]{2,1,0:T(8,128)(2,1)S(1)}, u32[]{:S(2)}, u32[]{:S(2)}) collective-permute-start(bf16[1,32,2048]{2,1,0:T(8,128)(2,1)S(1)} %get-tuple-element.57), channel_id=1, source_target_pairs={{0,1},{1,0},{2,3},{3,2},{4,5},{5,4},{6,7},{7,6},{8,9},{9,8},{10,11... | collective-permute-start | bytes 393224 | tf_op jit(solution)/shard_map/ppermute | solution.py:40
  11.6 1.9 %collective-permute-start.11 = (bf16[1,32,2048]{2,1,0:T(8,128)(2,1)S(1)}, bf16[1,32,2048]{2,1,0:T(8,128)(2,1)S(1)}, u32[]{:S(2)}, u32[]{:S(2)}) collective-permute-start(bf16[1,32,2048]{2,1,0:T(8,128)(2,1)S(1)} %get-tuple-element.57), channel_id=1, source_target_pairs={{0,65},{1,64},{2,67},{3,66},{4,69},{5,68},{6,71},{7,70},{8,73},{9,... | collective-permute-start | bytes 393224 | tf_op jit(solution)/shard_map/ppermute | solution.py:47
  13.5 1.3 %collective-permute-start.7 = (bf16[2,32,2048]{2,1,0:T(8,128)(2,1)S(1)}, bf16[2,32,2048]{2,1,0:T(8,128)(2,1)S(1)}, u32[]{:S(2)}, u32[]{:S(2)}) collective-permute-start(bf16[2,32,2048]{2,1,0:T(8,128)(2,1)S(1)} %get-tuple-element.59), channel_id=1, source_target_pairs={{0,4},{1,5},{2,6},{3,7},{4,0},{5,1},{6,2},{7,3},{8,12},{9,13},{10,... | collective-permute-start | bytes 786440 | tf_op jit(solution)/shard_map/ppermute | solution.py:40
  14.8 1.9 %collective-permute-done.2 = bf16[2,32,2048]{2,1,0:T(8,128)(2,1)S(1)} collective-permute-done((bf16[2,32,2048]{2,1,0:T(8,128)(2,1)S(1)}, bf16[2,32,2048]{2,1,0:T(8,128)(2,1)S(1)}, u32[]{:S(2)}, u32[]{:S(2)}) %collective-permute-start.2) | collective-permute-done | bytes 262176 | tf_op jit(solution)/shard_map/ppermute | solution.py:40
  17.6 2.6 %collective-permute-start.4 = (bf16[1,64,2048]{2,1,0:T(8,128)(2,1)S(1)}, bf16[1,64,2048]{2,1,0:T(8,128)(2,1)S(1)}, u32[]{:S(2)}, u32[]{:S(2)}) collective-permute-start(bf16[1,64,2048]{2,1,0:T(8,128)(2,1)S(1)} %get-tuple-element.60), channel_id=1, source_target_pairs={{0,48},{8,56},{16,32},{24,40},{32,16},{40,24},{48,0},{56,8},{64,11... | collective-permute-start | bytes 786440 | tf_op jit(solution)/shard_map/ppermute | solution.py:40
  20.1 2.9 %collective-permute-done.7 = bf16[2,32,2048]{2,1,0:T(8,128)(2,1)S(1)} collective-permute-done((bf16[2,32,2048]{2,1,0:T(8,128)(2,1)S(1)}, bf16[2,32,2048]{2,1,0:T(8,128)(2,1)S(1)}, u32[]{:S(2)}, u32[]{:S(2)}) %collective-permute-start.7) | collective-permute-done | bytes 262176 | tf_op jit(solution)/shard_map/ppermute | solution.py:40
  24.6 1.5 %collective-permute-start.8 = (bf16[1,32,2048]{2,1,0:T(8,128)(2,1)S(1)}, bf16[1,32,2048]{2,1,0:T(8,128)(2,1)S(1)}, u32[]{:S(2)}, u32[]{:S(2)}) collective-permute-start(bf16[1,32,2048]{2,1,0:T(8,128)(2,1)S(1)} %get-tuple-element.66), channel_id=1, source_target_pairs={{0,1},{1,0},{2,3},{3,2},{4,5},{5,4},{6,7},{7,6},{8,9},{9,8},{10,11... | collective-permute-start | bytes 393224 | tf_op jit(solution)/shard_map/ppermute | solution.py:40
  26.1 1.9 %collective-permute-start.9 = (bf16[1,32,2048]{2,1,0:T(8,128)(2,1)S(1)}, bf16[1,32,2048]{2,1,0:T(8,128)(2,1)S(1)}, u32[]{:S(2)}, u32[]{:S(2)}) collective-permute-start(bf16[1,32,2048]{2,1,0:T(8,128)(2,1)S(1)} %get-tuple-element.66), channel_id=1, source_target_pairs={{0,65},{1,64},{2,67},{3,66},{4,69},{5,68},{6,71},{7,70},{8,73},{9,... | collective-permute-start | bytes 393224 | tf_op jit(solution)/shard_map/ppermute | solution.py:47
  29.0 2.1 %collective-permute-start.16 = (bf16[2,32,2048]{2,1,0:T(8,128)(2,1)S(1)}, bf16[2,32,2048]{2,1,0:T(8,128)(2,1)S(1)}, u32[]{:S(2)}, u32[]{:S(2)}) collective-permute-start(bf16[2,32,2048]{2,1,0:T(8,128)(2,1)S(1)} %pad_maximum_fusion.8), channel_id=1, source_target_pairs={{0,48},{8,56},{16,32},{24,40},{32,16},{40,24},{48,0},{56,8},{64,11... | collective-permute-start | bytes 786440 | tf_op jit(solution)/shard_map/ppermute | solution.py:40
  33.2 1.5 %collective-permute-done.5 = bf16[1,64,2048]{2,1,0:T(8,128)(2,1)S(1)} collective-permute-done((bf16[1,64,2048]{2,1,0:T(8,128)(2,1)S(1)}, bf16[1,64,2048]{2,1,0:T(8,128)(2,1)S(1)}, u32[]{:S(2)}, u32[]{:S(2)}) %collective-permute-start.5) | collective-permute-done | bytes 262176 | tf_op jit(solution)/shard_map/ppermute | solution.py:40
  35.9 3.1 %collective-permute-start.13 = (bf16[2,64,2048]{2,1,0:T(8,128)(2,1)S(1)}, bf16[2,64,2048]{2,1,0:T(8,128)(2,1)S(1)}, u32[]{:S(2)}, u32[]{:S(2)}) collective-permute-start(bf16[2,64,2048]{2,1,0:T(8,128)(2,1)S(1)} %pad_maximum_fusion.3), channel_id=1, source_target_pairs={{0,48},{8,56},{16,32},{24,40},{32,16},{40,24},{48,0},{56,8},{64,11... | collective-permute-start | bytes 1572872 | tf_op jit(solution)/shard_map/ppermute | solution.py:40
  39.2 2.7 %collective-permute-done.15 = bf16[2,32,2048]{2,1,0:T(8,128)(2,1)S(1)} collective-permute-done((bf16[2,32,2048]{2,1,0:T(8,128)(2,1)S(1)}, bf16[2,32,2048]{2,1,0:T(8,128)(2,1)S(1)}, u32[]{:S(2)}, u32[]{:S(2)}) %collective-permute-start.15) | collective-permute-done | bytes 262176 | tf_op jit(solution)/shard_map/ppermute | solution.py:40
  41.9 1.6 %collective-permute-start.24 = (bf16[4,32,2048]{2,1,0:T(8,128)(2,1)S(1)}, bf16[4,32,2048]{2,1,0:T(8,128)(2,1)S(1)}, u32[]{:S(2)}, u32[]{:S(2)}) collective-permute-start(bf16[4,32,2048]{2,1,0:T(8,128)(2,1)S(1)} %pad_maximum_fusion.5.refs_0_), channel_id=1, source_target_pairs={{0,64},{8,72},{16,80},{24,88},{32,96},{40,104},{48,112},{56,120},{... | collective-permute-start | bytes 1572872 | tf_op jit(solution)/shard_map/ppermute | solution.py:40
  43.6 1.3 %collective-permute-done.21 = bf16[2,32,2048]{2,1,0:T(8,128)(2,1)S(1)} collective-permute-done((bf16[2,32,2048]{2,1,0:T(8,128)(2,1)S(1)}, bf16[2,32,2048]{2,1,0:T(8,128)(2,1)S(1)}, u32[]{:S(2)}, u32[]{:S(2)}) %collective-permute-start.21) | collective-permute-done | bytes 262176 | tf_op jit(solution)/shard_map/ppermute | solution.py:40
  45.0 1.6 %collective-permute-start.20 = (bf16[4,32,2048]{2,1,0:T(8,128)(2,1)S(1)}, bf16[4,32,2048]{2,1,0:T(8,128)(2,1)S(1)}, u32[]{:S(2)}, u32[]{:S(2)}) collective-permute-start(bf16[4,32,2048]{2,1,0:T(8,128)(2,1)S(1)} %pad_maximum_fusion.4.refs_0_), channel_id=1, source_target_pairs={{0,48},{8,56},{16,32},{24,40},{32,16},{40,24},{48,0},{56,8},{64,11... | collective-permute-start | bytes 1572872 | tf_op jit(solution)/shard_map/ppermute | solution.py:40
  46.7 3.1 %collective-permute-start.19 = (bf16[4,64,2048]{2,1,0:T(8,128)(2,1)S(1)}, bf16[4,64,2048]{2,1,0:T(8,128)(2,1)S(1)}, u32[]{:S(2)}, u32[]{:S(2)}) collective-permute-start(bf16[4,64,2048]{2,1,0:T(8,128)(2,1)S(1)} %pad_maximum_fusion.1.refs_0_), channel_id=1, source_target_pairs={{0,64},{8,72},{16,80},{24,88},{32,96},{40,104},{48,112},{56,120},{... | collective-permute-start | bytes 3145736 | tf_op jit(solution)/shard_map/ppermute | solution.py:40
  51.3 2.4 %collective-permute-done.24.refs_1_ = bf16[4,32,2048]{2,1,0:T(8,128)(2,1)S(1)} collective-permute-done((bf16[4,32,2048]{2,1,0:T(8,128)(2,1)S(1)}, bf16[4,32,2048]{2,1,0:T(8,128)(2,1)S(1)}, u32[]{:S(2)}, u32[]{:S(2)}) %collective-permute-start.24) | collective-permute-done | bytes 524320 | tf_op jit(solution)/shard_map/ppermute | solution.py:40
  53.8 1.5 %collective-permute-start.22 = (bf16[4,32,2048]{2,1,0:T(8,128)(2,1)S(1)}, bf16[4,32,2048]{2,1,0:T(8,128)(2,1)S(1)}, u32[]{:S(2)}, u32[]{:S(2)}) collective-permute-start(bf16[4,32,2048]{2,1,0:T(8,128)(2,1)S(1)} %pad_maximum_fusion.7.refs_0_), channel_id=1, source_target_pairs={{0,48},{8,56},{16,32},{24,40},{32,16},{40,24},{48,0},{56,8},{64,11... | collective-permute-start | bytes 1572872 | tf_op jit(solution)/shard_map/ppermute | solution.py:40
  56.4 13.7 %collective-permute-start.25 = (bf16[32,16512]{1,0:T(8,128)(2,1)S(1)}, bf16[32,16512]{1,0:T(8,128)(2,1)S(1)}, u32[]{:S(2)}, u32[]{:S(2)}) collective-permute-start(bf16[32,16512]{1,0:T(8,128)(2,1)S(1)} %get-tuple-element.78.refs_2_), channel_id=1, source_target_pairs={{0,8},{8,0},{16,24},{24,16},{32,40},{40,32},{48,56},{56,48},{64,72... | collective-permute-start | bytes 3170312 | tf_op jit(solution)/shard_map/ppermute | solution.py:40
  70.1 1.5 %rotate1_store1.3 = (bf16[32,16512]{1,0:T(8,128)(2,1)S(1)}, f32[32,128]{1,0:T(8,128)S(1)}, bf16[512,16384]{1,0:T(8,128)(2,1)}) custom-call(s32[3]{0:T(128)S(1)} %pad_add_fusion.where_ref, bf16[4,32,2048]{2,1,0:T(8,128)(2,1)S(1)} %pad_maximum_fusion.6.refs_0_, bf16[4,32,2048]{2,1,0:T(8,128)(2,1)S(1)} %collective-permute-done.23.refs_1_, ...), custom_call_target="tpu_custom_call" | custom-call | flops 20000000000 | bytes 1 | tf_op jit(solution)/shard_map/rotate1_store1/pallas_call | solution.py:247
  72.1 6.4 %collective-permute-start.26 = (bf16[32,16512]{1,0:T(8,128)(2,1)S(1)}, bf16[32,16512]{1,0:T(8,128)(2,1)S(1)}, u32[]{:S(2)}, u32[]{:S(2)}) collective-permute-start(bf16[32,16512]{1,0:T(8,128)(2,1)S(1)} %get-tuple-element.80.refs_2_), channel_id=1, source_target_pairs={{0,8},{8,0},{16,24},{24,16},{32,40},{40,32},{48,56},{56,48},{64,72... | collective-permute-start | bytes 3170312 | tf_op jit(solution)/shard_map/ppermute | solution.py:40
  78.5 1.5 %rotate1_store1.4 = (bf16[32,16512]{1,0:T(8,128)(2,1)S(1)}, f32[32,128]{1,0:T(8,128)S(1)}, bf16[512,16384]{1,0:T(8,128)(2,1)}) custom-call(s32[3]{0:T(128)S(1)} %pad_add_fusion.where_ref, bf16[4,32,2048]{2,1,0:T(8,128)(2,1)S(1)} %pad_maximum_fusion.7.refs_0_, ...), custom_call_target="tpu_custom_call", output_to_operand_aliasing={{2}: (4, {})} | custom-call | flops 20000000000 | bytes 1 | tf_op jit(solution)/shard_map/rotate1_store1/pallas_call | solution.py:247
  80.1 1.5 %rotate1_store1.5 = (bf16[32,16512]{1,0:T(8,128)(2,1)S(1)}, f32[32,128]{1,0:T(8,128)S(1)}, bf16[512,16384]{1,0:T(8,128)(2,1)}) custom-call(s32[3]{0:T(128)S(1)} %pad_add_fusion.where_ref, bf16[4,32,2048]{2,1,0:T(8,128)(2,1)S(1)} %pad_maximum_fusion.4.refs_0_, ...), custom_call_target="tpu_custom_call", output_to_operand_aliasing={{2}: (4, {})} | custom-call | flops 20000000000 | bytes 1 | tf_op jit(solution)/shard_map/rotate1_store1/pallas_call | solution.py:247
  82.6 2.2 %rotate2_store3.1 = (bf16[64,16512]{1,0:T(8,128)(2,1)S(1)}, f32[64,128]{1,0:T(8,128)S(1)}, bf16[512,16384]{1,0:T(8,128)(2,1)}, f32[32,128]{1,0:T(8,128)S(1)}, f32[32,128]{1,0:T(8,128)S(1)}) custom-call(s32[3]{0:T(128)S(1)} %pad_add_fusion.where_ref, bf16[4,64,2048]{2,1,0:T(8,128)(2,1)S(1)} %pad_maximum_fusion.1.refs_0_, ...), custom_call_target="tpu_custom_call", output_to_operand_aliasing={{2}: (6, {})} | custom-call | flops 20000000000 | bytes 1 | tf_op jit(solution)/shard_map/rotate2_store3/pallas_call | solution.py:247
  84.9 2.6 %rotate2_store4.1 = (bf16[64,16512]{1,0:T(8,128)(2,1)S(1)}, f32[64,128]{1,0:T(8,128)S(1)}, bf16[512,16384]{1,0:T(8,128)(2,1)}, f32[32,128]{1,0:T(8,128)S(1)}, f32[32,128]{1,0:T(8,128)S(1)}) custom-call(s32[3]{0:T(128)S(1)} %pad_add_fusion.where_ref, bf16[4,64,2048]{2,1,0:T(8,128)(2,1)S(1)} %pad_maximum_fusion.refs_0_, ...), custom_call_target="tpu_custom_call", output_to_operand_aliasing={{2}: (6, {})} | custom-call | flops 20000000000 | bytes 1 | tf_op jit(solution)/shard_map/rotate2_store4/pallas_call | solution.py:247
  89.1 2.6 %rotate0_store4.1 = (bf16[512,16384]{1,0:T(8,128)(2,1)}, f32[64,128]{1,0:T(8,128)S(1)}) custom-call(s32[3]{0:T(128)S(1)} %pad_add_fusion.where_ref, bf16[64,16512]{1,0:T(8,128)(2,1)S(1)} %get-tuple-element.92.refs_0_, bf16[64,16512]{1,0:T(8,128)(2,1)S(1)} %collective-permute-done.30.refs_1_, ...), custom_call_target="tpu_custom_call", output_to_operand_aliasing={{0}: (3, {})} | custom-call | flops 20000000000 | bytes 1 | tf_op jit(solution)/shard_map/rotate0_store4/pallas_call | solution.py:247
  92.1 2.5 %rotate0_store2.1 = (bf16[512,16384]{1,0:T(8,128)(2,1)}, f32[4,128]{1,0:T(4,128)}) custom-call(s32[3]{0:T(128)S(1)} %pad_add_fusion.where_ref, bf16[64,16512]{1,0:T(8,128)(2,1)S(1)} %collective-permute-done.29.refs_0_, f32[32,128]{1,0:T(8,128)S(1)} %get-tuple-element.94.refs_1_, ...), custom_call_target="tpu_custom_call", output_to_operand_aliasing={{0}: (13, {})} | custom-call | flops 20000000000 | bytes 1 | tf_op jit(solution)/shard_map/rotate0_store2/pallas_call | solution.py:247
  (59 shorter events, 13.4 us)
Async XLA Ops:
  2.0 3.0 %collective-permute-start = (bf16[8,32,1024]{2,1,0:T(8,128)(2,1)S(1)}, bf16[8,32,1024]{2,1,0:T(8,128)(2,1)S(1)}, u32[]{:S(2)}, u32[]{:S(2)}) collective-permute-start(bf16[8,32,1024]{2,1,0:T(8,128)(2,1)S(1)} %get-tuple-element.115), channel_id=1, source_target_pairs={{0,8},{8,0},{16,24},{24,16},{32,40},{40,32},{48,56},{56,48},{64,72... | collective-permute-start | bytes 1572872 | tf_op jit(solution)/shard_map/ppermute | solution.py:40
  6.4 10.3 %collective-permute-start.2 = (bf16[2,32,2048]{2,1,0:T(8,128)(2,1)S(1)}, bf16[2,32,2048]{2,1,0:T(8,128)(2,1)S(1)}, u32[]{:S(2)}, u32[]{:S(2)}) collective-permute-start(bf16[2,32,2048]{2,1,0:T(8,128)(2,1)S(1)} %get-tuple-element.58), channel_id=1, source_target_pairs={{0,6},{1,7},{2,4},{3,5},{4,2},{5,3},{6,0},{7,1},{8,14},{9,15},{10,... | collective-permute-start | bytes 786440 | tf_op jit(solution)/shard_map/ppermute | solution.py:40
  10.3 7.2 %collective-permute-start.1 = (bf16[2,32,2048]{2,1,0:T(8,128)(2,1)S(1)}, bf16[2,32,2048]{2,1,0:T(8,128)(2,1)S(1)}, u32[]{:S(2)}, u32[]{:S(2)}) collective-permute-start(bf16[2,32,2048]{2,1,0:T(8,128)(2,1)S(1)} %get-tuple-element.56), channel_id=1, source_target_pairs={{0,2},{1,3},{2,0},{3,1},{4,6},{5,7},{6,4},{7,5},{8,10},{9,11},{10,... | collective-permute-start | bytes 786440 | tf_op jit(solution)/shard_map/ppermute | solution.py:40
  10.3 14.2 %collective-permute-start.10 = (bf16[1,32,2048]{2,1,0:T(8,128)(2,1)S(1)}, bf16[1,32,2048]{2,1,0:T(8,128)(2,1)S(1)}, u32[]{:S(2)}, u32[]{:S(2)}) collective-permute-start(bf16[1,32,2048]{2,1,0:T(8,128)(2,1)S(1)} %get-tuple-element.57), channel_id=1, source_target_pairs={{0,1},{1,0},{2,3},{3,2},{4,5},{5,4},{6,7},{7,6},{8,9},{9,8},{10,11... | collective-permute-start | bytes 393224 | tf_op jit(solution)/shard_map/ppermute | solution.py:40
  11.6 12.9 %collective-permute-start.11 = (bf16[1,32,2048]{2,1,0:T(8,128)(2,1)S(1)}, bf16[1,32,2048]{2,1,0:T(8,128)(2,1)S(1)}, u32[]{:S(2)}, u32[]{:S(2)}) collective-permute-start(bf16[1,32,2048]{2,1,0:T(8,128)(2,1)S(1)} %get-tuple-element.57), channel_id=1, source_target_pairs={{0,65},{1,64},{2,67},{3,66},{4,69},{5,68},{6,71},{7,70},{8,73},{9,... | collective-permute-start | bytes 393224 | tf_op jit(solution)/shard_map/ppermute | solution.py:47
  13.5 9.5 %collective-permute-start.7 = (bf16[2,32,2048]{2,1,0:T(8,128)(2,1)S(1)}, bf16[2,32,2048]{2,1,0:T(8,128)(2,1)S(1)}, u32[]{:S(2)}, u32[]{:S(2)}) collective-permute-start(bf16[2,32,2048]{2,1,0:T(8,128)(2,1)S(1)} %get-tuple-element.59), channel_id=1, source_target_pairs={{0,4},{1,5},{2,6},{3,7},{4,0},{5,1},{6,2},{7,3},{8,12},{9,13},{10,... | collective-permute-start | bytes 786440 | tf_op jit(solution)/shard_map/ppermute | solution.py:40
  17.6 6.5 %collective-permute-start.4 = (bf16[1,64,2048]{2,1,0:T(8,128)(2,1)S(1)}, bf16[1,64,2048]{2,1,0:T(8,128)(2,1)S(1)}, u32[]{:S(2)}, u32[]{:S(2)}) collective-permute-start(bf16[1,64,2048]{2,1,0:T(8,128)(2,1)S(1)} %get-tuple-element.60), channel_id=1, source_target_pairs={{0,48},{8,56},{16,32},{24,40},{32,16},{40,24},{48,0},{56,8},{64,11... | collective-permute-start | bytes 786440 | tf_op jit(solution)/shard_map/ppermute | solution.py:40
  20.1 3.9 %collective-permute-start.3 = (bf16[1,32,2048]{2,1,0:T(8,128)(2,1)S(1)}, bf16[1,32,2048]{2,1,0:T(8,128)(2,1)S(1)}, u32[]{:S(2)}, u32[]{:S(2)}) collective-permute-start(bf16[1,32,2048]{2,1,0:T(8,128)(2,1)S(1)} %get-tuple-element.61), channel_id=1, source_target_pairs={{0,16},{8,24},{16,0},{24,8},{32,48},{40,56},{48,32},{56,40},{64,80... | collective-permute-start | bytes 393224 | tf_op jit(solution)/shard_map/ppermute | solution.py:40
  24.2 4.8 %collective-permute-start.12 = (bf16[1,32,2048]{2,1,0:T(8,128)(2,1)S(1)}, bf16[1,32,2048]{2,1,0:T(8,128)(2,1)S(1)}, u32[]{:S(2)}, u32[]{:S(2)}) collective-permute-start(bf16[1,32,2048]{2,1,0:T(8,128)(2,1)S(1)} %get-tuple-element.65), channel_id=1, source_target_pairs={{0,16},{8,24},{16,0},{24,8},{32,48},{40,56},{48,32},{56,40},{64,80... | collective-permute-start | bytes 393224 | tf_op jit(solution)/shard_map/ppermute | solution.py:40
  24.6 6.5 %collective-permute-start.8 = (bf16[1,32,2048]{2,1,0:T(8,128)(2,1)S(1)}, bf16[1,32,2048]{2,1,0:T(8,128)(2,1)S(1)}, u32[]{:S(2)}, u32[]{:S(2)}) collective-permute-start(bf16[1,32,2048]{2,1,0:T(8,128)(2,1)S(1)} %get-tuple-element.66), channel_id=1, source_target_pairs={{0,1},{1,0},{2,3},{3,2},{4,5},{5,4},{6,7},{7,6},{8,9},{9,8},{10,11... | collective-permute-start | bytes 393224 | tf_op jit(solution)/shard_map/ppermute | solution.py:40
  26.1 5.9 %collective-permute-start.9 = (bf16[1,32,2048]{2,1,0:T(8,128)(2,1)S(1)}, bf16[1,32,2048]{2,1,0:T(8,128)(2,1)S(1)}, u32[]{:S(2)}, u32[]{:S(2)}) collective-permute-start(bf16[1,32,2048]{2,1,0:T(8,128)(2,1)S(1)} %get-tuple-element.66), channel_id=1, source_target_pairs={{0,65},{1,64},{2,67},{3,66},{4,69},{5,68},{6,71},{7,70},{8,73},{9,... | collective-permute-start | bytes 393224 | tf_op jit(solution)/shard_map/ppermute | solution.py:47
  28.0 6.7 %collective-permute-start.5 = (bf16[1,64,2048]{2,1,0:T(8,128)(2,1)S(1)}, bf16[1,64,2048]{2,1,0:T(8,128)(2,1)S(1)}, u32[]{:S(2)}, u32[]{:S(2)}) collective-permute-start(bf16[1,64,2048]{2,1,0:T(8,128)(2,1)S(1)} %get-tuple-element.64), channel_id=1, source_target_pairs={{0,1},{1,0},{2,3},{3,2},{4,5},{5,4},{6,7},{7,6},{8,9},{9,8},{10,11... | collective-permute-start | bytes 786440 | tf_op jit(solution)/shard_map/ppermute | solution.py:40
  28.4 6.8 %collective-permute-start.6 = (bf16[1,64,2048]{2,1,0:T(8,128)(2,1)S(1)}, bf16[1,64,2048]{2,1,0:T(8,128)(2,1)S(1)}, u32[]{:S(2)}, u32[]{:S(2)}) collective-permute-start(bf16[1,64,2048]{2,1,0:T(8,128)(2,1)S(1)} %get-tuple-element.64), channel_id=1, source_target_pairs={{0,65},{1,64},{2,67},{3,66},{4,69},{5,68},{6,71},{7,70},{8,73},{9,... | collective-permute-start | bytes 786440 | tf_op jit(solution)/shard_map/ppermute | solution.py:47
  29.0 6.9 %collective-permute-start.16 = (bf16[2,32,2048]{2,1,0:T(8,128)(2,1)S(1)}, bf16[2,32,2048]{2,1,0:T(8,128)(2,1)S(1)}, u32[]{:S(2)}, u32[]{:S(2)}) collective-permute-start(bf16[2,32,2048]{2,1,0:T(8,128)(2,1)S(1)} %pad_maximum_fusion.8), channel_id=1, source_target_pairs={{0,48},{8,56},{16,32},{24,40},{32,16},{40,24},{48,0},{56,8},{64,11... | collective-permute-start | bytes 786440 | tf_op jit(solution)/shard_map/ppermute | solution.py:40
  31.1 15.5 %collective-permute-start.14 = (bf16[2,64,2048]{2,1,0:T(8,128)(2,1)S(1)}, bf16[2,64,2048]{2,1,0:T(8,128)(2,1)S(1)}, u32[]{:S(2)}, u32[]{:S(2)}) collective-permute-start(bf16[2,64,2048]{2,1,0:T(8,128)(2,1)S(1)} %pad_maximum_fusion.2), channel_id=1, source_target_pairs={{0,16},{8,24},{16,0},{24,8},{32,48},{40,56},{48,32},{56,40},{64,80... | collective-permute-start | bytes 1572872 | tf_op jit(solution)/shard_map/ppermute | solution.py:40
  32.0 7.0 %collective-permute-start.17 = (bf16[2,32,2048]{2,1,0:T(8,128)(2,1)S(1)}, bf16[2,32,2048]{2,1,0:T(8,128)(2,1)S(1)}, u32[]{:S(2)}, u32[]{:S(2)}) collective-permute-start(bf16[2,32,2048]{2,1,0:T(8,128)(2,1)S(1)} %pad_maximum_fusion.10), channel_id=1, source_target_pairs={{0,48},{8,56},{16,32},{24,40},{32,16},{40,24},{48,0},{56,8},{64,11... | collective-permute-start | bytes 786440 | tf_op jit(solution)/shard_map/ppermute | solution.py:40
  34.7 7.2 %collective-permute-start.15 = (bf16[2,32,2048]{2,1,0:T(8,128)(2,1)S(1)}, bf16[2,32,2048]{2,1,0:T(8,128)(2,1)S(1)}, u32[]{:S(2)}, u32[]{:S(2)}) collective-permute-start(bf16[2,32,2048]{2,1,0:T(8,128)(2,1)S(1)} %pad_maximum_fusion.11), channel_id=1, source_target_pairs={{0,64},{8,72},{16,80},{24,88},{32,96},{40,104},{48,112},{56,120},{... | collective-permute-start | bytes 786440 | tf_op jit(solution)/shard_map/ppermute | solution.py:40
  35.2 9.8 %collective-permute-start.21 = (bf16[2,32,2048]{2,1,0:T(8,128)(2,1)S(1)}, bf16[2,32,2048]{2,1,0:T(8,128)(2,1)S(1)}, u32[]{:S(2)}, u32[]{:S(2)}) collective-permute-start(bf16[2,32,2048]{2,1,0:T(8,128)(2,1)S(1)} %pad_maximum_fusion.9), channel_id=1, source_target_pairs={{0,16},{8,24},{16,0},{24,8},{32,48},{40,56},{48,32},{56,40},{64,80... | collective-permute-start | bytes 786440 | tf_op jit(solution)/shard_map/ppermute | solution.py:40
  35.9 14.1 %collective-permute-start.13 = (bf16[2,64,2048]{2,1,0:T(8,128)(2,1)S(1)}, bf16[2,64,2048]{2,1,0:T(8,128)(2,1)S(1)}, u32[]{:S(2)}, u32[]{:S(2)}) collective-permute-start(bf16[2,64,2048]{2,1,0:T(8,128)(2,1)S(1)} %pad_maximum_fusion.3), channel_id=1, source_target_pairs={{0,48},{8,56},{16,32},{24,40},{32,16},{40,24},{48,0},{56,8},{64,11... | collective-permute-start | bytes 1572872 | tf_op jit(solution)/shard_map/ppermute | solution.py:40
  39.1 17.3 %collective-permute-start.23 = (bf16[4,32,2048]{2,1,0:T(8,128)(2,1)S(1)}, bf16[4,32,2048]{2,1,0:T(8,128)(2,1)S(1)}, u32[]{:S(2)}, u32[]{:S(2)}) collective-permute-start(bf16[4,32,2048]{2,1,0:T(8,128)(2,1)S(1)} %pad_maximum_fusion.6.refs_0_), channel_id=1, source_target_pairs={{0,16},{8,24},{16,0},{24,8},{32,48},{40,56},{48,32},{56,40},{64,80... | collective-permute-start | bytes 1572872 | tf_op jit(solution)/shard_map/ppermute | solution.py:40
  41.9 11.8 %collective-permute-start.24 = (bf16[4,32,2048]{2,1,0:T(8,128)(2,1)S(1)}, bf16[4,32,2048]{2,1,0:T(8,128)(2,1)S(1)}, u32[]{:S(2)}, u32[]{:S(2)}) collective-permute-start(bf16[4,32,2048]{2,1,0:T(8,128)(2,1)S(1)} %pad_maximum_fusion.5.refs_0_), channel_id=1, source_target_pairs={{0,64},{8,72},{16,80},{24,88},{32,96},{40,104},{48,112},{56,120},{... | collective-permute-start | bytes 1572872 | tf_op jit(solution)/shard_map/ppermute | solution.py:40
  45.0 35.0 %collective-permute-start.20 = (bf16[4,32,2048]{2,1,0:T(8,128)(2,1)S(1)}, bf16[4,32,2048]{2,1,0:T(8,128)(2,1)S(1)}, u32[]{:S(2)}, u32[]{:S(2)}) collective-permute-start(bf16[4,32,2048]{2,1,0:T(8,128)(2,1)S(1)} %pad_maximum_fusion.4.refs_0_), channel_id=1, source_target_pairs={{0,48},{8,56},{16,32},{24,40},{32,16},{40,24},{48,0},{56,8},{64,11... | collective-permute-start | bytes 1572872 | tf_op jit(solution)/shard_map/ppermute | solution.py:40
  46.7 34.9 %collective-permute-start.19 = (bf16[4,64,2048]{2,1,0:T(8,128)(2,1)S(1)}, bf16[4,64,2048]{2,1,0:T(8,128)(2,1)S(1)}, u32[]{:S(2)}, u32[]{:S(2)}) collective-permute-start(bf16[4,64,2048]{2,1,0:T(8,128)(2,1)S(1)} %pad_maximum_fusion.1.refs_0_), channel_id=1, source_target_pairs={{0,64},{8,72},{16,80},{24,88},{32,96},{40,104},{48,112},{56,120},{... | collective-permute-start | bytes 3145736 | tf_op jit(solution)/shard_map/ppermute | solution.py:40
  50.1 34.8 %collective-permute-start.18 = (bf16[4,64,2048]{2,1,0:T(8,128)(2,1)S(1)}, bf16[4,64,2048]{2,1,0:T(8,128)(2,1)S(1)}, u32[]{:S(2)}, u32[]{:S(2)}) collective-permute-start(bf16[4,64,2048]{2,1,0:T(8,128)(2,1)S(1)} %pad_maximum_fusion.refs_0_), channel_id=1, source_target_pairs={{0,16},{8,24},{16,0},{24,8},{32,48},{40,56},{48,32},{56,40},{64,80... | collective-permute-start | bytes 3145736 | tf_op jit(solution)/shard_map/ppermute | solution.py:40
  53.8 18.3 %collective-permute-start.22 = (bf16[4,32,2048]{2,1,0:T(8,128)(2,1)S(1)}, bf16[4,32,2048]{2,1,0:T(8,128)(2,1)S(1)}, u32[]{:S(2)}, u32[]{:S(2)}) collective-permute-start(bf16[4,32,2048]{2,1,0:T(8,128)(2,1)S(1)} %pad_maximum_fusion.7.refs_0_), channel_id=1, source_target_pairs={{0,48},{8,56},{16,32},{24,40},{32,16},{40,24},{48,0},{56,8},{64,11... | collective-permute-start | bytes 1572872 | tf_op jit(solution)/shard_map/ppermute | solution.py:40
  56.4 26.2 %collective-permute-start.25 = (bf16[32,16512]{1,0:T(8,128)(2,1)S(1)}, bf16[32,16512]{1,0:T(8,128)(2,1)S(1)}, u32[]{:S(2)}, u32[]{:S(2)}) collective-permute-start(bf16[32,16512]{1,0:T(8,128)(2,1)S(1)} %get-tuple-element.78.refs_2_), channel_id=1, source_target_pairs={{0,8},{8,0},{16,24},{24,16},{32,40},{40,32},{48,56},{56,48},{64,72... | collective-permute-start | bytes 3170312 | tf_op jit(solution)/shard_map/ppermute | solution.py:40
  72.1 10.5 %collective-permute-start.26 = (bf16[32,16512]{1,0:T(8,128)(2,1)S(1)}, bf16[32,16512]{1,0:T(8,128)(2,1)S(1)}, u32[]{:S(2)}, u32[]{:S(2)}) collective-permute-start(bf16[32,16512]{1,0:T(8,128)(2,1)S(1)} %get-tuple-element.80.refs_2_), channel_id=1, source_target_pairs={{0,8},{8,0},{16,24},{24,16},{32,40},{40,32},{48,56},{56,48},{64,72... | collective-permute-start | bytes 3170312 | tf_op jit(solution)/shard_map/ppermute | solution.py:40
  80.0 4.9 %collective-permute-start.27 = (bf16[32,16512]{1,0:T(8,128)(2,1)S(1)}, bf16[32,16512]{1,0:T(8,128)(2,1)S(1)}, u32[]{:S(2)}, u32[]{:S(2)}) collective-permute-start(bf16[32,16512]{1,0:T(8,128)(2,1)S(1)} %get-tuple-element.83.refs_2_), channel_id=1, source_target_pairs={{0,8},{8,0},{16,24},{24,16},{32,40},{40,32},{48,56},{56,48},{64,72... | collective-permute-start | bytes 3170312 | tf_op jit(solution)/shard_map/ppermute | solution.py:40
  81.6 3.3 %collective-permute-start.28 = (bf16[32,16512]{1,0:T(8,128)(2,1)S(1)}, bf16[32,16512]{1,0:T(8,128)(2,1)S(1)}, u32[]{:S(2)}, u32[]{:S(2)}) collective-permute-start(bf16[32,16512]{1,0:T(8,128)(2,1)S(1)} %get-tuple-element.86.refs_2_), channel_id=1, source_target_pairs={{0,8},{8,0},{16,24},{24,16},{32,40},{40,32},{48,56},{56,48},{64,72... | collective-permute-start | bytes 3170312 | tf_op jit(solution)/shard_map/ppermute | solution.py:40
  84.8 4.3 %collective-permute-start.30 = (bf16[64,16512]{1,0:T(8,128)(2,1)S(1)}, bf16[64,16512]{1,0:T(8,128)(2,1)S(1)}, u32[]{:S(2)}, u32[]{:S(2)}) collective-permute-start(bf16[64,16512]{1,0:T(8,128)(2,1)S(1)} %get-tuple-element.89.refs_2_), channel_id=1, source_target_pairs={{0,8},{8,0},{16,24},{24,16},{32,40},{40,32},{48,56},{56,48},{64,72... | collective-permute-start | bytes 6340616 | tf_op jit(solution)/shard_map/ppermute | solution.py:40
  87.5 4.6 %collective-permute-start.29 = (bf16[64,16512]{1,0:T(8,128)(2,1)S(1)}, bf16[64,16512]{1,0:T(8,128)(2,1)S(1)}, u32[]{:S(2)}, u32[]{:S(2)}) collective-permute-start(bf16[64,16512]{1,0:T(8,128)(2,1)S(1)} %get-tuple-element.92.refs_0_), channel_id=1, source_target_pairs={{0,8},{8,0},{16,24},{24,16},{32,40},{40,32},{48,56},{56,48},{64,72... | collective-permute-start | bytes 6340616 | tf_op jit(solution)/shard_map/ppermute | solution.py:40

commit v5 on v4

--- a/solution.py
+++ b/solution.py
@@ -193,8 +193,12 @@
     if order:
         rotate(order, norm, where_ref, *inputs, *outputs, *take(1))
     if earlier:
-        (table,) = take(1)
-        for (pieces, side), ref in zip(earlier, scales):
+        (scale_ref,) = got_scale_refs
+        whole_table = scale_ref.shape[0] == 8 * half * 2
+        table = scale_ref if whole_table else take(1)[0]
+        if not whole_table:
+            table[...] = scales[0][...]
+        for (pieces, side), ref in zip(earlier, scales if whole_table else ()):
             for rows, place in places(where_ref, pieces, half, side):
                 table[place, :] = ref[rows, :]
         for pieces, scale in got_scales:
@@ -202,8 +206,7 @@
                 table[place, :] = scale[rows]
         shape = (EXTRA, EXTRA)
         row, lane = (lax.broadcasted_iota(jnp.int32, shape, axis) for axis in range(2))
-        (scale_ref,) = got_scale_refs
-        for q in range(scale_ref.shape[0]):
+        for q in range(0 if whole_table else scale_ref.shape[0]):
             block = table[q * EXTRA : (q + 1) * EXTRA, :]
             line = jnp.sum(jnp.where(row == lane, block, 0.0), axis=0, keepdims=True)
             scale_ref[q : q + 1, :] = line
@@ -241,7 +244,7 @@
         scratch.append(pltpu.SemaphoreType.DMA((sum(len(pieces) for pieces, _ in stored),)))
     heights = [part.shape[0] for part, (_, side) in zip(parts, stored) if side == 1]
     if earlier:
-        heights = [full // EXTRA]
+        heights = [full // EXTRA if len(earlier) == 1 else full]
     out_specs += [whole()] * len(heights)
     out_shape += [jax.ShapeDtypeStruct((height, EXTRA), jnp.float32) for height in heights]
     return pl.pallas_call(
@@ -313,7 +316,7 @@
                     named.append((int(letter), side))
             stored = [(CHUNKS[c][0], side) for c, side in named]
             parts = [(held, got)[side][c] for c, side in named]
-            earlier = dict(scales) if step == PLAN[-1] else {}
+            earlier = dict(scales) if step in PLAN[-2:] else {}
             inputs = ()
             if kind == "k":
                 inputs = (held[i], after(got[i]))
@@ -339,8 +342,11 @@
             if stored:
                 codes, *made = made
                 got_pieces = [pieces_of for pieces_of, side in stored if side == 1]
-                for pieces_of, scale in zip(got_pieces, made):
-                    scales[pieces_of, 1] = scale
+                if earlier:
+                    scales = {"all": made[0]}
+                else:
+                    for pieces_of, scale in zip(got_pieces, made):
+                        scales[pieces_of, 1] = scale
 
     return codes, made[0].reshape(rows)
 

time: 94.9 us -> 94.9 us (level)
  no operation moved by 1% of the time
where the time goes in v5:
time: 94.9 us; the launch traced here: 94.6 us
  starting transfers between devices  56.4 us (59%)
  waiting for transfers between devices  18.2 us (19%)
  Pallas kernels  16.9 us (18%)
  local copies, waits for them, and re-layouts  1.43 us (2%)
    ppermute x28, starting transfers between devices, swapped(): return lax.ppermute(value, axis, pairs)  52 us
    ppermute x28, waiting for transfers between devices, swapped(): return lax.ppermute(value, axis, pairs)  18.2 us
    pallas_call x8, Pallas kernels, codes_call(): pl.pallas_call(functools.partial(codes_kernel, order, norm, stored, half,...  15.6 us
    ppermute x3, starting transfers between devices, from_neighbours(): lax.ppermute(value, ('col', 'row'), pairs)  4.41 us
  transfers between devices with their start and end apart: 31, of which 13 were waited for; matrix products, arithmetic and copies ran while one was open for 1% of the time, Pallas kernels for 14%

profile of v5, /device:TPU:1, one launch (start us, length us, event | category | flops | bytes accessed | tf_op | source)
XLA Modules:
  0.0 94.6 jit_solution(12697956848236333928)
XLA Ops:
  0.7 1.3 %constant_dynamic-slice_fusion = (bf16[8,32,1024]{2,1,0:T(8,128)(2,1)S(1)}, bf16[8,32,1024]{2,1,0:T(8,128)(2,1)S(1)}) fusion(bf16[8,64,1024]{2,1,0:T(8,128)(2,1)} %bitcast.17, s32[]{:T(128)S(6)} %select_n.20, s32[]{:T(128)S(6)} %select_n.19), kind=kLoop, calls=%fused_computation.19 | loop fusion | bytes 2097160 | tf_op jit(solution)/shard_map/dynamic_slice | solution.py:275
  2.0 1.5 %collective-permute-start = (bf16[8,32,1024]{2,1,0:T(8,128)(2,1)S(1)}, bf16[8,32,1024]{2,1,0:T(8,128)(2,1)S(1)}, u32[]{:S(2)}, u32[]{:S(2)}) collective-permute-start(bf16[8,32,1024]{2,1,0:T(8,128)(2,1)S(1)} %get-tuple-element.115), channel_id=1, source_target_pairs={{0,8},{8,0},{16,24},{24,16},{32,40},{40,32},{48,56},{56,48},{64,72... | collective-permute-start | bytes 1572872 | tf_op jit(solution)/shard_map/ppermute | solution.py:40
  3.5 1.5 %collective-permute-done.got_ref = bf16[8,32,1024]{2,1,0:T(8,128)(2,1)S(1)} collective-permute-done((bf16[8,32,1024]{2,1,0:T(8,128)(2,1)S(1)}, bf16[8,32,1024]{2,1,0:T(8,128)(2,1)S(1)}, u32[]{:S(2)}, u32[]{:S(2)}) %collective-permute-start) | collective-permute-done | bytes 524320 | tf_op jit(solution)/shard_map/ppermute | solution.py:40
  5.0 1.3 %first_rotation.1 = bf16[8,32,2048]{2,1,0:T(8,128)(2,1)S(1)} custom-call(s32[3]{0:T(128)S(1)} %pad_add_fusion.where_ref, bf16[8,32,1024]{2,1,0:T(8,128)(2,1)S(1)} %get-tuple-element.116.own_ref, bf16[8,32,1024]{2,1,0:T(8,128)(2,1)S(1)} %collective-permute-done.got_ref), custom_call_target="tpu_custom_call" | custom-call | flops 20000000000 | bytes 1 | tf_op jit(solution)/shard_map/first_rotation/pallas_call | solution.py:102
  6.4 3.9 %collective-permute-start.2 = (bf16[2,32,2048]{2,1,0:T(8,128)(2,1)S(1)}, bf16[2,32,2048]{2,1,0:T(8,128)(2,1)S(1)}, u32[]{:S(2)}, u32[]{:S(2)}) collective-permute-start(bf16[2,32,2048]{2,1,0:T(8,128)(2,1)S(1)} %get-tuple-element.58), channel_id=1, source_target_pairs={{0,6},{1,7},{2,4},{3,5},{4,2},{5,3},{6,0},{7,1},{8,14},{9,15},{10,... | collective-permute-start | bytes 786440 | tf_op jit(solution)/shard_map/ppermute | solution.py:40
  10.3 1.3 %collective-permute-start.10 = (bf16[1,32,2048]{2,1,0:T(8,128)(2,1)S(1)}, bf16[1,32,2048]{2,1,0:T(8,128)(2,1)S(1)}, u32[]{:S(2)}, u32[]{:S(2)}) collective-permute-start(bf16[1,32,2048]{2,1,0:T(8,128)(2,1)S(1)} %get-tuple-element.57), channel_id=1, source_target_pairs={{0,1},{1,0},{2,3},{3,2},{4,5},{5,4},{6,7},{7,6},{8,9},{9,8},{10,11... | collective-permute-start | bytes 393224 | tf_op jit(solution)/shard_map/ppermute | solution.py:40
  11.6 1.9 %collective-permute-start.11 = (bf16[1,32,2048]{2,1,0:T(8,128)(2,1)S(1)}, bf16[1,32,2048]{2,1,0:T(8,128)(2,1)S(1)}, u32[]{:S(2)}, u32[]{:S(2)}) collective-permute-start(bf16[1,32,2048]{2,1,0:T(8,128)(2,1)S(1)} %get-tuple-element.57), channel_id=1, source_target_pairs={{0,65},{1,64},{2,67},{3,66},{4,69},{5,68},{6,71},{7,70},{8,73},{9,... | collective-permute-start | bytes 393224 | tf_op jit(solution)/shard_map/ppermute | solution.py:47
  13.5 1.3 %collective-permute-start.7 = (bf16[2,32,2048]{2,1,0:T(8,128)(2,1)S(1)}, bf16[2,32,2048]{2,1,0:T(8,128)(2,1)S(1)}, u32[]{:S(2)}, u32[]{:S(2)}) collective-permute-start(bf16[2,32,2048]{2,1,0:T(8,128)(2,1)S(1)} %get-tuple-element.59), channel_id=1, source_target_pairs={{0,4},{1,5},{2,6},{3,7},{4,0},{5,1},{6,2},{7,3},{8,12},{9,13},{10,... | collective-permute-start | bytes 786440 | tf_op jit(solution)/shard_map/ppermute | solution.py:40
  14.8 1.9 %collective-permute-done.2 = bf16[2,32,2048]{2,1,0:T(8,128)(2,1)S(1)} collective-permute-done((bf16[2,32,2048]{2,1,0:T(8,128)(2,1)S(1)}, bf16[2,32,2048]{2,1,0:T(8,128)(2,1)S(1)}, u32[]{:S(2)}, u32[]{:S(2)}) %collective-permute-start.2) | collective-permute-done | bytes 262176 | tf_op jit(solution)/shard_map/ppermute | solution.py:40
  17.6 2.6 %collective-permute-start.4 = (bf16[1,64,2048]{2,1,0:T(8,128)(2,1)S(1)}, bf16[1,64,2048]{2,1,0:T(8,128)(2,1)S(1)}, u32[]{:S(2)}, u32[]{:S(2)}) collective-permute-start(bf16[1,64,2048]{2,1,0:T(8,128)(2,1)S(1)} %get-tuple-element.60), channel_id=1, source_target_pairs={{0,48},{8,56},{16,32},{24,40},{32,16},{40,24},{48,0},{56,8},{64,11... | collective-permute-start | bytes 786440 | tf_op jit(solution)/shard_map/ppermute | solution.py:40
  20.1 2.9 %collective-permute-done.7 = bf16[2,32,2048]{2,1,0:T(8,128)(2,1)S(1)} collective-permute-done((bf16[2,32,2048]{2,1,0:T(8,128)(2,1)S(1)}, bf16[2,32,2048]{2,1,0:T(8,128)(2,1)S(1)}, u32[]{:S(2)}, u32[]{:S(2)}) %collective-permute-start.7) | collective-permute-done | bytes 262176 | tf_op jit(solution)/shard_map/ppermute | solution.py:40
  24.6 1.5 %collective-permute-start.8 = (bf16[1,32,2048]{2,1,0:T(8,128)(2,1)S(1)}, bf16[1,32,2048]{2,1,0:T(8,128)(2,1)S(1)}, u32[]{:S(2)}, u32[]{:S(2)}) collective-permute-start(bf16[1,32,2048]{2,1,0:T(8,128)(2,1)S(1)} %get-tuple-element.66), channel_id=1, source_target_pairs={{0,1},{1,0},{2,3},{3,2},{4,5},{5,4},{6,7},{7,6},{8,9},{9,8},{10,11... | collective-permute-start | bytes 393224 | tf_op jit(solution)/shard_map/ppermute | solution.py:40
  26.1 1.9 %collective-permute-start.9 = (bf16[1,32,2048]{2,1,0:T(8,128)(2,1)S(1)}, bf16[1,32,2048]{2,1,0:T(8,128)(2,1)S(1)}, u32[]{:S(2)}, u32[]{:S(2)}) collective-permute-start(bf16[1,32,2048]{2,1,0:T(8,128)(2,1)S(1)} %get-tuple-element.66), channel_id=1, source_target_pairs={{0,65},{1,64},{2,67},{3,66},{4,69},{5,68},{6,71},{7,70},{8,73},{9,... | collective-permute-start | bytes 393224 | tf_op jit(solution)/shard_map/ppermute | solution.py:47
  29.0 2.1 %collective-permute-start.16 = (bf16[2,32,2048]{2,1,0:T(8,128)(2,1)S(1)}, bf16[2,32,2048]{2,1,0:T(8,128)(2,1)S(1)}, u32[]{:S(2)}, u32[]{:S(2)}) collective-permute-start(bf16[2,32,2048]{2,1,0:T(8,128)(2,1)S(1)} %pad_maximum_fusion.8), channel_id=1, source_target_pairs={{0,48},{8,56},{16,32},{24,40},{32,16},{40,24},{48,0},{56,8},{64,11... | collective-permute-start | bytes 786440 | tf_op jit(solution)/shard_map/ppermute | solution.py:40
  33.2 1.5 %collective-permute-done.5 = bf16[1,64,2048]{2,1,0:T(8,128)(2,1)S(1)} collective-permute-done((bf16[1,64,2048]{2,1,0:T(8,128)(2,1)S(1)}, bf16[1,64,2048]{2,1,0:T(8,128)(2,1)S(1)}, u32[]{:S(2)}, u32[]{:S(2)}) %collective-permute-start.5) | collective-permute-done | bytes 262176 | tf_op jit(solution)/shard_map/ppermute | solution.py:40
  35.9 3.1 %collective-permute-start.13 = (bf16[2,64,2048]{2,1,0:T(8,128)(2,1)S(1)}, bf16[2,64,2048]{2,1,0:T(8,128)(2,1)S(1)}, u32[]{:S(2)}, u32[]{:S(2)}) collective-permute-start(bf16[2,64,2048]{2,1,0:T(8,128)(2,1)S(1)} %pad_maximum_fusion.3), channel_id=1, source_target_pairs={{0,48},{8,56},{16,32},{24,40},{32,16},{40,24},{48,0},{56,8},{64,11... | collective-permute-start | bytes 1572872 | tf_op jit(solution)/shard_map/ppermute | solution.py:40
  39.2 2.7 %collective-permute-done.15 = bf16[2,32,2048]{2,1,0:T(8,128)(2,1)S(1)} collective-permute-done((bf16[2,32,2048]{2,1,0:T(8,128)(2,1)S(1)}, bf16[2,32,2048]{2,1,0:T(8,128)(2,1)S(1)}, u32[]{:S(2)}, u32[]{:S(2)}) %collective-permute-start.15) | collective-permute-done | bytes 262176 | tf_op jit(solution)/shard_map/ppermute | solution.py:40
  41.9 1.6 %collective-permute-start.24 = (bf16[4,32,2048]{2,1,0:T(8,128)(2,1)S(1)}, bf16[4,32,2048]{2,1,0:T(8,128)(2,1)S(1)}, u32[]{:S(2)}, u32[]{:S(2)}) collective-permute-start(bf16[4,32,2048]{2,1,0:T(8,128)(2,1)S(1)} %pad_maximum_fusion.5.refs_0_), channel_id=1, source_target_pairs={{0,64},{8,72},{16,80},{24,88},{32,96},{40,104},{48,112},{56,120},{... | collective-permute-start | bytes 1572872 | tf_op jit(solution)/shard_map/ppermute | solution.py:40
  43.6 1.3 %collective-permute-done.21 = bf16[2,32,2048]{2,1,0:T(8,128)(2,1)S(1)} collective-permute-done((bf16[2,32,2048]{2,1,0:T(8,128)(2,1)S(1)}, bf16[2,32,2048]{2,1,0:T(8,128)(2,1)S(1)}, u32[]{:S(2)}, u32[]{:S(2)}) %collective-permute-start.21) | collective-permute-done | bytes 262176 | tf_op jit(solution)/shard_map/ppermute | solution.py:40
  44.9 1.6 %collective-permute-start.20 = (bf16[4,32,2048]{2,1,0:T(8,128)(2,1)S(1)}, bf16[4,32,2048]{2,1,0:T(8,128)(2,1)S(1)}, u32[]{:S(2)}, u32[]{:S(2)}) collective-permute-start(bf16[4,32,2048]{2,1,0:T(8,128)(2,1)S(1)} %pad_maximum_fusion.4.refs_0_), channel_id=1, source_target_pairs={{0,48},{8,56},{16,32},{24,40},{32,16},{40,24},{48,0},{56,8},{64,11... | collective-permute-start | bytes 1572872 | tf_op jit(solution)/shard_map/ppermute | solution.py:40
  46.7 3.1 %collective-permute-start.19 = (bf16[4,64,2048]{2,1,0:T(8,128)(2,1)S(1)}, bf16[4,64,2048]{2,1,0:T(8,128)(2,1)S(1)}, u32[]{:S(2)}, u32[]{:S(2)}) collective-permute-start(bf16[4,64,2048]{2,1,0:T(8,128)(2,1)S(1)} %pad_maximum_fusion.1.refs_0_), channel_id=1, source_target_pairs={{0,64},{8,72},{16,80},{24,88},{32,96},{40,104},{48,112},{56,120},{... | collective-permute-start | bytes 3145736 | tf_op jit(solution)/shard_map/ppermute | solution.py:40
  51.3 2.5 %collective-permute-done.24.refs_1_ = bf16[4,32,2048]{2,1,0:T(8,128)(2,1)S(1)} collective-permute-done((bf16[4,32,2048]{2,1,0:T(8,128)(2,1)S(1)}, bf16[4,32,2048]{2,1,0:T(8,128)(2,1)S(1)}, u32[]{:S(2)}, u32[]{:S(2)}) %collective-permute-start.24) | collective-permute-done | bytes 524320 | tf_op jit(solution)/shard_map/ppermute | solution.py:40
  53.8 1.4 %collective-permute-start.22 = (bf16[4,32,2048]{2,1,0:T(8,128)(2,1)S(1)}, bf16[4,32,2048]{2,1,0:T(8,128)(2,1)S(1)}, u32[]{:S(2)}, u32[]{:S(2)}) collective-permute-start(bf16[4,32,2048]{2,1,0:T(8,128)(2,1)S(1)} %pad_maximum_fusion.7.refs_0_), channel_id=1, source_target_pairs={{0,48},{8,56},{16,32},{24,40},{32,16},{40,24},{48,0},{56,8},{64,11... | collective-permute-start | bytes 1572872 | tf_op jit(solution)/shard_map/ppermute | solution.py:40
  56.4 13.7 %collective-permute-start.25 = (bf16[32,16512]{1,0:T(8,128)(2,1)S(1)}, bf16[32,16512]{1,0:T(8,128)(2,1)S(1)}, u32[]{:S(2)}, u32[]{:S(2)}) collective-permute-start(bf16[32,16512]{1,0:T(8,128)(2,1)S(1)} %get-tuple-element.78.refs_2_), channel_id=1, source_target_pairs={{0,8},{8,0},{16,24},{24,16},{32,40},{40,32},{48,56},{56,48},{64,72... | collective-permute-start | bytes 3170312 | tf_op jit(solution)/shard_map/ppermute | solution.py:40
  70.1 1.5 %rotate1_store1.3 = (bf16[32,16512]{1,0:T(8,128)(2,1)S(1)}, f32[32,128]{1,0:T(8,128)S(1)}, bf16[512,16384]{1,0:T(8,128)(2,1)}) custom-call(s32[3]{0:T(128)S(1)} %pad_add_fusion.where_ref, bf16[4,32,2048]{2,1,0:T(8,128)(2,1)S(1)} %pad_maximum_fusion.6.refs_0_, bf16[4,32,2048]{2,1,0:T(8,128)(2,1)S(1)} %collective-permute-done.23.refs_1_, ...), custom_call_target="tpu_custom_call" | custom-call | flops 20000000000 | bytes 1 | tf_op jit(solution)/shard_map/rotate1_store1/pallas_call | solution.py:250
  72.1 6.3 %collective-permute-start.26 = (bf16[32,16512]{1,0:T(8,128)(2,1)S(1)}, bf16[32,16512]{1,0:T(8,128)(2,1)S(1)}, u32[]{:S(2)}, u32[]{:S(2)}) collective-permute-start(bf16[32,16512]{1,0:T(8,128)(2,1)S(1)} %get-tuple-element.80.refs_2_), channel_id=1, source_target_pairs={{0,8},{8,0},{16,24},{24,16},{32,40},{40,32},{48,56},{56,48},{64,72... | collective-permute-start | bytes 3170312 | tf_op jit(solution)/shard_map/ppermute | solution.py:40
  78.5 1.5 %rotate1_store1.4 = (bf16[32,16512]{1,0:T(8,128)(2,1)S(1)}, f32[32,128]{1,0:T(8,128)S(1)}, bf16[512,16384]{1,0:T(8,128)(2,1)}) custom-call(s32[3]{0:T(128)S(1)} %pad_add_fusion.where_ref, bf16[4,32,2048]{2,1,0:T(8,128)(2,1)S(1)} %pad_maximum_fusion.7.refs_0_, ...), custom_call_target="tpu_custom_call", output_to_operand_aliasing={{2}: (4, {})} | custom-call | flops 20000000000 | bytes 1 | tf_op jit(solution)/shard_map/rotate1_store1/pallas_call | solution.py:250
  80.1 1.5 %rotate1_store1.5 = (bf16[32,16512]{1,0:T(8,128)(2,1)S(1)}, f32[32,128]{1,0:T(8,128)S(1)}, bf16[512,16384]{1,0:T(8,128)(2,1)}) custom-call(s32[3]{0:T(128)S(1)} %pad_add_fusion.where_ref, bf16[4,32,2048]{2,1,0:T(8,128)(2,1)S(1)} %pad_maximum_fusion.4.refs_0_, ...), custom_call_target="tpu_custom_call", output_to_operand_aliasing={{2}: (4, {})} | custom-call | flops 20000000000 | bytes 1 | tf_op jit(solution)/shard_map/rotate1_store1/pallas_call | solution.py:250
  82.6 2.2 %rotate2_store3.1 = (bf16[64,16512]{1,0:T(8,128)(2,1)S(1)}, f32[64,128]{1,0:T(8,128)S(1)}, bf16[512,16384]{1,0:T(8,128)(2,1)}, f32[32,128]{1,0:T(8,128)S(1)}, f32[32,128]{1,0:T(8,128)S(1)}) custom-call(s32[3]{0:T(128)S(1)} %pad_add_fusion.where_ref, bf16[4,64,2048]{2,1,0:T(8,128)(2,1)S(1)} %pad_maximum_fusion.1.refs_0_, ...), custom_call_target="tpu_custom_call", output_to_operand_aliasing={{2}: (6, {})} | custom-call | flops 20000000000 | bytes 1 | tf_op jit(solution)/shard_map/rotate2_store3/pallas_call | solution.py:250
  85.0 2.6 %rotate2_store4.1 = (bf16[64,16512]{1,0:T(8,128)(2,1)S(1)}, f32[64,128]{1,0:T(8,128)S(1)}, bf16[512,16384]{1,0:T(8,128)(2,1)}, f32[32,128]{1,0:T(8,128)S(1)}, f32[32,128]{1,0:T(8,128)S(1)}) custom-call(s32[3]{0:T(128)S(1)} %pad_add_fusion.where_ref, bf16[4,64,2048]{2,1,0:T(8,128)(2,1)S(1)} %pad_maximum_fusion.refs_0_, ...), custom_call_target="tpu_custom_call", output_to_operand_aliasing={{2}: (6, {})} | custom-call | flops 20000000000 | bytes 1 | tf_op jit(solution)/shard_map/rotate2_store4/pallas_call | solution.py:250
  89.1 2.6 %rotate0_store4.1 = (bf16[512,16384]{1,0:T(8,128)(2,1)}, f32[512,128]{1,0:T(8,128)S(1)}) custom-call(s32[3]{0:T(128)S(1)} %pad_add_fusion.where_ref, bf16[64,16512]{1,0:T(8,128)(2,1)S(1)} %get-tuple-element.92.refs_0_, bf16[64,16512]{1,0:T(8,128)(2,1)S(1)} %collective-permute-done.30.refs_1_, ...), custom_call_target="tpu_custom_call", output_to_operand_aliasing={{0}: (13, {})} | custom-call | flops 20000000000 | bytes 1 | tf_op jit(solution)/shard_map/rotate0_store4/pallas_call | solution.py:250
  92.1 2.5 %rotate0_store2.1 = (bf16[512,16384]{1,0:T(8,128)(2,1)}, f32[4,128]{1,0:T(4,128)}) custom-call(s32[3]{0:T(128)S(1)} %pad_add_fusion.where_ref, bf16[64,16512]{1,0:T(8,128)(2,1)S(1)} %collective-permute-done.29.refs_0_, f32[512,128]{1,0:T(8,128)S(1)} %get-tuple-element.106.refs_1_, ...), custom_call_target="tpu_custom_call", output_to_operand_aliasing={{0}: (3, {})} | custom-call | flops 20000000000 | bytes 1 | tf_op jit(solution)/shard_map/rotate0_store2/pallas_call | solution.py:250
  (59 shorter events, 13.5 us)
Async XLA Ops:
  2.0 3.0 %collective-permute-start = (bf16[8,32,1024]{2,1,0:T(8,128)(2,1)S(1)}, bf16[8,32,1024]{2,1,0:T(8,128)(2,1)S(1)}, u32[]{:S(2)}, u32[]{:S(2)}) collective-permute-start(bf16[8,32,1024]{2,1,0:T(8,128)(2,1)S(1)} %get-tuple-element.115), channel_id=1, source_target_pairs={{0,8},{8,0},{16,24},{24,16},{32,40},{40,32},{48,56},{56,48},{64,72... | collective-permute-start | bytes 1572872 | tf_op jit(solution)/shard_map/ppermute | solution.py:40
  6.4 10.3 %collective-permute-start.2 = (bf16[2,32,2048]{2,1,0:T(8,128)(2,1)S(1)}, bf16[2,32,2048]{2,1,0:T(8,128)(2,1)S(1)}, u32[]{:S(2)}, u32[]{:S(2)}) collective-permute-start(bf16[2,32,2048]{2,1,0:T(8,128)(2,1)S(1)} %get-tuple-element.58), channel_id=1, source_target_pairs={{0,6},{1,7},{2,4},{3,5},{4,2},{5,3},{6,0},{7,1},{8,14},{9,15},{10,... | collective-permute-start | bytes 786440 | tf_op jit(solution)/shard_map/ppermute | solution.py:40
  10.3 7.2 %collective-permute-start.1 = (bf16[2,32,2048]{2,1,0:T(8,128)(2,1)S(1)}, bf16[2,32,2048]{2,1,0:T(8,128)(2,1)S(1)}, u32[]{:S(2)}, u32[]{:S(2)}) collective-permute-start(bf16[2,32,2048]{2,1,0:T(8,128)(2,1)S(1)} %get-tuple-element.56), channel_id=1, source_target_pairs={{0,2},{1,3},{2,0},{3,1},{4,6},{5,7},{6,4},{7,5},{8,10},{9,11},{10,... | collective-permute-start | bytes 786440 | tf_op jit(solution)/shard_map/ppermute | solution.py:40
  10.3 14.2 %collective-permute-start.10 = (bf16[1,32,2048]{2,1,0:T(8,128)(2,1)S(1)}, bf16[1,32,2048]{2,1,0:T(8,128)(2,1)S(1)}, u32[]{:S(2)}, u32[]{:S(2)}) collective-permute-start(bf16[1,32,2048]{2,1,0:T(8,128)(2,1)S(1)} %get-tuple-element.57), channel_id=1, source_target_pairs={{0,1},{1,0},{2,3},{3,2},{4,5},{5,4},{6,7},{7,6},{8,9},{9,8},{10,11... | collective-permute-start | bytes 393224 | tf_op jit(solution)/shard_map/ppermute | solution.py:40
  11.6 12.9 %collective-permute-start.11 = (bf16[1,32,2048]{2,1,0:T(8,128)(2,1)S(1)}, bf16[1,32,2048]{2,1,0:T(8,128)(2,1)S(1)}, u32[]{:S(2)}, u32[]{:S(2)}) collective-permute-start(bf16[1,32,2048]{2,1,0:T(8,128)(2,1)S(1)} %get-tuple-element.57), channel_id=1, source_target_pairs={{0,65},{1,64},{2,67},{3,66},{4,69},{5,68},{6,71},{7,70},{8,73},{9,... | collective-permute-start | bytes 393224 | tf_op jit(solution)/shard_map/ppermute | solution.py:47
  13.5 9.5 %collective-permute-start.7 = (bf16[2,32,2048]{2,1,0:T(8,128)(2,1)S(1)}, bf16[2,32,2048]{2,1,0:T(8,128)(2,1)S(1)}, u32[]{:S(2)}, u32[]{:S(2)}) collective-permute-start(bf16[2,32,2048]{2,1,0:T(8,128)(2,1)S(1)} %get-tuple-element.59), channel_id=1, source_target_pairs={{0,4},{1,5},{2,6},{3,7},{4,0},{5,1},{6,2},{7,3},{8,12},{9,13},{10,... | collective-permute-start | bytes 786440 | tf_op jit(solution)/shard_map/ppermute | solution.py:40
  17.6 6.5 %collective-permute-start.4 = (bf16[1,64,2048]{2,1,0:T(8,128)(2,1)S(1)}, bf16[1,64,2048]{2,1,0:T(8,128)(2,1)S(1)}, u32[]{:S(2)}, u32[]{:S(2)}) collective-permute-start(bf16[1,64,2048]{2,1,0:T(8,128)(2,1)S(1)} %get-tuple-element.60), channel_id=1, source_target_pairs={{0,48},{8,56},{16,32},{24,40},{32,16},{40,24},{48,0},{56,8},{64,11... | collective-permute-start | bytes 786440 | tf_op jit(solution)/shard_map/ppermute | solution.py:40
  20.1 3.9 %collective-permute-start.3 = (bf16[1,32,2048]{2,1,0:T(8,128)(2,1)S(1)}, bf16[1,32,2048]{2,1,0:T(8,128)(2,1)S(1)}, u32[]{:S(2)}, u32[]{:S(2)}) collective-permute-start(bf16[1,32,2048]{2,1,0:T(8,128)(2,1)S(1)} %get-tuple-element.61), channel_id=1, source_target_pairs={{0,16},{8,24},{16,0},{24,8},{32,48},{40,56},{48,32},{56,40},{64,80... | collective-permute-start | bytes 393224 | tf_op jit(solution)/shard_map/ppermute | solution.py:40
  24.2 4.8 %collective-permute-start.12 = (bf16[1,32,2048]{2,1,0:T(8,128)(2,1)S(1)}, bf16[1,32,2048]{2,1,0:T(8,128)(2,1)S(1)}, u32[]{:S(2)}, u32[]{:S(2)}) collective-permute-start(bf16[1,32,2048]{2,1,0:T(8,128)(2,1)S(1)} %get-tuple-element.65), channel_id=1, source_target_pairs={{0,16},{8,24},{16,0},{24,8},{32,48},{40,56},{48,32},{56,40},{64,80... | collective-permute-start | bytes 393224 | tf_op jit(solution)/shard_map/ppermute | solution.py:40
  24.6 6.5 %collective-permute-start.8 = (bf16[1,32,2048]{2,1,0:T(8,128)(2,1)S(1)}, bf16[1,32,2048]{2,1,0:T(8,128)(2,1)S(1)}, u32[]{:S(2)}, u32[]{:S(2)}) collective-permute-start(bf16[1,32,2048]{2,1,0:T(8,128)(2,1)S(1)} %get-tuple-element.66), channel_id=1, source_target_pairs={{0,1},{1,0},{2,3},{3,2},{4,5},{5,4},{6,7},{7,6},{8,9},{9,8},{10,11... | collective-permute-start | bytes 393224 | tf_op jit(solution)/shard_map/ppermute | solution.py:40
  26.1 5.9 %collective-permute-start.9 = (bf16[1,32,2048]{2,1,0:T(8,128)(2,1)S(1)}, bf16[1,32,2048]{2,1,0:T(8,128)(2,1)S(1)}, u32[]{:S(2)}, u32[]{:S(2)}) collective-permute-start(bf16[1,32,2048]{2,1,0:T(8,128)(2,1)S(1)} %get-tuple-element.66), channel_id=1, source_target_pairs={{0,65},{1,64},{2,67},{3,66},{4,69},{5,68},{6,71},{7,70},{8,73},{9,... | collective-permute-start | bytes 393224 | tf_op jit(solution)/shard_map/ppermute | solution.py:47
  28.0 6.7 %collective-permute-start.5 = (bf16[1,64,2048]{2,1,0:T(8,128)(2,1)S(1)}, bf16[1,64,2048]{2,1,0:T(8,128)(2,1)S(1)}, u32[]{:S(2)}, u32[]{:S(2)}) collective-permute-start(bf16[1,64,2048]{2,1,0:T(8,128)(2,1)S(1)} %get-tuple-element.64), channel_id=1, source_target_pairs={{0,1},{1,0},{2,3},{3,2},{4,5},{5,4},{6,7},{7,6},{8,9},{9,8},{10,11... | collective-permute-start | bytes 786440 | tf_op jit(solution)/shard_map/ppermute | solution.py:40
  28.4 6.8 %collective-permute-start.6 = (bf16[1,64,2048]{2,1,0:T(8,128)(2,1)S(1)}, bf16[1,64,2048]{2,1,0:T(8,128)(2,1)S(1)}, u32[]{:S(2)}, u32[]{:S(2)}) collective-permute-start(bf16[1,64,2048]{2,1,0:T(8,128)(2,1)S(1)} %get-tuple-element.64), channel_id=1, source_target_pairs={{0,65},{1,64},{2,67},{3,66},{4,69},{5,68},{6,71},{7,70},{8,73},{9,... | collective-permute-start | bytes 786440 | tf_op jit(solution)/shard_map/ppermute | solution.py:47
  29.0 6.9 %collective-permute-start.16 = (bf16[2,32,2048]{2,1,0:T(8,128)(2,1)S(1)}, bf16[2,32,2048]{2,1,0:T(8,128)(2,1)S(1)}, u32[]{:S(2)}, u32[]{:S(2)}) collective-permute-start(bf16[2,32,2048]{2,1,0:T(8,128)(2,1)S(1)} %pad_maximum_fusion.8), channel_id=1, source_target_pairs={{0,48},{8,56},{16,32},{24,40},{32,16},{40,24},{48,0},{56,8},{64,11... | collective-permute-start | bytes 786440 | tf_op jit(solution)/shard_map/ppermute | solution.py:40
  31.1 15.5 %collective-permute-start.14 = (bf16[2,64,2048]{2,1,0:T(8,128)(2,1)S(1)}, bf16[2,64,2048]{2,1,0:T(8,128)(2,1)S(1)}, u32[]{:S(2)}, u32[]{:S(2)}) collective-permute-start(bf16[2,64,2048]{2,1,0:T(8,128)(2,1)S(1)} %pad_maximum_fusion.2), channel_id=1, source_target_pairs={{0,16},{8,24},{16,0},{24,8},{32,48},{40,56},{48,32},{56,40},{64,80... | collective-permute-start | bytes 1572872 | tf_op jit(solution)/shard_map/ppermute | solution.py:40
  32.0 7.0 %collective-permute-start.17 = (bf16[2,32,2048]{2,1,0:T(8,128)(2,1)S(1)}, bf16[2,32,2048]{2,1,0:T(8,128)(2,1)S(1)}, u32[]{:S(2)}, u32[]{:S(2)}) collective-permute-start(bf16[2,32,2048]{2,1,0:T(8,128)(2,1)S(1)} %pad_maximum_fusion.10), channel_id=1, source_target_pairs={{0,48},{8,56},{16,32},{24,40},{32,16},{40,24},{48,0},{56,8},{64,11... | collective-permute-start | bytes 786440 | tf_op jit(solution)/shard_map/ppermute | solution.py:40
  34.7 7.3 %collective-permute-start.15 = (bf16[2,32,2048]{2,1,0:T(8,128)(2,1)S(1)}, bf16[2,32,2048]{2,1,0:T(8,128)(2,1)S(1)}, u32[]{:S(2)}, u32[]{:S(2)}) collective-permute-start(bf16[2,32,2048]{2,1,0:T(8,128)(2,1)S(1)} %pad_maximum_fusion.11), channel_id=1, source_target_pairs={{0,64},{8,72},{16,80},{24,88},{32,96},{40,104},{48,112},{56,120},{... | collective-permute-start | bytes 786440 | tf_op jit(solution)/shard_map/ppermute | solution.py:40
  35.1 9.8 %collective-permute-start.21 = (bf16[2,32,2048]{2,1,0:T(8,128)(2,1)S(1)}, bf16[2,32,2048]{2,1,0:T(8,128)(2,1)S(1)}, u32[]{:S(2)}, u32[]{:S(2)}) collective-permute-start(bf16[2,32,2048]{2,1,0:T(8,128)(2,1)S(1)} %pad_maximum_fusion.9), channel_id=1, source_target_pairs={{0,16},{8,24},{16,0},{24,8},{32,48},{40,56},{48,32},{56,40},{64,80... | collective-permute-start | bytes 786440 | tf_op jit(solution)/shard_map/ppermute | solution.py:40
  35.9 14.1 %collective-permute-start.13 = (bf16[2,64,2048]{2,1,0:T(8,128)(2,1)S(1)}, bf16[2,64,2048]{2,1,0:T(8,128)(2,1)S(1)}, u32[]{:S(2)}, u32[]{:S(2)}) collective-permute-start(bf16[2,64,2048]{2,1,0:T(8,128)(2,1)S(1)} %pad_maximum_fusion.3), channel_id=1, source_target_pairs={{0,48},{8,56},{16,32},{24,40},{32,16},{40,24},{48,0},{56,8},{64,11... | collective-permute-start | bytes 1572872 | tf_op jit(solution)/shard_map/ppermute | solution.py:40
  39.1 17.3 %collective-permute-start.23 = (bf16[4,32,2048]{2,1,0:T(8,128)(2,1)S(1)}, bf16[4,32,2048]{2,1,0:T(8,128)(2,1)S(1)}, u32[]{:S(2)}, u32[]{:S(2)}) collective-permute-start(bf16[4,32,2048]{2,1,0:T(8,128)(2,1)S(1)} %pad_maximum_fusion.6.refs_0_), channel_id=1, source_target_pairs={{0,16},{8,24},{16,0},{24,8},{32,48},{40,56},{48,32},{56,40},{64,80... | collective-permute-start | bytes 1572872 | tf_op jit(solution)/shard_map/ppermute | solution.py:40
  41.9 11.9 %collective-permute-start.24 = (bf16[4,32,2048]{2,1,0:T(8,128)(2,1)S(1)}, bf16[4,32,2048]{2,1,0:T(8,128)(2,1)S(1)}, u32[]{:S(2)}, u32[]{:S(2)}) collective-permute-start(bf16[4,32,2048]{2,1,0:T(8,128)(2,1)S(1)} %pad_maximum_fusion.5.refs_0_), channel_id=1, source_target_pairs={{0,64},{8,72},{16,80},{24,88},{32,96},{40,104},{48,112},{56,120},{... | collective-permute-start | bytes 1572872 | tf_op jit(solution)/shard_map/ppermute | solution.py:40
  44.9 35.1 %collective-permute-start.20 = (bf16[4,32,2048]{2,1,0:T(8,128)(2,1)S(1)}, bf16[4,32,2048]{2,1,0:T(8,128)(2,1)S(1)}, u32[]{:S(2)}, u32[]{:S(2)}) collective-permute-start(bf16[4,32,2048]{2,1,0:T(8,128)(2,1)S(1)} %pad_maximum_fusion.4.refs_0_), channel_id=1, source_target_pairs={{0,48},{8,56},{16,32},{24,40},{32,16},{40,24},{48,0},{56,8},{64,11... | collective-permute-start | bytes 1572872 | tf_op jit(solution)/shard_map/ppermute | solution.py:40
  46.7 34.9 %collective-permute-start.19 = (bf16[4,64,2048]{2,1,0:T(8,128)(2,1)S(1)}, bf16[4,64,2048]{2,1,0:T(8,128)(2,1)S(1)}, u32[]{:S(2)}, u32[]{:S(2)}) collective-permute-start(bf16[4,64,2048]{2,1,0:T(8,128)(2,1)S(1)} %pad_maximum_fusion.1.refs_0_), channel_id=1, source_target_pairs={{0,64},{8,72},{16,80},{24,88},{32,96},{40,104},{48,112},{56,120},{... | collective-permute-start | bytes 3145736 | tf_op jit(solution)/shard_map/ppermute | solution.py:40
  50.1 34.9 %collective-permute-start.18 = (bf16[4,64,2048]{2,1,0:T(8,128)(2,1)S(1)}, bf16[4,64,2048]{2,1,0:T(8,128)(2,1)S(1)}, u32[]{:S(2)}, u32[]{:S(2)}) collective-permute-start(bf16[4,64,2048]{2,1,0:T(8,128)(2,1)S(1)} %pad_maximum_fusion.refs_0_), channel_id=1, source_target_pairs={{0,16},{8,24},{16,0},{24,8},{32,48},{40,56},{48,32},{56,40},{64,80... | collective-permute-start | bytes 3145736 | tf_op jit(solution)/shard_map/ppermute | solution.py:40
  53.8 18.3 %collective-permute-start.22 = (bf16[4,32,2048]{2,1,0:T(8,128)(2,1)S(1)}, bf16[4,32,2048]{2,1,0:T(8,128)(2,1)S(1)}, u32[]{:S(2)}, u32[]{:S(2)}) collective-permute-start(bf16[4,32,2048]{2,1,0:T(8,128)(2,1)S(1)} %pad_maximum_fusion.7.refs_0_), channel_id=1, source_target_pairs={{0,48},{8,56},{16,32},{24,40},{32,16},{40,24},{48,0},{56,8},{64,11... | collective-permute-start | bytes 1572872 | tf_op jit(solution)/shard_map/ppermute | solution.py:40
  56.4 26.2 %collective-permute-start.25 = (bf16[32,16512]{1,0:T(8,128)(2,1)S(1)}, bf16[32,16512]{1,0:T(8,128)(2,1)S(1)}, u32[]{:S(2)}, u32[]{:S(2)}) collective-permute-start(bf16[32,16512]{1,0:T(8,128)(2,1)S(1)} %get-tuple-element.78.refs_2_), channel_id=1, source_target_pairs={{0,8},{8,0},{16,24},{24,16},{32,40},{40,32},{48,56},{56,48},{64,72... | collective-permute-start | bytes 3170312 | tf_op jit(solution)/shard_map/ppermute | solution.py:40
  72.1 10.5 %collective-permute-start.26 = (bf16[32,16512]{1,0:T(8,128)(2,1)S(1)}, bf16[32,16512]{1,0:T(8,128)(2,1)S(1)}, u32[]{:S(2)}, u32[]{:S(2)}) collective-permute-start(bf16[32,16512]{1,0:T(8,128)(2,1)S(1)} %get-tuple-element.80.refs_2_), channel_id=1, source_target_pairs={{0,8},{8,0},{16,24},{24,16},{32,40},{40,32},{48,56},{56,48},{64,72... | collective-permute-start | bytes 3170312 | tf_op jit(solution)/shard_map/ppermute | solution.py:40
  80.0 5.0 %collective-permute-start.27 = (bf16[32,16512]{1,0:T(8,128)(2,1)S(1)}, bf16[32,16512]{1,0:T(8,128)(2,1)S(1)}, u32[]{:S(2)}, u32[]{:S(2)}) collective-permute-start(bf16[32,16512]{1,0:T(8,128)(2,1)S(1)} %get-tuple-element.83.refs_2_), channel_id=1, source_target_pairs={{0,8},{8,0},{16,24},{24,16},{32,40},{40,32},{48,56},{56,48},{64,72... | collective-permute-start | bytes 3170312 | tf_op jit(solution)/shard_map/ppermute | solution.py:40
  81.6 3.3 %collective-permute-start.28 = (bf16[32,16512]{1,0:T(8,128)(2,1)S(1)}, bf16[32,16512]{1,0:T(8,128)(2,1)S(1)}, u32[]{:S(2)}, u32[]{:S(2)}) collective-permute-start(bf16[32,16512]{1,0:T(8,128)(2,1)S(1)} %get-tuple-element.86.refs_2_), channel_id=1, source_target_pairs={{0,8},{8,0},{16,24},{24,16},{32,40},{40,32},{48,56},{56,48},{64,72... | collective-permute-start | bytes 3170312 | tf_op jit(solution)/shard_map/ppermute | solution.py:40
  84.8 4.3 %collective-permute-start.30 = (bf16[64,16512]{1,0:T(8,128)(2,1)S(1)}, bf16[64,16512]{1,0:T(8,128)(2,1)S(1)}, u32[]{:S(2)}, u32[]{:S(2)}) collective-permute-start(bf16[64,16512]{1,0:T(8,128)(2,1)S(1)} %get-tuple-element.89.refs_2_), channel_id=1, source_target_pairs={{0,8},{8,0},{16,24},{24,16},{32,40},{40,32},{48,56},{56,48},{64,72... | collective-permute-start | bytes 6340616 | tf_op jit(solution)/shard_map/ppermute | solution.py:40
  87.6 4.6 %collective-permute-start.29 = (bf16[64,16512]{1,0:T(8,128)(2,1)S(1)}, bf16[64,16512]{1,0:T(8,128)(2,1)S(1)}, u32[]{:S(2)}, u32[]{:S(2)}) collective-permute-start(bf16[64,16512]{1,0:T(8,128)(2,1)S(1)} %get-tuple-element.92.refs_0_), channel_id=1, source_target_pairs={{0,8},{8,0},{16,24},{24,16},{32,40},{40,32},{48,56},{56,48},{64,72... | collective-permute-start | bytes 6340616 | tf_op jit(solution)/shard_map/ppermute | solution.py:40
